TPU v7x, 256 devices: a whole 4x4x8 slice. The times are simulated.
256 devices in a mesh: pole: 16 (over z, y_hi), grid: 16 (over y_lo, x, core).
Axes of the slice: x: 4, y: 4 (y_hi: 2, y_lo: 2; y = y_hi * 2 + y_lo), z: 8, core: 2. Of those that a mesh axis runs over, the one named last changes fastest.
Arguments:
- factor_cols: bfloat16 [16, 2, 3072, 1536], P('pole', None, 'grid'), may hold values from -1.1953125 to 1.1953125
- ancestor_inverse: bfloat16 [16, 2, 3072, 3072], P('pole', None, 'grid'), may hold values from -2 to 2, as said below
- pivot_inverse: float32 [16, 2, 3, 512, 512], P('pole', None, None, 'grid'), may hold values from -6 to 6
- structure: int32 [96, 3], replicated, may hold values 0 or 1
- widths: int32 [3], replicated, may hold values from 1 to 512, as said below
- pole_weights: float32 [16, 2], P('pole'), may hold values from -4 to 4
Outputs:
- column_inverse: bfloat16 [16, 2, 3072, 1536], P('pole', None, 'grid')
- pivot_block: float32 [16, 2, 3, 512, 512], P('pole', None, None, 'grid')
- density_column: float32 [3072, 1536], P('grid', 'pole')
- density_pivot: float32 [3, 512, 512], P(None, 'grid', 'pole')
Inputs may be any that keep to these rules, and one draw needn't show every extreme that they name: `ancestor_inverse`: for every pole, each of the two planes is a symmetric matrix. The 3 widths sum to 768, and one of them is 512.
All inputs are finite; a program needn't handle non-finite values.
Results may differ from a plain program's by a relative error of at most 0.0004.
Values may be sent and summed in bfloat16 or wider, within the bound.
No kernel may reach another device: no remote copies, remote signals or barrier semaphores. Data moves between devices by JAX's collectives and lax.ppermute only.
A program may use at most 128 MiB of HBM per device.

v0:
```python
import jax
import jax.numpy as jnp
from jax import lax
from jax.sharding import PartitionSpec as P

BLK = 32


def local(factor_cols, ancestor_inverse, pivot_inverse, structure, widths, pole_weights):
    row_count = factor_cols.shape[2]
    col_count = factor_cols.shape[3]
    sup_count = pivot_inverse.shape[2]
    pivot_rows = pivot_inverse.shape[3]
    slot_width = pivot_inverse.shape[4]
    grid_at = lax.axis_index("grid")
    row_ids = grid_at * row_count + jnp.arange(row_count, dtype=jnp.int32)
    block_ids = jnp.arange(structure.shape[0], dtype=jnp.int32)
    block_hot = (row_ids[:, None] // BLK == block_ids[None, :]).astype(jnp.float32)
    row_live = jnp.dot(block_hot, structure.astype(jnp.float32), preferred_element_type=jnp.float32)
    col_ids = jnp.arange(col_count, dtype=jnp.int32)
    col_in = col_ids % slot_width
    sup_hot = (
        col_ids[None, :] // slot_width == jnp.arange(sup_count, dtype=jnp.int32)[:, None]
    ).astype(jnp.int32)
    col_width = jnp.sum(sup_hot * widths[:, None], axis=0)
    live_col = (col_in < col_width).astype(jnp.float32)
    mask = (
        jnp.dot(row_live, sup_hot.astype(jnp.float32), preferred_element_type=jnp.float32)
        * live_col[None, :]
    )
    masked = factor_cols[0] * mask.astype(jnp.bfloat16)[None]
    inverse_rows = ancestor_inverse[0]
    piece = lax.all_gather(masked, "grid", axis=1, tiled=True)
    real_part = jnp.dot(inverse_rows[0], piece[0], preferred_element_type=jnp.float32) - jnp.dot(
        inverse_rows[1], piece[1], preferred_element_type=jnp.float32
    )
    imag_part = jnp.dot(inverse_rows[0], piece[1], preferred_element_type=jnp.float32) + jnp.dot(
        inverse_rows[1], piece[0], preferred_element_type=jnp.float32
    )
    product = jnp.stack([real_part, imag_part])
    column_full = -(product * mask[None])
    column_inverse = column_full.astype(jnp.bfloat16)
    left_cols = masked.astype(jnp.float32).reshape(2, row_count, sup_count, slot_width)
    right_cols = column_full.reshape(2, row_count, sup_count, slot_width)

    def across(first, second):
        return jnp.einsum("rkc,rkd->kcd", first, second, precision=lax.Precision.HIGHEST)

    q_real = across(left_cols[0], right_cols[0]) - across(left_cols[1], right_cols[1])
    q_imag = across(left_cols[0], right_cols[1]) + across(left_cols[1], right_cols[0])
    stacked_q = jnp.stack([q_real, q_imag])
    summed = lax.psum_scatter(stacked_q, "grid", scatter_dimension=2, tiled=True)
    pivot_ids = grid_at * pivot_rows + jnp.arange(pivot_rows, dtype=jnp.int32)
    live_rows = (pivot_ids[None, :] < widths[:, None]).astype(jnp.float32)
    live_cols = (jnp.arange(slot_width, dtype=jnp.int32)[None, :] < widths[:, None]).astype(
        jnp.float32
    )
    pivot_block = (pivot_inverse[0] - summed) * (live_rows[:, :, None] * live_cols[:, None, :])[
        None
    ]
    weight_real = pole_weights[0, 0]
    weight_imag = pole_weights[0, 1]
    term_column = weight_real * column_full[1] + weight_imag * column_full[0]
    term_pivot = weight_real * pivot_block[1] + weight_imag * pivot_block[0]
    density_column, density_pivot = (
        lax.psum_scatter(term_column, "pole", scatter_dimension=1, tiled=True),
        lax.psum_scatter(term_pivot, "pole", scatter_dimension=2, tiled=True),
    )
    return (column_inverse[None], pivot_block[None], density_column, density_pivot)


def solution(mesh):
    in_specs = (
        P("pole", None, "grid", None),
        P("pole", None, "grid", None),
        P("pole", None, None, "grid", None),
        P(),
        P(),
        P("pole", None),
    )
    out_specs = (
        P("pole", None, "grid", None),
        P("pole", None, None, "grid", None),
        P("grid", "pole"),
        P(None, "grid", "pole"),
    )
    return jax.shard_map(local, mesh=mesh, in_specs=in_specs, out_specs=out_specs, check_vma=False)
```

profile of v0, /device:TPU:8, one launch (start us, length us, event | category | flops | bytes accessed | tf_op | source)
XLA Modules:
  0.0 646.9 jit_solution(1701408950320835942)
XLA Ops:
  7.2 0.8 select_reduce_fusion
  8.1 1.3 fusion.51
  9.4 1.1 bitcast_multiply_fusion
  10.6 1.2 copy-done
  12.4 1.2 squeeze.57
  14.2 103.5 %all-gather.2.cloned.1.call-done = bf16[2,3072,1536]{2,1,0:T(8,128)(2,1)} async-done(((bf16[2,192,1536]{2,1,0:T(8,128)(2,1)}), bf16[2,3072,1536]{2,1,0:T(8,128)(2,1)}) %all-gather.2.cloned.1.call-update) | async-done | bytes 18874384 | tf_op jit(solution)/shard_map/all_gather | solution.py:33
  117.6 6.2 fusion
  123.8 6.8 %fusion.1 = f32[1536,192]{0,1:T(8,128)S(1)} fusion(bf16[2,3072,1536]{2,1,0:T(8,128)(2,1)} %all-gather.2.cloned.1.call-done, bf16[1,2,192,3072]{3,2,1,0:T(8,128)(2,1)} %param.7), kind=kOutput, calls=%fused_computation.3 | convolution fusion | flops 1811939328 | bytes 11796480 | tf_op jit(solution)/shard_map/dot_general | solution.py:37
  131.0 2.0 fusion.5
  133.0 2.0 fusion.4
  136.0 3.3 add_bitcast_fusion.1
  139.3 1.9 squeeze.56
  141.3 2.8 squeeze.58
  144.1 1.9 fusion.23
  146.1 2.0 fusion.19
  148.1 2.0 subtract_bitcast_fusion
  150.0 2.0 add_bitcast_fusion
  152.0 3.4 pad_maximum_fusion
  155.5 1.2 copy-done.7
  156.7 1.6 copy.38
  158.7 70.0 %reduce-scatter.8.cloned.1.call-done = f32[2,3,32,512]{3,2,1,0:T(8,128)} async-done(((f32[2,3,512,512]{3,2,1,0:T(8,128)}), f32[2,3,32,512]{3,2,1,0:T(8,128)}) %reduce-scatter.8.cloned.1.call-update) | async-done | bytes 393232 | tf_op jit(solution)/shard_map/reduce_scatter | solution.py:52
  228.7 1.1 fusion.29
  229.8 0.7 copy-done.8
  230.5 2.2 fusion.31
  232.7 2.2 copy.40
  234.9 2.3 reshape.209
  237.3 1.4 fusion.7
  238.6 198.1 %reduce-scatter.10.cloned.1.call-done = f32[96,192]{1,0:T(8,128)} async-done(((f32[1536,192]{1,0:T(8,128)}), f32[96,192]{1,0:T(8,128)}) %reduce-scatter.10.cloned.1.call-update) | async-done | bytes 73744
  436.7 1.6 copy.39
  438.4 200.4 %reduce-scatter.12.cloned.1.call-done = f32[32,96]{1,0:T(8,128)} async-done(((f32[512,96]{1,0:T(8,128)}), f32[32,96]{1,0:T(8,128)}) %reduce-scatter.12.cloned.1.call-update) | async-done | bytes 12304
  638.8 0.8 reshape.210
  639.6 0.7 copy.41
  (46 shorter events, 2.9 us)
Async XLA Ops:
  7.2 2.3 copy-start.9
  7.2 110.5 %all-gather.2.cloned.1.call-start = ((), (), s32[]{:S(2)}) async-start(), calls=%async_computation.3 | async-start | bytes 20054016 | tf_op jit(solution)/shard_map/all_gather | solution.py:33
  10.6 1.3 copy-start
  10.6 218.1 %reduce-scatter.8.cloned.1.call-start = ((), (), s32[]{:S(2)}) async-start(), calls=%async_computation.4 | async-start | bytes 6684672 | tf_op jit(solution)/shard_map/reduce_scatter | solution.py:52
  11.9 1.7 copy-start.12
  117.6 13.0 %copy-start.13 = (bf16[2,3072,1536]{2,1,0:T(8,128)(2,1)S(1)}, bf16[2,3072,1536]{2,1,0:T(8,128)(2,1)}, u32[]{:S(2)}) copy-start(bf16[2,3072,1536]{2,1,0:T(8,128)(2,1)} %all-gather.2.cloned.1.call-done) | copy-start | bytes 56623108
  123.8 7.2 %copy-start.14 = (bf16[1,2,192,3072]{3,2,1,0:T(8,128)(2,1)S(1)}, bf16[1,2,192,3072]{3,2,1,0:T(8,128)(2,1)}, u32[]{:S(2)}) copy-start(bf16[1,2,192,3072]{3,2,1,0:T(8,128)(2,1)} %param.7) | copy-start | bytes 7077892
  133.0 2.0 copy-start.3
  135.0 1.0 copy-start.5
  144.1 2.0 copy-start.1
  146.1 2.0 copy-start.2
  155.4 1.3 copy-start.7
  155.5 281.3 %reduce-scatter.10.cloned.1.call-start = ((), (), s32[]{:S(2)}) async-start(), calls=%async_computation.5 | async-start | bytes 1671168
  156.7 1.7 copy-start.11
  158.3 70.4 %copy-start.10 = (f32[1,2,3,32,512]{4,3,2,1,0:T(8,128)S(1)}, f32[1,2,3,32,512]{4,3,2,1,0:T(8,128)}, u32[]{:S(2)}) copy-start(f32[1,2,3,32,512]{4,3,2,1,0:T(8,128)} %param.8) | copy-start | bytes 1179652
  158.3 480.5 %reduce-scatter.12.cloned.1.call-start = ((), (), s32[]{:S(2)}) async-start(), calls=%async_computation.6 | async-start | bytes 278528
  229.8 0.7 copy-start.8
  230.5 6.7 %copy-start.4 = (f32[1536,192]{0,1:T(8,128)S(1)}, f32[1536,192]{0,1:T(8,128)}, u32[]{:S(2)}) copy-start(f32[1536,192]{0,1:T(8,128)} %copy-done.3) | copy-start | bytes 3538948
  230.5 6.7 %copy-start.6 = (f32[1536,192]{0,1:T(8,128)S(1)}, f32[1536,192]{0,1:T(8,128)}, u32[]{:S(2)}) copy-start(f32[1536,192]{0,1:T(8,128)} %copy-done.5) | copy-start | bytes 3538948
Sparse Core Ops, SparseCore 0:
  10.7 106.8 all-gather.1
  155.6 73.0 reduce-scatter.7
  232.6 204.1 reduce-scatter.9
  440.9 197.8 reduce-scatter.11
where the time goes:
time: 648 us; the launch traced here: 647 us
  waiting for transfers between devices  572 us (88%)
  matrix products  26.2 us (4%)
  local copies, waits for them, and re-layouts  20.5 us (3%)
  between operations  14.1 us (2%)
  other arithmetic  13.8 us (2%)
    unnamed x6, waiting for transfers between devices  399 us
    all_gather x1, waiting for transfers between devices, local(): piece = lax.all_gather(masked, 'grid', axis=1, tiled=True)  103 us
    reduce_scatter x1, waiting for transfers between devices, local(): lax.psum_scatter(stacked_q, 'grid', scatter_dimension=2, tiled=True)  70 us
    unnamed x36, local copies, waits for them, and re-layouts  13.5 us
  transfers between devices with their start and end apart: 4, of which 4 were waited for; matrix products, arithmetic and copies ran while one was open for 2% of the time, Pallas kernels for 0%

commit v1 on v0

v1 whole, which is shorter than its diff:
```python
import functools

import jax
import jax.numpy as jnp
from jax import lax
from jax.experimental import pallas as pl
from jax.experimental.pallas import tpu as pltpu
from jax.sharding import PartitionSpec as P

F32 = jnp.float32
BF16 = jnp.bfloat16
BIG = 512
ROWS = 192
HB = 256
HS = 128
HC = HB + HS

NX, NY, NCORE = 4, 2, 2
NZ, NH = 8, 2


def grid_perm(source):
    def at(y, x, c):
        return (y * NX + x % NX) * NCORE + c

    return [
        (at(*source(y, x, c)), at(y, x, c)) for y in range(NY) for x in range(NX) for c in range(NCORE)
    ]


def pole_perm(source):
    def at(z, h):
        return (z % NZ) * NH + h

    return [(at(*source(z, h)), at(z, h)) for z in range(NZ) for h in range(NH)]


CORE = grid_perm(lambda y, x, c: (y, x, 1 - c))
FROM_AHEAD = grid_perm(lambda y, x, c: (y, x + 1 - 2 * c, c))
FROM_BEHIND = grid_perm(lambda y, x, c: (y, x - 1 + 2 * c, c))
FROM_Y = grid_perm(lambda y, x, c: (1 - y, x, c))


def from_x(step):
    return grid_perm(lambda y, x, c: (y, x - step, c))


def from_z(step):
    return pole_perm(lambda z, h: (z - step, h))


FROM_H = pole_perm(lambda z, h: (z, 1 - h))


def place():
    g = lax.axis_index("grid")
    c = lax.rem(g, 2)
    x = lax.rem(lax.div(g, 2), NX)
    y = lax.div(g, 2 * NX)
    return g, c, x, y


def supers(widths):
    kb = jnp.where(widths[0] == BIG, 0, jnp.where(widths[1] == BIG, 1, 2))
    k1 = jnp.where(kb == 0, 1, 0)
    k2 = jnp.where(kb == 2, 1, 2)
    return kb, k1, k2, widths[k1]


def iota(shape, axis):
    return lax.broadcasted_iota(jnp.int32, shape, axis)


def row_mask(structure, block, count, k, lanes):
    return jnp.concatenate(
        [jnp.full((32, lanes), structure[block + i, k].astype(F32), F32) for i in range(count)], axis=0
    )


def call(body, outs, ins, name, flops=0, scratch=()):
    vm = pl.BlockSpec(memory_space=pltpu.VMEM)
    sm = pl.BlockSpec(memory_space=pltpu.SMEM)
    size = sum(a.size * a.dtype.itemsize for a, _ in ins) + sum(
        o.size * o.dtype.itemsize for o in outs
    )
    return pl.pallas_call(
        body,
        out_shape=tuple(outs),
        in_specs=[sm if kind == "s" else vm for _, kind in ins],
        out_specs=tuple(vm for _ in outs),
        scratch_shapes=list(scratch),
        compiler_params=pltpu.CompilerParams(vmem_limit_bytes=48 * 1024 * 1024),
        cost_estimate=pl.CostEstimate(flops=flops, bytes_accessed=size, transcendentals=0),
        name=name,
    )(*[a for a, _ in ins])


def sds(shape, dtype):
    return jax.ShapeDtypeStruct(shape, dtype)


def prep_kernel(structure, widths, f, keep, send):
    g, c, _, _ = place()
    kb, k1, k2, a = supers(widths)
    base = g * 6
    mask_b = row_mask(structure, base, 6, kb, HB).astype(BF16)
    mask_1 = row_mask(structure, base, 6, k1, HB).astype(BF16)
    mask_2 = row_mask(structure, base, 6, k2, HB).astype(BF16)
    shift = (iota((HB, HB), 0) + a == iota((HB, HB), 1)).astype(BF16)
    first = iota((ROWS, HB), 1) < a

    def at(k, part):
        return pl.ds(pl.multiple_of(k * BIG + part * HB, HB), HB)

    for p in range(2):
        o = p * HC
        keep[:, o : o + HB] = f[p, :, at(kb, c)] * mask_b
        send[:, o : o + HB] = f[p, :, at(kb, 1 - c)] * mask_b
        one = (f[p, :, at(k1, 0)] * mask_1).astype(F32)
        two = jnp.dot(f[p, :, at(k2, 0)] * mask_2, shift, preferred_element_type=F32)
        small = jnp.where(first, one, two)
        low, high = small[:, :HS], small[:, HS:]
        keep[:, o + HB : o + HC] = jnp.where(c == 0, low, high).astype(BF16)
        send[:, o + HB : o + HC] = jnp.where(c == 0, high, low).astype(BF16)


def left_kernel(widths, keep, send, got_mine, got_theirs, big, small):
    _, c, _, _ = place()
    _, _, _, a = supers(widths)
    back = (iota((HB, HB), 0) == iota((HB, HB), 1) + a).astype(BF16)
    mine = jnp.concatenate([keep[...], got_mine[...]], axis=0)
    theirs = jnp.concatenate([send[...], got_theirs[...]], axis=0)
    for p in range(2):
        o = p * HC
        big[c, p] = mine[:, o : o + HB].astype(F32).T.astype(BF16)
        big[1 - c, p] = theirs[:, o : o + HB].astype(F32).T.astype(BF16)
        m, t = mine[:, o + HB : o + HC].astype(F32), theirs[:, o + HB : o + HC].astype(F32)
        low, high = jnp.where(c == 0, m, t), jnp.where(c == 0, t, m)
        both = jnp.concatenate([low, high], axis=1)
        small[0, p] = both.T.astype(BF16)
        small[1, p] = jnp.dot(both.astype(BF16), back, preferred_element_type=F32).T.astype(BF16)


def add_blocks(get, a2s, blocks, put):
    z = None
    for a2, b in zip(a2s, blocks):
        d = jnp.dot(a2[...], b[...], preferred_element_type=F32)
        z = d if z is None else z + d
    for s in range(2):
        re, im = z[2 * s * ROWS : (2 * s + 1) * ROWS], z[(2 * s + 1) * ROWS : (2 * s + 2) * ROWS]
        old_re, old_im = get(s)
        put(s, old_re + (re[:, :HC] - im[:, HC:]), old_im + (re[:, HC:] + im[:, :HC]))


def acc_kernel(count, has_acc, *refs):
    refs = list(refs)
    old = refs.pop(0) if has_acc else None
    a2s, blocks, out = refs[:count], refs[count : 2 * count], refs[2 * count]

    def get(s):
        if old is None:
            return 0.0, 0.0
        return old[s, :, :HC], old[s, :, HC:]

    def put(s, re, im):
        out[s, :, :HC] = re
        out[s, :, HC:] = im

    add_blocks(get, a2s, blocks, put)


def column_kernel(structure, widths, old, a2, b, big, small, own, sib, q0, q1, q2, q3, gs, qb):
    g, c, x, _ = place()
    kb, k1, k2, a = supers(widths)

    def get(s):
        return old[s, :, :HC], old[s, :, HC:]

    def put(s, re, im):
        base = (g + s * (1 - 2 * c)) * 6
        mask_b = row_mask(structure, base, 6, kb, HB)
        mask_1 = row_mask(structure, base, 6, k1, HS)
        mask_2 = row_mask(structure, base, 6, k2, HS)
        mask_s = jnp.where(iota((ROWS, HS), 1) + c * HS < a, mask_1, mask_2)
        out = own if s == 0 else sib
        for p, v in ((0, re), (1, im)):
            vb = -(v[:, :HB] * mask_b)
            vs = -(v[:, HB:] * mask_s)
            out[:, p * HC : p * HC + HB] = vb
            out[:, p * HC + HB : (p + 1) * HC] = vs
            rows = slice(s * ROWS, (s + 1) * ROWS)
            for part, lo, hi in ((vb, p * HB, (p + 1) * HB), (vs, 2 * HB + p * HS, 2 * HB + (p + 1) * HS)):
                top = part.astype(BF16)
                gs[0, rows, lo:hi] = top
                gs[1, rows, lo:hi] = (part - top.astype(F32)).astype(BF16)

    add_blocks(get, [a2], [b], put)

    def across(left, lo, hi):
        return jnp.dot(left, gs[0, :, lo:hi], preferred_element_type=F32) + jnp.dot(
            left, gs[1, :, lo:hi], preferred_element_type=F32
        )

    for h in range(2):
        re = across(big[h, 0], 0, 2 * HB)
        im = across(big[h, 1], 0, 2 * HB)
        for t in range(NX):
            r = slice(64 * t, 64 * t + 64)
            qb[t, :, h * 2 * HB : h * 2 * HB + HB] = re[r, :HB] - im[r, HB:]
            qb[t, :, h * 2 * HB + HB : (h + 1) * 2 * HB] = re[r, HB:] + im[r, :HB]
    col = iota((HB, HS), 1) + c * HS
    row = iota((HB, HS), 0)
    parts = []
    for v in range(2):
        re = across(small[v, 0], 2 * HB, 2 * HB + 2 * HS)
        im = across(small[v, 1], 2 * HB, 2 * HB + 2 * HS)
        parts.append((re[:, :HS] - im[:, HS:], re[:, HS:] + im[:, :HS]))
    for p in range(2):
        e = jnp.where(
            col < a, jnp.where(row < a, parts[0][p], 0.0), jnp.where(row < HB - a, parts[1][p], 0.0)
        )
        for t in range(NX):
            qb[t, :, 4 * HB + p * HS : 4 * HB + (p + 1) * HS] = e[64 * t : 64 * t + 64]
    for d, q in enumerate((q0, q1, q2, q3)):
        q[...] = qb[lax.rem(x + d, NX)]


def spread_kernel(widths, weights, mine, other, out, *terms):
    _, c, _, _ = place()
    z = lax.div(lax.axis_index("pole"), NH)
    kb, k1, k2, a = supers(widths)
    wr, wi = weights[0, 0], weights[0, 1]
    back = (iota((HB, HB), 0) == iota((HB, HB), 1) + a).astype(BF16)
    lane = iota((ROWS, HB), 1)
    halves = []
    for ref in (mine, other):
        halves.append([(ref[:, p * HC : p * HC + HB], ref[:, p * HC + HB : (p + 1) * HC]) for p in range(2)])

    def at(k, part):
        return pl.ds(pl.multiple_of(k * BIG + part * HB, HB), HB)

    zero = jnp.zeros((ROWS, HB), BF16)
    planes = []
    for p in range(2):
        m, t = halves[0][p], halves[1][p]
        out[p, :, at(kb, c)] = m[0].astype(BF16)
        out[p, :, at(kb, 1 - c)] = t[0].astype(BF16)
        low, high = jnp.where(c == 0, m[1], t[1]), jnp.where(c == 0, t[1], m[1])
        s = jnp.concatenate([low, high], axis=1)
        sb = s.astype(BF16)
        out[p, :, at(k1, 0)] = jnp.where(lane < a, s, 0.0).astype(BF16)
        out[p, :, at(k1, 1)] = zero
        out[p, :, at(k2, 0)] = jnp.dot(sb, back, preferred_element_type=F32).astype(BF16)
        out[p, :, at(k2, 1)] = zero
        b0, b1 = jnp.where(c == 0, m[0], t[0]), jnp.where(c == 0, t[0], m[0])
        planes.append(jnp.concatenate([b0, b1, s], axis=1))
    d = wr * planes[1] + wi * planes[0]
    scratch = terms[-1]
    scratch[...] = d
    for i in range(NZ):
        to = lax.rem(z + i, NZ)
        terms[i][...] = scratch[pl.ds(pl.multiple_of(to * 24, 8), 24), :]


def fold_kernel(q0, q1, q2, q3, keep, send):
    _, _, _, y = place()
    t = q0[...] + q1[...] + q2[...] + q3[...]
    first, second, e = t[:, :BIG], t[:, BIG : 2 * BIG], t[:, 2 * BIG :]
    keep[:, :BIG] = jnp.where(y == 0, first, second)
    send[:, :BIG] = jnp.where(y == 0, second, first)
    keep[:, BIG:] = e
    send[:, BIG:] = e


def chip_kernel(keep, got, mine, send):
    _, c, _, _ = place()
    t = keep[...] + got[...]
    mine[...] = jnp.where(c == 0, t[:32], t[32:])
    send[...] = jnp.where(c == 0, t[32:], t[:32])


def pivot_kernel(widths, weights, pivot, mine, other, *rest):
    g, c, _, _ = place()
    z = lax.div(lax.axis_index("pole"), NH)
    kb, k1, k2, a = supers(widths)
    wr, wi = weights[0, 0], weights[0, 1]
    sums, out, outs, term, pay = rest[:NZ], rest[NZ], rest[NZ + 1 : 2 * NZ + 1], rest[-2], rest[-1]
    m, t = mine[...], other[...]
    row = iota((32, BIG), 0) + g * 32
    lane = iota((32, BIG), 1)
    wide = jnp.zeros((32, HB), F32)
    q = []
    for p in range(2):
        mb, tb = m[:, p * HB : (p + 1) * HB], t[:, p * HB : (p + 1) * HB]
        ms, ts = (v[:, BIG + p * HS : BIG + (p + 1) * HS] for v in (m, t))
        full = jnp.concatenate([jnp.where(c == 0, mb, tb), jnp.where(c == 0, tb, mb)], axis=1)
        e = jnp.concatenate([jnp.where(c == 0, ms, ts), jnp.where(c == 0, ts, ms)], axis=1)
        moved = pltpu.roll(e, HB - a, 1)
        q.append((full, jnp.concatenate([e, wide], axis=1), jnp.concatenate([moved, wide], axis=1)))
    for i, (k, w) in enumerate(((kb, BIG), (k1, a), (k2, HB - a))):
        live = (row < w) & (lane < w)
        blocks = []
        for p in range(2):
            v = jnp.where(live, pivot[p, k] - q[p][i], 0.0)
            out[p, k] = v
            blocks.append(v)
        term[k] = wr * blocks[1] + wi * blocks[0]
    s = sums[0][...]
    for ref in sums[1:]:
        s = s + ref[...]
    line = iota((24, HB), 1)
    small = s[:, BIG:]
    none = jnp.zeros((24, HB), F32)
    first = jnp.concatenate([jnp.where(line < a, small, 0.0), none], axis=1)
    second = jnp.concatenate(
        [jnp.where(line < HB - a, pltpu.roll(small, HB - a, 1), 0.0), none], axis=1
    )
    full = s[:, :BIG]
    slots = [
        jnp.where(kb == k, full, jnp.where(k1 == k, first, second)) for k in range(3)
    ]
    spread = jnp.concatenate(slots, axis=1)
    terms = [term[k] for k in range(3)]
    for i in range(NZ):
        pay[i, :24] = spread[:, 192 * i : 192 * (i + 1)]
        pay[i, 24:] = jnp.concatenate([v[:, 64 * i : 64 * i + 64] for v in terms], axis=1)
    for i in range(NZ):
        outs[i][...] = pay[lax.rem(z + i, NZ)]


def gather_kernel(*refs):
    pays, keep, send, all_rows = refs[:NZ], refs[NZ], refs[NZ + 1], refs[NZ + 2]
    pole = lax.axis_index("pole")
    z, h = lax.div(pole, NH), lax.rem(pole, NH)
    total = None
    for i, ref in enumerate(pays):
        source = lax.rem(z - i + NZ, NZ)
        all_rows[pl.ds(pl.multiple_of(source * 24, 8), 24), :] = ref[:24]
        total = ref[24:] if total is None else total + ref[24:]
    v = all_rows[...]
    halves = []
    for i in range(NH):
        piv = jnp.concatenate([total[:, 64 * k + 32 * i : 64 * k + 32 * i + 32] for k in range(3)], axis=1)
        halves.append((v[:, 96 * i : 96 * i + 96], piv))
    for ref, (one, two) in ((keep, (0, 1)), (send, (1, 0))):
        ref[:ROWS] = jnp.where(h == 0, halves[one][0], halves[two][0])
        ref[ROWS:] = jnp.where(h == 0, halves[one][1], halves[two][1])


def local(factor_cols, ancestor_inverse, pivot_inverse, structure, widths, pole_weights):
    g, c, x, y = place()
    side = 1 - 2 * c

    def over_grid(v, perm):
        return lax.ppermute(v, "grid", perm)

    def over_pole(v, perm):
        return lax.ppermute(v, "pole", perm)

    block = sds((ROWS, 2 * HC), BF16)
    keep, send = call(
        prep_kernel,
        [block, block],
        [(structure, "s"), (widths, "s"), (factor_cols[0], "v")],
        "prep",
        flops=2 * 2 * ROWS * HB * HB,
    )
    got_mine = over_grid(send, CORE)
    a_own = ancestor_inverse[0].reshape(2 * ROWS, -1)
    a_sib = over_grid(a_own, CORE)
    here = jnp.where(
        c == 0, jnp.concatenate([keep, got_mine], 0), jnp.concatenate([got_mine, keep], 0)
    )
    ahead = over_grid(here, FROM_AHEAD)
    behind = over_grid(here, FROM_BEHIND)
    beside = over_grid(here, FROM_Y)
    got_theirs = over_grid(keep, CORE)
    a_all = jnp.concatenate([a_own, a_sib], axis=0)

    def chip(dx, dy):
        return lax.rem(y + dy, NY) * NX + lax.rem(x + dx + NX, NX)

    def cols(at):
        return lax.dynamic_slice_in_dim(a_all, at * 2 * ROWS, 2 * ROWS, axis=1)

    def add(old, pairs):
        n = len(pairs)
        ins = ([] if old is None else [(old, "v")]) + [(cols(at), "v") for at, _ in pairs]
        ins += [(b, "v") for _, b in pairs]
        return call(
            functools.partial(acc_kernel, n, old is not None),
            [sds((2, ROWS, 2 * HC), F32)],
            ins,
            "product",
            flops=2 * n * 4 * ROWS * 2 * ROWS * 2 * HC,
        )[0]

    big, small = call(
        left_kernel,
        [sds((2, 2, HB, 2 * ROWS), BF16), sds((2, 2, HB, 2 * ROWS), BF16)],
        [(widths, "s"), (keep, "v"), (send, "v"), (got_mine, "v"), (got_theirs, "v")],
        "left",
        flops=2 * 2 * 2 * ROWS * HB * HB,
    )
    far = over_grid(ahead, FROM_AHEAD)
    beside_behind = over_grid(beside, FROM_BEHIND)
    beside_ahead = over_grid(ahead, FROM_Y)
    acc = add(
        None,
        [(chip(0, 0), here), (chip(side, 0), ahead), (chip(-side, 0), behind), (chip(0, 1), beside)],
    )
    beside_far = over_grid(beside_ahead, FROM_AHEAD)
    acc = add(
        acc,
        [(chip(2, 0), far), (chip(-side, 1), beside_behind), (chip(side, 1), beside_ahead)],
    )
    quarter = sds((64, 4 * HB + 2 * HS), F32)
    own, sib, q0, q1, q2, q3 = call(
        column_kernel,
        [sds((ROWS, 2 * HC), F32)] * 2 + [quarter] * 4,
        [
            (structure, "s"),
            (widths, "s"),
            (acc, "v"),
            (cols(chip(2, 1)), "v"),
            (beside_far, "v"),
            (big, "v"),
            (small, "v"),
        ],
        "column",
        flops=2 * 4 * ROWS * 2 * ROWS * 2 * HC + 2 * 2 * 1024 * 2 * ROWS * 768,
        scratch=[
            pltpu.VMEM((2, 2 * ROWS, 2 * HC), BF16),
            pltpu.VMEM((NX, 64, 4 * HB + 2 * HS), F32),
        ],
    )
    q1, q2, q3 = over_grid(q1, from_x(1)), over_grid(q2, from_x(2)), over_grid(q3, from_x(3))
    other = over_grid(sib, CORE)
    share = sds((24, 768), F32)
    spread = call(
        spread_kernel,
        [sds((2, ROWS, 3 * BIG), BF16)] + [share] * NZ,
        [(widths, "s"), (pole_weights, "s"), (own, "v"), (other, "v")],
        "spread",
        scratch=[pltpu.VMEM((ROWS, 768), F32)],
    )
    column_inverse, terms = spread[0], list(spread[1:])
    for i in range(1, NZ):
        terms[i] = over_pole(terms[i], from_z(i))
    rows64 = sds((64, BIG + HB), F32)
    q_keep, q_send = call(
        fold_kernel, [rows64] * 2, [(v, "v") for v in (q0, q1, q2, q3)], "fold"
    )
    q_got = over_grid(q_send, FROM_Y)
    rows32 = sds((32, BIG + HB), F32)
    p_mine, p_send = call(chip_kernel, [rows32] * 2, [(q_keep, "v"), (q_got, "v")], "chip")
    p_got = over_grid(p_send, CORE)
    pay = sds((56, 192), F32)
    pivots = call(
        pivot_kernel,
        [sds((2, 3, 32, BIG), F32)] + [pay] * NZ,
        [(widths, "s"), (pole_weights, "s"), (pivot_inverse[0], "v"), (p_mine, "v"), (p_got, "v")]
        + [(v, "v") for v in terms],
        "pivot",
        scratch=[pltpu.VMEM((3, 32, BIG), F32), pltpu.VMEM((NZ, 56, 192), F32)],
    )
    pivot_block, pays = pivots[0], list(pivots[1:])
    for i in range(1, NZ):
        pays[i] = over_pole(pays[i], from_z(i))
    last = sds((ROWS + 32, 96), F32)
    d_keep, d_send = call(
        gather_kernel,
        [last] * 2,
        [(v, "v") for v in pays],
        "slots",
        scratch=[pltpu.VMEM((ROWS, 192), F32)],
    )
    d_got = over_pole(d_send, FROM_H)
    total = d_keep + d_got
    density_column = total[:ROWS]
    density_pivot = total[ROWS:].reshape(32, 3, 32).transpose(1, 0, 2)
    return (column_inverse[None], pivot_block[None], density_column, density_pivot)


def solution(mesh):
    in_specs = (
        P("pole", None, "grid", None),
        P("pole", None, "grid", None),
        P("pole", None, None, "grid", None),
        P(),
        P(),
        P("pole", None),
    )
    out_specs = (
        P("pole", None, "grid", None),
        P("pole", None, None, "grid", None),
        P("grid", "pole"),
        P(None, "grid", "pole"),
    )
    return jax.shard_map(local, mesh=mesh, in_specs=in_specs, out_specs=out_specs, check_vma=False)
```

time: 648 us -> 138 us (0.21)
  waiting for transfers between devices: 572 us -> 61.5 us
  starting transfers between devices: 0.16 us -> 48.4 us
  matrix products: 26.2 us -> 0 us
  Pallas kernels: 0 us -> 17 us
  local copies, waits for them, and re-layouts: 20.5 us -> 5.63 us
  between operations: 14.1 us -> 0.85 us
  other arithmetic: 13.8 us -> 3.6 us
    unnamed x6 -> x0, waiting for transfers between devices: 399 us -> none
    all_gather x1 -> x0, waiting for transfers between devices: 103 us -> none  [local(): piece = lax.all_gather(masked, 'grid', axis=1, tiled=True)]
    reduce_scatter x1 -> x0, waiting for transfers between devices: 70 us -> none  [local(): lax.psum_scatter(stacked_q, 'grid', scatter_dimension=2, tiled=True)]
    ppermute x0 -> x31, waiting for transfers between devices: none -> 61.5 us  [the longest x16 43.9 us: over_grid(): return lax.ppermute(v, 'grid', perm)]
    ppermute x0 -> x31, starting transfers between devices: none -> 48.4 us  [the longest x15 33.7 us: over_pole(): return lax.ppermute(v, 'pole', perm)]
    dot_general x9 -> x0, matrix products: 26.2 us -> none  [the longest x4 7.88 us: across(): jnp.einsum('rkc,rkd->kcd', first, second, precision=lax.Precision.HIGHEST)]
    pallas_call x0 -> x10, Pallas kernels: none -> 17 us  [call(): pl.pallas_call(body, out_shape=tuple(outs), in_specs=[sm if kind == 's' e...]
    unnamed x36 -> x20, local copies, waits for them, and re-layouts: 13.5 us -> 4.89 us
  transfers between devices with their start and end apart: 4 -> 31, of which waited for: 4 -> 18; matrix products, arithmetic and copies ran while one was open for 2% -> 3% of each run, Pallas kernels for 0% -> 8%
where the time goes in v1:
time: 138 us; the launch traced here: 137 us
  waiting for transfers between devices  61.5 us (45%)
  starting transfers between devices  48.4 us (35%)
  Pallas kernels  17 us (12%)
  local copies, waits for them, and re-layouts  5.63 us (4%)
  other arithmetic  3.6 us (3%)
    ppermute x16, waiting for transfers between devices, over_grid(): return lax.ppermute(v, 'grid', perm)  43.9 us
    ppermute x15, starting transfers between devices, over_pole(): return lax.ppermute(v, 'pole', perm)  33.7 us
    ppermute x15, waiting for transfers between devices, over_pole(): return lax.ppermute(v, 'pole', perm)  17.6 us
    pallas_call x10, Pallas kernels, call(): pl.pallas_call(body, out_shape=tuple(outs), in_specs=[sm if kind == 's' e...  17 us
    ppermute x16, starting transfers between devices, over_grid(): return lax.ppermute(v, 'grid', perm)  14.6 us
    unnamed x20, local copies, waits for them, and re-layouts  4.89 us
    concatenate x2, other arithmetic, local(): a_all = jnp.concatenate([a_own, a_sib], axis=0)  3.4 us
  transfers between devices with their start and end apart: 31, of which 18 were waited for; matrix products, arithmetic and copies ran while one was open for 3% of the time, Pallas kernels for 8%

profile of v1, /device:TPU:8, one launch (start us, length us, event | category | flops | bytes accessed | tf_op | source)
XLA Modules:
  0.0 136.9 jit_solution(5600824852281544111)
XLA Ops:
  3.5 1.6 %prep.1 = (bf16[192,768]{1,0:T(8,128)(2,1)S(1)}, bf16[192,768]{1,0:T(8,128)(2,1)S(1)}) custom-call(s32[96,3]{1,0:T(8,128)S(1)} %copy.14.structure, s32[3]{0:T(128)S(1)} %copy-done.5, bf16[2,192,1536]{2,1,0:T(8,128)(2,1)S(1)} %bitcast.6), custom_call_target="tpu_custom_call" | custom-call | flops 50331648 | bytes 1770636 | tf_op jit(solution)/shard_map/prep/pallas_call | solution.py:86
  7.0 2.8 %collective-permute-start.2 = (bf16[384,768]{1,0:T(8,128)(2,1)S(1)}, bf16[384,768]{1,0:T(8,128)(2,1)}, u32[]{:S(2)}, u32[]{:S(2)}) collective-permute-start(bf16[384,768]{1,0:T(8,128)(2,1)S(1)} %maximum_select_fusion.refs_4_), channel_id=1, source_target_pairs={{2,0},{7,1},{4,2},{1,3},{6,4},{3,5},{0,6},{5,7},{10,8},{15,9},{12,... | collective-permute-start | bytes 1769480 | tf_op jit(solution)/shard_map/ppermute | solution.py:355
  10.3 7.0 %collective-permute-done.2.refs_5_ = bf16[384,768]{1,0:T(8,128)(2,1)} collective-permute-done((bf16[384,768]{1,0:T(8,128)(2,1)S(1)}, bf16[384,768]{1,0:T(8,128)(2,1)}, u32[]{:S(2)}, u32[]{:S(2)}) %collective-permute-start.2) | collective-permute-done | bytes 589856 | tf_op jit(solution)/shard_map/ppermute | solution.py:355
  17.3 2.0 %collective-permute-start.7 = (bf16[384,768]{1,0:T(8,128)(2,1)}, bf16[384,768]{1,0:T(8,128)(2,1)S(1)}, u32[]{:S(2)}, u32[]{:S(2)}) collective-permute-start(bf16[384,768]{1,0:T(8,128)(2,1)} %collective-permute-done.2.refs_5_), channel_id=1, source_target_pairs={{8,0},{9,1},{10,2},{11,3},{12,4},{13,5},{14,6},{15,7},{0,8},{1,9},... | collective-permute-start | bytes 1769480 | tf_op jit(solution)/shard_map/ppermute | solution.py:355
  20.9 2.2 %collective-permute-start.5 = (bf16[384,768]{1,0:T(8,128)(2,1)}, bf16[384,768]{1,0:T(8,128)(2,1)S(1)}, u32[]{:S(2)}, u32[]{:S(2)}) collective-permute-start(bf16[384,768]{1,0:T(8,128)(2,1)} %collective-permute-done.2.refs_5_), channel_id=1, source_target_pairs={{2,0},{7,1},{4,2},{1,3},{6,4},{3,5},{0,6},{5,7},{10,8},{15,9},{12,... | collective-permute-start | bytes 1769480 | tf_op jit(solution)/shard_map/ppermute | solution.py:355
  23.1 3.1 %collective-permute-done.4.refs_7_ = bf16[384,768]{1,0:T(8,128)(2,1)} collective-permute-done((bf16[384,768]{1,0:T(8,128)(2,1)S(1)}, bf16[384,768]{1,0:T(8,128)(2,1)}, u32[]{:S(2)}, u32[]{:S(2)}) %collective-permute-start.4) | collective-permute-done | bytes 589856 | tf_op jit(solution)/shard_map/ppermute | solution.py:355
  27.3 9.3 %collective-permute-done.7.refs_6_ = bf16[384,768]{1,0:T(8,128)(2,1)S(1)} collective-permute-done((bf16[384,768]{1,0:T(8,128)(2,1)}, bf16[384,768]{1,0:T(8,128)(2,1)S(1)}, u32[]{:S(2)}, u32[]{:S(2)}) %collective-permute-start.7) | collective-permute-done | bytes 589856 | tf_op jit(solution)/shard_map/ppermute | solution.py:355
  36.6 2.2 %collective-permute-start.8 = (bf16[384,768]{1,0:T(8,128)(2,1)S(1)}, bf16[384,768]{1,0:T(8,128)(2,1)S(1)}, u32[]{:S(2)}, u32[]{:S(2)}) collective-permute-start(bf16[384,768]{1,0:T(8,128)(2,1)S(1)} %collective-permute-done.7.refs_6_), channel_id=1, source_target_pairs={{2,0},{7,1},{4,2},{1,3},{6,4},{3,5},{0,6},{5,7},{10,8},{15,9},{12,... | collective-permute-start | bytes 1769480 | tf_op jit(solution)/shard_map/ppermute | solution.py:355
  38.8 1.5 %fusion.7 = (bf16[768,384]{1,0:T(8,128)(2,1)S(1)}, bf16[768,384]{1,0:T(8,128)(2,1)S(1)}) fusion(s32[]{:T(128)S(6)} %select_n.40, bf16[384,3072]{1,0:T(8,128)(2,1)} %bitcast.9, bf16[384,3072]{1,0:T(8,128)(2,1)} %collective-permute-done, s32[]{:T(128)S(6)} %select_n.39), kind=kLoop, calls=%fused_computation.23 | loop fusion | flops 2359296 | bytes 5898248 | tf_op jit(solution)/shard_map/concatenate | solution.py:378
  40.8 1.9 %fusion = (bf16[768,384]{1,0:T(8,128)(2,1)S(1)}, bf16[768,384]{1,0:T(8,128)(2,1)S(1)}, bf16[768,384]{1,0:T(8,128)(2,1)S(1)}, bf16[768,384]{1,0:T(8,128)(2,1)S(1)...) fusion(s32[]{:T(128)S(6)} %select_n.41, bf16[384,3072]{1,0:T(8,128)(2,1)S(1)} %bitcast.10, ...), kind=kLoop, calls=%fused_computation.16 | loop fusion | flops 7077888 | bytes 8257560 | tf_op jit(solution)/shard_map/concatenate | solution.py:378
  42.7 4.0 %product.2.refs_0_ = f32[2,192,768]{2,1,0:T(8,128)S(1)} custom-call(bf16[768,384]{1,0:T(8,128)(2,1)S(1)} %get-tuple-element.77.refs_0_, bf16[768,384]{1,0:T(8,128)(2,1)S(1)} %get-tuple-element.78.refs_1_, bf16[768,384]{1,0:T(8,128)(2,1)S(1)} %get-tuple-element.79.refs_2_, bf16[768,384]{1,0:T(8,128)(2,1)S(1)} %get-tuple-element.80.refs_3_, ...), custom_call_target="tpu_custom_call" | custom-call | flops 1811939328 | bytes 5898240 | tf_op jit(solution)/shard_map/product/pallas_call | solution.py:86
  47.3 2.0 %product.3.old = f32[2,192,768]{2,1,0:T(8,128)S(1)} custom-call(f32[2,192,768]{2,1,0:T(8,128)S(1)} %product.2.refs_0_, bf16[768,384]{1,0:T(8,128)(2,1)S(1)} %get-tuple-element.81.refs_1_, bf16[768,384]{1,0:T(8,128)(2,1)S(1)} %get-tuple-element.83.refs_2_, bf16[768,384]{1,0:T(8,128)(2,1)S(1)} %get-tuple-element.82.refs_3_, ...), custom_call_target="tpu_custom_call" | custom-call | flops 1358954496 | bytes 5898240 | tf_op jit(solution)/shard_map/product/pallas_call | solution.py:86
  50.3 4.5 %column.1 = (f32[192,768]{1,0:T(8,128)S(1)}, f32[192,768]{1,0:T(8,128)S(1)}, f32[64,1280]{1,0:T(8,128)S(1)}, f32[64,1280]{1,0:T(8,128)S(1)}, f32[64,1280]{1,0:T(8,128)S(1)}, /*index=5*/f32[64,1280]{1,0:T(8,128)S(1)}) custom-call(s32[96,3]{1,0:T(8,128)S(1)} %copy-done.4, s32[3]{0:T(128)S(1)} %copy-done.6, f32[2,192,768]{2,1,0:T(8,128)} %copy-done.1, ...), custom_call_target="tpu_custom_call" | custom-call | flops 1660944384 | bytes 6423692 | tf_op jit(solution)/shard_map/column/pallas_call | solution.py:86
  55.1 2.2 %collective-permute-start.12 = (f32[64,1280]{1,0:T(8,128)S(1)}, f32[64,1280]{1,0:T(8,128)S(1)}, u32[]{:S(2)}, u32[]{:S(2)}) collective-permute-start(f32[64,1280]{1,0:T(8,128)S(1)} %get-tuple-element.47), channel_id=1, source_target_pairs={{4,0},{5,1},{6,2},{7,3},{0,4},{1,5},{2,6},{3,7},{12,8},{13,9},{14,... | collective-permute-start | bytes 983048 | tf_op jit(solution)/shard_map/ppermute | solution.py:355
  58.5 14.8 %collective-permute-done.11.q1 = f32[64,1280]{1,0:T(8,128)S(1)} collective-permute-done((f32[64,1280]{1,0:T(8,128)S(1)}, f32[64,1280]{1,0:T(8,128)S(1)}, u32[]{:S(2)}, u32[]{:S(2)}) %collective-permute-start.11) | collective-permute-done | bytes 327712 | tf_op jit(solution)/shard_map/ppermute | solution.py:355
  74.4 5.9 %collective-permute-done.14.got = f32[64,768]{1,0:T(8,128)S(1)} collective-permute-done((f32[64,768]{1,0:T(8,128)S(1)}, f32[64,768]{1,0:T(8,128)S(1)}, u32[]{:S(2)}, u32[]{:S(2)}) %collective-permute-start.14) | collective-permute-done | bytes 196640 | tf_op jit(solution)/shard_map/ppermute | solution.py:355
  80.4 2.0 %spread.1 = (bf16[2,192,1536]{2,1,0:T(8,128)(2,1)}, f32[24,768]{1,0:T(8,128)S(1)}, f32[24,768]{1,0:T(8,128)S(1)}, f32[24,768]{1,0:T(8,128)S(1)}, f32[24,768]{1,0...) custom-call(s32[3]{0:T(128)S(1)} %copy-done.6, ...), custom_call_target="tpu_custom_call" | custom-call | bytes 2949140 | tf_op jit(solution)/shard_map/spread/pallas_call | solution.py:86
  83.3 3.3 %collective-permute-start.17 = (f32[24,768]{1,0:T(8,128)S(1)}, f32[24,768]{1,0:T(8,128)S(1)}, u32[]{:S(2)}, u32[]{:S(2)}) collective-permute-start(f32[24,768]{1,0:T(8,128)S(1)} %get-tuple-element.55), channel_id=1, source_target_pairs={{192,0},{208,16},{224,32},{240,48},{0,64},{16,80},{32,96},{48,112}... | collective-permute-start | bytes 221192 | tf_op jit(solution)/shard_map/ppermute | solution.py:358
  86.6 4.0 %collective-permute-start.18 = (f32[24,768]{1,0:T(8,128)S(1)}, f32[24,768]{1,0:T(8,128)S(1)}, u32[]{:S(2)}, u32[]{:S(2)}) collective-permute-start(f32[24,768]{1,0:T(8,128)S(1)} %get-tuple-element.56), channel_id=1, source_target_pairs={{160,0},{176,16},{192,32},{208,48},{224,64},{240,80},{0,96},{16,11... | collective-permute-start | bytes 221192 | tf_op jit(solution)/shard_map/ppermute | solution.py:358
  91.2 4.9 %collective-permute-start.20 = (f32[24,768]{1,0:T(8,128)S(1)}, f32[24,768]{1,0:T(8,128)S(1)}, u32[]{:S(2)}, u32[]{:S(2)}) collective-permute-start(f32[24,768]{1,0:T(8,128)S(1)} %get-tuple-element.58), channel_id=1, source_target_pairs={{96,0},{112,16},{128,32},{144,48},{160,64},{176,80},{192,96},{208,... | collective-permute-start | bytes 221192 | tf_op jit(solution)/shard_map/ppermute | solution.py:358
  96.1 2.7 %collective-permute-start.21 = (f32[24,768]{1,0:T(8,128)S(1)}, f32[24,768]{1,0:T(8,128)S(1)}, u32[]{:S(2)}, u32[]{:S(2)}) collective-permute-start(f32[24,768]{1,0:T(8,128)S(1)} %get-tuple-element.59), channel_id=1, source_target_pairs={{64,0},{80,16},{96,32},{112,48},{128,64},{144,80},{160,96},{176,11... | collective-permute-start | bytes 221192 | tf_op jit(solution)/shard_map/ppermute | solution.py:358
  99.8 1.5 %collective-permute-done.18.rest_3_ = f32[24,768]{1,0:T(8,128)S(1)} collective-permute-done((f32[24,768]{1,0:T(8,128)S(1)}, f32[24,768]{1,0:T(8,128)S(1)}, u32[]{:S(2)}, u32[]{:S(2)}) %collective-permute-start.18) | collective-permute-done | bytes 73760 | tf_op jit(solution)/shard_map/ppermute | solution.py:358
  101.3 4.5 %collective-permute-done.20.rest_5_ = f32[24,768]{1,0:T(8,128)S(1)} collective-permute-done((f32[24,768]{1,0:T(8,128)S(1)}, f32[24,768]{1,0:T(8,128)S(1)}, u32[]{:S(2)}, u32[]{:S(2)}) %collective-permute-start.20) | collective-permute-done | bytes 73760 | tf_op jit(solution)/shard_map/ppermute | solution.py:358
  107.4 1.5 %pivot.1 = (f32[2,3,32,512]{3,2,1,0:T(8,128)}, f32[56,192]{1,0:T(8,128)S(1)}, f32[56,192]{1,0:T(8,128)S(1)}, f32[56,192]{1,0:T(8,128)S(1)}, f32[56,192]{1,0:T(8,...) custom-call(s32[3]{0:T(128)S(1)} %copy-done.6, ...), custom_call_target="tpu_custom_call" | custom-call | bytes 1916948 | tf_op jit(solution)/shard_map/pivot/pallas_call | solution.py:86
  108.9 2.1 %collective-permute-start.23 = (f32[56,192]{1,0:T(8,128)S(1)}, f32[56,192]{1,0:T(8,128)S(1)}, u32[]{:S(2)}, u32[]{:S(2)}) collective-permute-start(f32[56,192]{1,0:T(8,128)S(1)} %get-tuple-element.63), channel_id=1, source_target_pairs={{224,0},{240,16},{0,32},{16,48},{32,64},{48,80},{64,96},{80,112},{... | collective-permute-start | bytes 129032 | tf_op jit(solution)/shard_map/ppermute | solution.py:358
  112.2 2.3 %collective-permute-start.25 = (f32[56,192]{1,0:T(8,128)S(1)}, f32[56,192]{1,0:T(8,128)S(1)}, u32[]{:S(2)}, u32[]{:S(2)}) collective-permute-start(f32[56,192]{1,0:T(8,128)S(1)} %get-tuple-element.65), channel_id=1, source_target_pairs={{160,0},{176,16},{192,32},{208,48},{224,64},{240,80},{0,96},{16,11... | collective-permute-start | bytes 129032 | tf_op jit(solution)/shard_map/ppermute | solution.py:358
  114.5 3.0 %collective-permute-start.26 = (f32[56,192]{1,0:T(8,128)S(1)}, f32[56,192]{1,0:T(8,128)S(1)}, u32[]{:S(2)}, u32[]{:S(2)}) collective-permute-start(f32[56,192]{1,0:T(8,128)S(1)} %get-tuple-element.66), channel_id=1, source_target_pairs={{128,0},{144,16},{160,32},{176,48},{192,64},{208,80},{224,96},{240... | collective-permute-start | bytes 129032 | tf_op jit(solution)/shard_map/ppermute | solution.py:358
  117.5 2.9 %collective-permute-start.27 = (f32[56,192]{1,0:T(8,128)S(1)}, f32[56,192]{1,0:T(8,128)S(1)}, u32[]{:S(2)}, u32[]{:S(2)}) collective-permute-start(f32[56,192]{1,0:T(8,128)S(1)} %get-tuple-element.67), channel_id=1, source_target_pairs={{96,0},{112,16},{128,32},{144,48},{160,64},{176,80},{192,96},{208,... | collective-permute-start | bytes 129032 | tf_op jit(solution)/shard_map/ppermute | solution.py:358
  123.6 2.1 %collective-permute-done.27.refs_5_ = f32[56,192]{1,0:T(8,128)S(1)} collective-permute-done((f32[56,192]{1,0:T(8,128)S(1)}, f32[56,192]{1,0:T(8,128)S(1)}, u32[]{:S(2)}, u32[]{:S(2)}) %collective-permute-start.27) | collective-permute-done | bytes 43040 | tf_op jit(solution)/shard_map/ppermute | solution.py:358
  125.7 3.0 %collective-permute-done.28.refs_6_ = f32[56,192]{1,0:T(8,128)S(1)} collective-permute-done((f32[56,192]{1,0:T(8,128)S(1)}, f32[56,192]{1,0:T(8,128)S(1)}, u32[]{:S(2)}, u32[]{:S(2)}) %collective-permute-start.28) | collective-permute-done | bytes 43040 | tf_op jit(solution)/shard_map/ppermute | solution.py:358
  129.1 2.4 %collective-permute-start.30 = (f32[224,96]{1,0:T(8,128)S(1)}, f32[224,96]{1,0:T(8,128)S(1)}, u32[]{:S(2)}, u32[]{:S(2)}) collective-permute-start(f32[224,96]{1,0:T(8,128)S(1)} %get-tuple-element.71), channel_id=1, source_target_pairs={{16,0},{0,16},{48,32},{32,48},{80,64},{64,80},{112,96},{96,112},{1... | collective-permute-start | bytes 258056 | tf_op jit(solution)/shard_map/ppermute | solution.py:358
  131.5 4.0 %collective-permute-done.30 = f32[224,96]{1,0:T(8,128)S(1)} collective-permute-done((f32[224,96]{1,0:T(8,128)S(1)}, f32[224,96]{1,0:T(8,128)S(1)}, u32[]{:S(2)}, u32[]{:S(2)}) %collective-permute-start.30) | collective-permute-done | bytes 86048 | tf_op jit(solution)/shard_map/ppermute | solution.py:358
  (67 shorter events, 22.8 us)
Async XLA Ops:
  0.6 38.1 %collective-permute-start = (bf16[384,3072]{1,0:T(8,128)(2,1)}, bf16[384,3072]{1,0:T(8,128)(2,1)}, u32[]{:S(2)}, u32[]{:S(2)}) collective-permute-start(bf16[384,3072]{1,0:T(8,128)(2,1)} %bitcast.8), channel_id=1, source_target_pairs={{1,0},{0,1},{3,2},{2,3},{5,4},{4,5},{7,6},{6,7},{9,8},{8,9},{11,10... | collective-permute-start | bytes 7077896 | tf_op jit(solution)/shard_map/ppermute | solution.py:355
  5.1 1.8 %collective-permute-start.1 = (bf16[192,768]{1,0:T(8,128)(2,1)S(1)}, bf16[192,768]{1,0:T(8,128)(2,1)S(1)}, u32[]{:S(2)}, u32[]{:S(2)}) collective-permute-start(bf16[192,768]{1,0:T(8,128)(2,1)S(1)} %get-tuple-element.39.send), channel_id=1, source_target_pairs={{1,0},{0,1},{3,2},{2,3},{5,4},{4,5},{7,6},{6,7},{9,8},{8,9},{11,10... | collective-permute-start | bytes 884744 | tf_op jit(solution)/shard_map/ppermute | solution.py:355
  7.0 10.2 %collective-permute-start.2 = (bf16[384,768]{1,0:T(8,128)(2,1)S(1)}, bf16[384,768]{1,0:T(8,128)(2,1)}, u32[]{:S(2)}, u32[]{:S(2)}) collective-permute-start(bf16[384,768]{1,0:T(8,128)(2,1)S(1)} %maximum_select_fusion.refs_4_), channel_id=1, source_target_pairs={{2,0},{7,1},{4,2},{1,3},{6,4},{3,5},{0,6},{5,7},{10,8},{15,9},{12,... | collective-permute-start | bytes 1769480 | tf_op jit(solution)/shard_map/ppermute | solution.py:355
  9.9 16.4 %collective-permute-start.4 = (bf16[384,768]{1,0:T(8,128)(2,1)S(1)}, bf16[384,768]{1,0:T(8,128)(2,1)}, u32[]{:S(2)}, u32[]{:S(2)}) collective-permute-start(bf16[384,768]{1,0:T(8,128)(2,1)S(1)} %maximum_select_fusion.refs_4_), channel_id=1, source_target_pairs={{8,0},{9,1},{10,2},{11,3},{12,4},{13,5},{14,6},{15,7},{0,8},{1,9},... | collective-permute-start | bytes 1769480 | tf_op jit(solution)/shard_map/ppermute | solution.py:355
  17.3 19.3 %collective-permute-start.7 = (bf16[384,768]{1,0:T(8,128)(2,1)}, bf16[384,768]{1,0:T(8,128)(2,1)S(1)}, u32[]{:S(2)}, u32[]{:S(2)}) collective-permute-start(bf16[384,768]{1,0:T(8,128)(2,1)} %collective-permute-done.2.refs_5_), channel_id=1, source_target_pairs={{8,0},{9,1},{10,2},{11,3},{12,4},{13,5},{14,6},{15,7},{0,8},{1,9},... | collective-permute-start | bytes 1769480 | tf_op jit(solution)/shard_map/ppermute | solution.py:355
  19.3 1.6 %collective-permute-start.9 = (bf16[192,768]{1,0:T(8,128)(2,1)S(1)}, bf16[192,768]{1,0:T(8,128)(2,1)S(1)}, u32[]{:S(2)}, u32[]{:S(2)}) collective-permute-start(bf16[192,768]{1,0:T(8,128)(2,1)S(1)} %get-tuple-element.38.keep), channel_id=1, source_target_pairs={{1,0},{0,1},{3,2},{2,3},{5,4},{4,5},{7,6},{6,7},{9,8},{8,9},{11,10... | collective-permute-start | bytes 884744 | tf_op jit(solution)/shard_map/ppermute | solution.py:355
  19.4 23.3 %collective-permute-start.3 = (bf16[384,768]{1,0:T(8,128)(2,1)S(1)}, bf16[384,768]{1,0:T(8,128)(2,1)}, u32[]{:S(2)}, u32[]{:S(2)}) collective-permute-start(bf16[384,768]{1,0:T(8,128)(2,1)S(1)} %maximum_select_fusion.refs_4_), channel_id=1, source_target_pairs={{6,0},{3,1},{0,2},{5,3},{2,4},{7,5},{4,6},{1,7},{14,8},{11,9},{8,1... | collective-permute-start | bytes 1769480 | tf_op jit(solution)/shard_map/ppermute | solution.py:355
  20.9 25.9 %collective-permute-start.5 = (bf16[384,768]{1,0:T(8,128)(2,1)}, bf16[384,768]{1,0:T(8,128)(2,1)S(1)}, u32[]{:S(2)}, u32[]{:S(2)}) collective-permute-start(bf16[384,768]{1,0:T(8,128)(2,1)} %collective-permute-done.2.refs_5_), channel_id=1, source_target_pairs={{2,0},{7,1},{4,2},{1,3},{6,4},{3,5},{0,6},{5,7},{10,8},{15,9},{12,... | collective-permute-start | bytes 1769480 | tf_op jit(solution)/shard_map/ppermute | solution.py:355
  26.2 21.1 %collective-permute-start.6 = (bf16[384,768]{1,0:T(8,128)(2,1)}, bf16[384,768]{1,0:T(8,128)(2,1)S(1)}, u32[]{:S(2)}, u32[]{:S(2)}) collective-permute-start(bf16[384,768]{1,0:T(8,128)(2,1)} %collective-permute-done.4.refs_7_), channel_id=1, source_target_pairs={{6,0},{3,1},{0,2},{5,3},{2,4},{7,5},{4,6},{1,7},{14,8},{11,9},{8,1... | collective-permute-start | bytes 1769480 | tf_op jit(solution)/shard_map/ppermute | solution.py:355
  36.6 13.8 %collective-permute-start.8 = (bf16[384,768]{1,0:T(8,128)(2,1)S(1)}, bf16[384,768]{1,0:T(8,128)(2,1)S(1)}, u32[]{:S(2)}, u32[]{:S(2)}) collective-permute-start(bf16[384,768]{1,0:T(8,128)(2,1)S(1)} %collective-permute-done.7.refs_6_), channel_id=1, source_target_pairs={{2,0},{7,1},{4,2},{1,3},{6,4},{3,5},{0,6},{5,7},{10,8},{15,9},{12,... | collective-permute-start | bytes 1769480 | tf_op jit(solution)/shard_map/ppermute | solution.py:355
  54.9 25.5 %collective-permute-start.10 = (f32[192,768]{1,0:T(8,128)S(1)}, f32[192,768]{1,0:T(8,128)S(1)}, u32[]{:S(2)}, u32[]{:S(2)}) collective-permute-start(f32[192,768]{1,0:T(8,128)S(1)} %get-tuple-element.43), channel_id=1, source_target_pairs={{1,0},{0,1},{3,2},{2,3},{5,4},{4,5},{7,6},{6,7},{9,8},{8,9},{11,10... | collective-permute-start | bytes 1769480 | tf_op jit(solution)/shard_map/ppermute | solution.py:355
  55.0 18.4 %collective-permute-start.11 = (f32[64,1280]{1,0:T(8,128)S(1)}, f32[64,1280]{1,0:T(8,128)S(1)}, u32[]{:S(2)}, u32[]{:S(2)}) collective-permute-start(f32[64,1280]{1,0:T(8,128)S(1)} %get-tuple-element.46), channel_id=1, source_target_pairs={{6,0},{7,1},{0,2},{1,3},{2,4},{3,5},{4,6},{5,7},{14,8},{15,9},{8,1... | collective-permute-start | bytes 983048 | tf_op jit(solution)/shard_map/ppermute | solution.py:355
  55.1 18.3 %collective-permute-start.12 = (f32[64,1280]{1,0:T(8,128)S(1)}, f32[64,1280]{1,0:T(8,128)S(1)}, u32[]{:S(2)}, u32[]{:S(2)}) collective-permute-start(f32[64,1280]{1,0:T(8,128)S(1)} %get-tuple-element.47), channel_id=1, source_target_pairs={{4,0},{5,1},{6,2},{7,3},{0,4},{1,5},{2,6},{3,7},{12,8},{13,9},{14,... | collective-permute-start | bytes 983048 | tf_op jit(solution)/shard_map/ppermute | solution.py:355
  57.3 16.7 %collective-permute-start.13 = (f32[64,1280]{1,0:T(8,128)S(1)}, f32[64,1280]{1,0:T(8,128)S(1)}, u32[]{:S(2)}, u32[]{:S(2)}) collective-permute-start(f32[64,1280]{1,0:T(8,128)S(1)} %get-tuple-element.48), channel_id=1, source_target_pairs={{2,0},{3,1},{4,2},{5,3},{6,4},{7,5},{0,6},{1,7},{10,8},{11,9},{12,... | collective-permute-start | bytes 983048 | tf_op jit(solution)/shard_map/ppermute | solution.py:355
  74.0 33.4 %copy-start.2 = (f32[1,2,3,32,512]{4,3,2,1,0:T(8,128)S(1)}, f32[1,2,3,32,512]{4,3,2,1,0:T(8,128)}, u32[]{:S(2)}) copy-start(f32[1,2,3,32,512]{4,3,2,1,0:T(8,128)} %param.8) | copy-start | bytes 1179652
  74.1 6.2 %collective-permute-start.14 = (f32[64,768]{1,0:T(8,128)S(1)}, f32[64,768]{1,0:T(8,128)S(1)}, u32[]{:S(2)}, u32[]{:S(2)}) collective-permute-start(f32[64,768]{1,0:T(8,128)S(1)} %get-tuple-element.50), channel_id=1, source_target_pairs={{8,0},{9,1},{10,2},{11,3},{12,4},{13,5},{14,6},{15,7},{0,8},{1,9},... | collective-permute-start | bytes 589832 | tf_op jit(solution)/shard_map/ppermute | solution.py:355
  80.3 10.9 %collective-permute-start.15 = (f32[32,768]{1,0:T(8,128)S(1)}, f32[32,768]{1,0:T(8,128)S(1)}, u32[]{:S(2)}, u32[]{:S(2)}) collective-permute-start(f32[32,768]{1,0:T(8,128)S(1)} %get-tuple-element.52), channel_id=1, source_target_pairs={{1,0},{0,1},{3,2},{2,3},{5,4},{4,5},{7,6},{6,7},{9,8},{8,9},{11,10... | collective-permute-start | bytes 294920 | tf_op jit(solution)/shard_map/ppermute | solution.py:355
  82.4 13.7 %collective-permute-start.16 = (f32[24,768]{1,0:T(8,128)S(1)}, f32[24,768]{1,0:T(8,128)S(1)}, u32[]{:S(2)}, u32[]{:S(2)}) collective-permute-start(f32[24,768]{1,0:T(8,128)S(1)} %get-tuple-element.54), channel_id=1, source_target_pairs={{224,0},{240,16},{0,32},{16,48},{32,64},{48,80},{64,96},{80,112},{... | collective-permute-start | bytes 221192 | tf_op jit(solution)/shard_map/ppermute | solution.py:358
  83.3 15.5 %collective-permute-start.17 = (f32[24,768]{1,0:T(8,128)S(1)}, f32[24,768]{1,0:T(8,128)S(1)}, u32[]{:S(2)}, u32[]{:S(2)}) collective-permute-start(f32[24,768]{1,0:T(8,128)S(1)} %get-tuple-element.55), channel_id=1, source_target_pairs={{192,0},{208,16},{224,32},{240,48},{0,64},{16,80},{32,96},{48,112}... | collective-permute-start | bytes 221192 | tf_op jit(solution)/shard_map/ppermute | solution.py:358
  86.6 14.7 %collective-permute-start.18 = (f32[24,768]{1,0:T(8,128)S(1)}, f32[24,768]{1,0:T(8,128)S(1)}, u32[]{:S(2)}, u32[]{:S(2)}) collective-permute-start(f32[24,768]{1,0:T(8,128)S(1)} %get-tuple-element.56), channel_id=1, source_target_pairs={{160,0},{176,16},{192,32},{208,48},{224,64},{240,80},{0,96},{16,11... | collective-permute-start | bytes 221192 | tf_op jit(solution)/shard_map/ppermute | solution.py:358
  90.7 10.7 %collective-permute-start.19 = (f32[24,768]{1,0:T(8,128)S(1)}, f32[24,768]{1,0:T(8,128)S(1)}, u32[]{:S(2)}, u32[]{:S(2)}) collective-permute-start(f32[24,768]{1,0:T(8,128)S(1)} %get-tuple-element.57), channel_id=1, source_target_pairs={{128,0},{144,16},{160,32},{176,48},{192,64},{208,80},{224,96},{240... | collective-permute-start | bytes 221192 | tf_op jit(solution)/shard_map/ppermute | solution.py:358
  91.2 14.6 %collective-permute-start.20 = (f32[24,768]{1,0:T(8,128)S(1)}, f32[24,768]{1,0:T(8,128)S(1)}, u32[]{:S(2)}, u32[]{:S(2)}) collective-permute-start(f32[24,768]{1,0:T(8,128)S(1)} %get-tuple-element.58), channel_id=1, source_target_pairs={{96,0},{112,16},{128,32},{144,48},{160,64},{176,80},{192,96},{208,... | collective-permute-start | bytes 221192 | tf_op jit(solution)/shard_map/ppermute | solution.py:358
  96.1 10.8 %collective-permute-start.21 = (f32[24,768]{1,0:T(8,128)S(1)}, f32[24,768]{1,0:T(8,128)S(1)}, u32[]{:S(2)}, u32[]{:S(2)}) collective-permute-start(f32[24,768]{1,0:T(8,128)S(1)} %get-tuple-element.59), channel_id=1, source_target_pairs={{64,0},{80,16},{96,32},{112,48},{128,64},{144,80},{160,96},{176,11... | collective-permute-start | bytes 221192 | tf_op jit(solution)/shard_map/ppermute | solution.py:358
  98.8 8.6 %collective-permute-start.22 = (f32[24,768]{1,0:T(8,128)S(1)}, f32[24,768]{1,0:T(8,128)S(1)}, u32[]{:S(2)}, u32[]{:S(2)}) collective-permute-start(f32[24,768]{1,0:T(8,128)S(1)} %get-tuple-element.60), channel_id=1, source_target_pairs={{32,0},{48,16},{64,32},{80,48},{96,64},{112,80},{128,96},{144,112}... | collective-permute-start | bytes 221192 | tf_op jit(solution)/shard_map/ppermute | solution.py:358
  108.9 11.5 %collective-permute-start.23 = (f32[56,192]{1,0:T(8,128)S(1)}, f32[56,192]{1,0:T(8,128)S(1)}, u32[]{:S(2)}, u32[]{:S(2)}) collective-permute-start(f32[56,192]{1,0:T(8,128)S(1)} %get-tuple-element.63), channel_id=1, source_target_pairs={{224,0},{240,16},{0,32},{16,48},{32,64},{48,80},{64,96},{80,112},{... | collective-permute-start | bytes 129032 | tf_op jit(solution)/shard_map/ppermute | solution.py:358
  111.0 10.7 %collective-permute-start.24 = (f32[56,192]{1,0:T(8,128)S(1)}, f32[56,192]{1,0:T(8,128)S(1)}, u32[]{:S(2)}, u32[]{:S(2)}) collective-permute-start(f32[56,192]{1,0:T(8,128)S(1)} %get-tuple-element.64), channel_id=1, source_target_pairs={{192,0},{208,16},{224,32},{240,48},{0,64},{16,80},{32,96},{48,112}... | collective-permute-start | bytes 129032 | tf_op jit(solution)/shard_map/ppermute | solution.py:358
  112.2 10.6 %collective-permute-start.25 = (f32[56,192]{1,0:T(8,128)S(1)}, f32[56,192]{1,0:T(8,128)S(1)}, u32[]{:S(2)}, u32[]{:S(2)}) collective-permute-start(f32[56,192]{1,0:T(8,128)S(1)} %get-tuple-element.65), channel_id=1, source_target_pairs={{160,0},{176,16},{192,32},{208,48},{224,64},{240,80},{0,96},{16,11... | collective-permute-start | bytes 129032 | tf_op jit(solution)/shard_map/ppermute | solution.py:358
  114.5 9.1 %collective-permute-start.26 = (f32[56,192]{1,0:T(8,128)S(1)}, f32[56,192]{1,0:T(8,128)S(1)}, u32[]{:S(2)}, u32[]{:S(2)}) collective-permute-start(f32[56,192]{1,0:T(8,128)S(1)} %get-tuple-element.66), channel_id=1, source_target_pairs={{128,0},{144,16},{160,32},{176,48},{192,64},{208,80},{224,96},{240... | collective-permute-start | bytes 129032 | tf_op jit(solution)/shard_map/ppermute | solution.py:358
  117.5 8.2 %collective-permute-start.27 = (f32[56,192]{1,0:T(8,128)S(1)}, f32[56,192]{1,0:T(8,128)S(1)}, u32[]{:S(2)}, u32[]{:S(2)}) collective-permute-start(f32[56,192]{1,0:T(8,128)S(1)} %get-tuple-element.67), channel_id=1, source_target_pairs={{96,0},{112,16},{128,32},{144,48},{160,64},{176,80},{192,96},{208,... | collective-permute-start | bytes 129032 | tf_op jit(solution)/shard_map/ppermute | solution.py:358
  120.4 8.3 %collective-permute-start.28 = (f32[56,192]{1,0:T(8,128)S(1)}, f32[56,192]{1,0:T(8,128)S(1)}, u32[]{:S(2)}, u32[]{:S(2)}) collective-permute-start(f32[56,192]{1,0:T(8,128)S(1)} %get-tuple-element.68), channel_id=1, source_target_pairs={{64,0},{80,16},{96,32},{112,48},{128,64},{144,80},{160,96},{176,11... | collective-permute-start | bytes 129032 | tf_op jit(solution)/shard_map/ppermute | solution.py:358
  121.7 7.1 %collective-permute-start.29 = (f32[56,192]{1,0:T(8,128)S(1)}, f32[56,192]{1,0:T(8,128)S(1)}, u32[]{:S(2)}, u32[]{:S(2)}) collective-permute-start(f32[56,192]{1,0:T(8,128)S(1)} %get-tuple-element.69), channel_id=1, source_target_pairs={{32,0},{48,16},{64,32},{80,48},{96,64},{112,80},{128,96},{144,112}... | collective-permute-start | bytes 129032 | tf_op jit(solution)/shard_map/ppermute | solution.py:358
  129.1 6.4 %collective-permute-start.30 = (f32[224,96]{1,0:T(8,128)S(1)}, f32[224,96]{1,0:T(8,128)S(1)}, u32[]{:S(2)}, u32[]{:S(2)}) collective-permute-start(f32[224,96]{1,0:T(8,128)S(1)} %get-tuple-element.71), channel_id=1, source_target_pairs={{16,0},{0,16},{48,32},{32,48},{80,64},{64,80},{112,96},{96,112},{1... | collective-permute-start | bytes 258056 | tf_op jit(solution)/shard_map/ppermute | solution.py:358
  (8 other events, 59.9 us)

commit v2 on v1

v2 whole, which is shorter than its diff:
```python
import functools

import jax
import jax.numpy as jnp
from jax import lax
from jax.experimental import pallas as pl
from jax.experimental.pallas import tpu as pltpu
from jax.sharding import PartitionSpec as P

F32 = jnp.float32
BF16 = jnp.bfloat16
BIG = 512
ROWS = 192
HB = 256
HS = 128
HC = HB + HS

NX, NY, NCORE = 4, 2, 2
NZ, NH = 8, 2


def grid_perm(source):
    def at(y, x, c):
        return (y * NX + x % NX) * NCORE + c

    return [
        (at(*source(y, x, c)), at(y, x, c)) for y in range(NY) for x in range(NX) for c in range(NCORE)
    ]


CORE = grid_perm(lambda y, x, c: (y, x, 1 - c))
FROM_AHEAD = grid_perm(lambda y, x, c: (y, x + 1 - 2 * c, c))
FROM_BEHIND = grid_perm(lambda y, x, c: (y, x - 1 + 2 * c, c))
FROM_Y = grid_perm(lambda y, x, c: (1 - y, x, c))


def pole_perm(source):
    def at(z, h):
        return z * NH + h

    return [(at(*source(z, h)), at(z, h)) for z in range(NZ) for h in range(NH)]


Z_PAIR = pole_perm(lambda z, h: (z ^ 1, h))
Z_GROUPS = [[z * NH + h for z in range(b, NZ, 2) for h in range(NH)] for b in range(2)]


def place():
    g = lax.axis_index("grid")
    c = lax.rem(g, 2)
    x = lax.rem(lax.div(g, 2), NX)
    y = lax.div(g, 2 * NX)
    return g, c, x, y


def parity():
    return lax.rem(lax.div(lax.axis_index("pole"), NH), 2)


def slot(i, bit):
    return 4 * (i // 2) + 2 * bit + i % 2


def supers(widths):
    kb = jnp.where(widths[0] == BIG, 0, jnp.where(widths[1] == BIG, 1, 2))
    k1 = jnp.where(kb == 0, 1, 0)
    k2 = jnp.where(kb == 2, 1, 2)
    return kb, k1, k2, widths[k1]


def iota(shape, axis):
    return lax.broadcasted_iota(jnp.int32, shape, axis)


def row_mask(structure, block, count, k, lanes):
    return jnp.concatenate(
        [jnp.full((32, lanes), structure[block + i, k].astype(F32), F32) for i in range(count)], axis=0
    )


def call(body, outs, ins, name, flops=0, scratch=(), blocks=None, limit=16, out_space=pltpu.VMEM):
    specs = []
    for a, kind in ins:
        if kind == "s":
            specs.append(pl.BlockSpec(memory_space=pltpu.SMEM))
        elif kind == "v":
            specs.append(pl.BlockSpec(memory_space=pltpu.VMEM))
        else:
            specs.append(pl.BlockSpec((a.shape[0], 2 * ROWS), lambda i, at, n=kind[0]: (0, at[n])))
    size = sum(a.size * a.dtype.itemsize for a, kind in ins if kind in ("s", "v")) + sum(
        o.size * o.dtype.itemsize for o in outs
    )
    common = dict(
        out_shape=tuple(pltpu.HBM(o.shape, o.dtype) for o in outs) if out_space is pltpu.HBM else tuple(outs),
        compiler_params=pltpu.CompilerParams(vmem_limit_bytes=limit * 1024 * 1024),
        cost_estimate=pl.CostEstimate(flops=flops, bytes_accessed=size, transcendentals=0),
        name=name,
    )
    out_specs = tuple(pl.BlockSpec(memory_space=out_space) for _ in outs)
    operands = [a for a, _ in ins]
    if blocks is None:
        return pl.pallas_call(
            body, in_specs=specs, out_specs=out_specs, scratch_shapes=list(scratch), **common
        )(*operands)
    grid_spec = pltpu.PrefetchScalarGridSpec(
        num_scalar_prefetch=1,
        grid=(1,),
        in_specs=specs,
        out_specs=out_specs,
        scratch_shapes=list(scratch),
    )
    return pl.pallas_call(body, grid_spec=grid_spec, **common)(jnp.stack(blocks), *operands)


def sds(shape, dtype):
    return jax.ShapeDtypeStruct(shape, dtype)


def prep_kernel(structure, widths, f, keep, send):
    g, c, _, _ = place()
    kb, k1, k2, a = supers(widths)
    base = g * 6
    mask_b = row_mask(structure, base, 6, kb, HB).astype(BF16)
    mask_1 = row_mask(structure, base, 6, k1, HB).astype(BF16)
    mask_2 = row_mask(structure, base, 6, k2, HB).astype(BF16)
    shift = (iota((HB, HB), 0) + a == iota((HB, HB), 1)).astype(BF16)
    first = iota((ROWS, HB), 1) < a

    def at(k, part):
        return pl.ds(pl.multiple_of(k * BIG + part * HB, HB), HB)

    for p in range(2):
        o = p * HC
        keep[:, o : o + HB] = f[p, :, at(kb, c)] * mask_b
        send[:, o : o + HB] = f[p, :, at(kb, 1 - c)] * mask_b
        one = (f[p, :, at(k1, 0)] * mask_1).astype(F32)
        two = jnp.dot(f[p, :, at(k2, 0)] * mask_2, shift, preferred_element_type=F32)
        small = jnp.where(first, one, two)
        low, high = small[:, :HS], small[:, HS:]
        keep[:, o + HB : o + HC] = jnp.where(c == 0, low, high).astype(BF16)
        send[:, o + HB : o + HC] = jnp.where(c == 0, high, low).astype(BF16)


def left_kernel(widths, keep, send, got_mine, got_theirs, big, small):
    _, c, _, _ = place()
    _, _, _, a = supers(widths)
    back = (iota((HB, HB), 0) == iota((HB, HB), 1) + a).astype(BF16)
    mine = jnp.concatenate([keep[...], got_mine[...]], axis=0)
    theirs = jnp.concatenate([send[...], got_theirs[...]], axis=0)
    for p in range(2):
        o = p * HC
        big[c, p] = mine[:, o : o + HB].astype(F32).T.astype(BF16)
        big[1 - c, p] = theirs[:, o : o + HB].astype(F32).T.astype(BF16)
        m, t = mine[:, o + HB : o + HC].astype(F32), theirs[:, o + HB : o + HC].astype(F32)
        low, high = jnp.where(c == 0, m, t), jnp.where(c == 0, t, m)
        both = jnp.concatenate([low, high], axis=1)
        small[0, p] = both.T.astype(BF16)
        small[1, p] = jnp.dot(both.astype(BF16), back, preferred_element_type=F32).T.astype(BF16)


def add_blocks(get, a_own, a_sib, us, vs, put, rows):
    _, c, _, _ = place()
    for i, (u, v) in enumerate(zip(us, vs)):
        for part, ref in ((c, u), (1 - c, v)):
            rows[pl.ds(pl.multiple_of((2 * i + part) * ROWS, ROWS), ROWS), :] = ref[...]
    for s, refs in enumerate((a_own, a_sib)):
        left = jnp.concatenate([ref[...] for ref in refs], axis=1)
        z = jnp.dot(left, rows[...], preferred_element_type=F32)
        re, im = z[:ROWS], z[ROWS:]
        old_re, old_im = get(s)
        put(s, old_re + (re[:, :HC] - im[:, HC:]), old_im + (re[:, HC:] + im[:, :HC]))


def acc_kernel(count, has_acc, *refs):
    refs = list(refs[1:])
    old = refs.pop(0) if has_acc else None
    a_own, a_sib, us, vs = (refs[i * count : (i + 1) * count] for i in range(4))
    out, rows = refs[4 * count :]

    def get(s):
        if old is None:
            return 0.0, 0.0
        return old[s, :, :HC], old[s, :, HC:]

    def put(s, re, im):
        out[s, :, :HC] = re
        out[s, :, HC:] = im

    add_blocks(get, a_own, a_sib, us, vs, put, rows)


def column_kernel(_, structure, widths, old, a_own, a_sib, u, v, big, small, own_out, sib_out, q_out, rows, gs, own, sib, q, sems):
    g, c, _, _ = place()
    kb, k1, k2, a = supers(widths)

    def get(s):
        return old[s, :, :HC], old[s, :, HC:]

    def put(s, re, im):
        base = (g + s * (1 - 2 * c)) * 6
        mask_b = row_mask(structure, base, 6, kb, HB)
        mask_1 = row_mask(structure, base, 6, k1, HS)
        mask_2 = row_mask(structure, base, 6, k2, HS)
        mask_s = jnp.where(iota((ROWS, HS), 1) + c * HS < a, mask_1, mask_2)
        out = own if s == 0 else sib
        for p, w in ((0, re), (1, im)):
            vb = -(w[:, :HB] * mask_b)
            vs = -(w[:, HB:] * mask_s)
            out[:, p * HC : p * HC + HB] = vb
            out[:, p * HC + HB : (p + 1) * HC] = vs
            at = slice(s * ROWS, (s + 1) * ROWS)
            for part, lo, hi in ((vb, p * HB, (p + 1) * HB), (vs, 2 * HB + p * HS, 2 * HB + (p + 1) * HS)):
                top = part.astype(BF16)
                gs[0, at, lo:hi] = top
                gs[1, at, lo:hi] = (part - top.astype(F32)).astype(BF16)

    add_blocks(get, [a_own], [a_sib], [u], [v], put, rows)
    copies = [pltpu.make_async_copy(sib, sib_out, sems.at[0]), pltpu.make_async_copy(own, own_out, sems.at[1])]
    for copy in copies:
        copy.start()

    def across(left, lo, hi):
        return jnp.dot(left, gs[0, :, lo:hi], preferred_element_type=F32) + jnp.dot(
            left, gs[1, :, lo:hi], preferred_element_type=F32
        )

    for h in range(2):
        re = across(big[h, 0], 0, 2 * HB)
        im = across(big[h, 1], 0, 2 * HB)
        for t in range(8):
            r = slice(32 * t, 32 * t + 32)
            q[8 * h + t, :, :HB] = re[r, :HB] - im[r, HB:]
            q[8 * h + t, :, HB:BIG] = re[r, HB:] + im[r, :HB]
    col = iota((HB, HS), 1) + c * HS
    row = iota((HB, HS), 0)
    parts = []
    for i in range(2):
        re = across(small[i, 0], 2 * HB, 2 * HB + 2 * HS)
        im = across(small[i, 1], 2 * HB, 2 * HB + 2 * HS)
        parts.append((re[:, :HS] - im[:, HS:], re[:, HS:] + im[:, :HS]))
    for p in range(2):
        e = jnp.where(
            col < a, jnp.where(row < a, parts[0][p], 0.0), jnp.where(row < HB - a, parts[1][p], 0.0)
        )
        at = slice(BIG + p * HS, BIG + (p + 1) * HS)
        for t in range(8):
            q[t, :, at] = e[32 * t : 32 * t + 32]
            q[8 + t, :, at] = jnp.zeros((32, HS), F32)
    copies.append(pltpu.make_async_copy(q, q_out, sems.at[2]))
    copies[2].start()
    for copy in copies:
        copy.wait()


def spread_kernel(widths, weights, mine, other, out, keep, send, wide):
    _, c, _, _ = place()
    odd = parity()
    kb, k1, k2, a = supers(widths)
    wr, wi = weights[0, 0], weights[0, 1]
    back = (iota((HB, HB), 0) == iota((HB, HB), 1) + a).astype(BF16)
    lane = iota((ROWS, HB), 1)
    halves = []
    for ref in (mine, other):
        halves.append([(ref[:, p * HC : p * HC + HB], ref[:, p * HC + HB : (p + 1) * HC]) for p in range(2)])

    def at(k, part):
        return pl.ds(pl.multiple_of(k * BIG + part * HB, HB), HB)

    zero = jnp.zeros((ROWS, HB), BF16)
    small = []
    for p in range(2):
        m, t = halves[0][p], halves[1][p]
        out[p, :, at(kb, c)] = m[0].astype(BF16)
        out[p, :, at(kb, 1 - c)] = t[0].astype(BF16)
        low, high = jnp.where(c == 0, m[1], t[1]), jnp.where(c == 0, t[1], m[1])
        s = jnp.concatenate([low, high], axis=1)
        sb = s.astype(BF16)
        out[p, :, at(k1, 0)] = jnp.where(lane < a, s, 0.0).astype(BF16)
        out[p, :, at(k1, 1)] = zero
        out[p, :, at(k2, 0)] = jnp.dot(sb, back, preferred_element_type=F32).astype(BF16)
        out[p, :, at(k2, 1)] = zero
        small.append(s)
    for i, part in ((0, c), (1, 1 - c)):
        wide[:, at(kb, part)] = wr * halves[i][1][0] + wi * halves[i][0][0]
    d = wr * small[1] + wi * small[0]
    none = jnp.zeros((ROWS, HB), F32)
    wide[:, at(k1, 0)] = jnp.where(lane < a, d, 0.0)
    wide[:, at(k1, 1)] = none
    wide[:, at(k2, 0)] = jnp.where(lane < HB - a, pltpu.roll(d, HB - a, 1), 0.0)
    wide[:, at(k2, 1)] = none
    v = wide[...]
    for j in range(8):
        parts = [
            jnp.concatenate([v[48 * i : 48 * i + 48, 96 * p : 96 * p + 96] for i in range(4)], axis=1)
            for p in (slot(j, 0), slot(j, 1))
        ]
        keep[j] = jnp.where(odd == 0, parts[0], parts[1])
        send[j] = jnp.where(odd == 0, parts[1], parts[0])


def pivot_kernel(widths, weights, pivot, sums, keep, got, block, pay, wide):
    g = lax.axis_index("grid")
    kb, k1, k2, a = supers(widths)
    wr, wi = weights[0, 0], weights[0, 1]
    m, t = sums[0], sums[1]
    for i in range(1, 8):
        m, t = m + sums[2 * i], t + sums[2 * i + 1]
    row = iota((32, BIG), 0) + g * 32
    line = iota((32, BIG), 1)
    blank = jnp.zeros((32, HB), F32)
    q = []
    for p in range(2):
        full = jnp.concatenate([u[:, p * HB : (p + 1) * HB] for u in (m, t)], axis=1)
        e = jnp.concatenate([u[:, BIG + p * HS : BIG + (p + 1) * HS] for u in (m, t)], axis=1)
        moved = pltpu.roll(e, HB - a, 1)
        q.append((full, jnp.concatenate([e, blank], axis=1), jnp.concatenate([moved, blank], axis=1)))
    for i, (k, w) in enumerate(((kb, BIG), (k1, a), (k2, HB - a))):
        live = (row < w) & (line < w)
        blocks = []
        for p in range(2):
            b = jnp.where(live, pivot[p, k] - q[p][i], 0.0)
            block[p, k] = b
            blocks.append(b)
        wide[pl.ds(pl.multiple_of(k * 32, 32), 32), :] = wr * blocks[1] + wi * blocks[0]
    v = wide[...]
    for j in range(8):
        pay[j, :48] = keep[j] + got[j]
        for bit in range(2):
            p = slot(j, bit)
            pay[j, 48 + 8 * bit : 56 + 8 * bit] = jnp.concatenate(
                [v[8 * i : 8 * i + 8, 32 * p : 32 * p + 32] for i in range(12)], axis=1
            )


def density_kernel(pays, column, keep, send):
    odd = parity()
    v = pays[0]
    for i in range(1, 8):
        v = v + pays[i]
    for i in range(4):
        column[48 * i : 48 * i + 48] = v[:48, 96 * i : 96 * i + 96]
    keep[...] = jnp.where(odd == 0, v[48:56], v[56:])
    send[...] = jnp.where(odd == 0, v[56:], v[48:56])


def last_kernel(keep, got, pivot):
    v = keep[...] + got[...]
    for i in range(12):
        pivot[i // 4, 8 * (i % 4) : 8 * (i % 4) + 8] = v[:, 32 * i : 32 * i + 32]


def local(factor_cols, ancestor_inverse, pivot_inverse, structure, widths, pole_weights):
    g, c, x, y = place()
    side = 1 - 2 * c

    def over_grid(v, perm):
        return lax.ppermute(v, "grid", perm)

    block = sds((ROWS, 2 * HC), BF16)
    keep, send = call(
        prep_kernel,
        [block, block],
        [(structure, "s"), (widths, "s"), (factor_cols[0], "v")],
        "prep",
        flops=2 * 2 * ROWS * HB * HB,
    )
    a_own = ancestor_inverse[0].reshape(2 * ROWS, -1)
    a_sib = over_grid(a_own, CORE)
    keep, send, a_sib = lax.optimization_barrier((keep, send, a_sib))
    got_mine, got_theirs = over_grid(send, CORE), over_grid(keep, CORE)
    got_mine, got_theirs = lax.optimization_barrier((got_mine, got_theirs))

    def chip(dx, dy):
        return lax.rem(y + dy, NY) * NX + lax.rem(x + dx + NX, NX)

    def first(v):
        return [over_grid(v, perm) for perm in (FROM_AHEAD, FROM_BEHIND, FROM_Y)]

    def second(ahead, behind, beside):
        return [over_grid(ahead, FROM_AHEAD), over_grid(beside, FROM_BEHIND), over_grid(ahead, FROM_Y)]

    def add(old, places, us, vs):
        n = len(places)
        ins = ([] if old is None else [(old, "v")]) + [(a, (i,)) for a in (a_own, a_sib) for i in range(n)]
        ins += [(b, "v") for b in (*us, *vs)]
        return call(
            functools.partial(acc_kernel, n, old is not None),
            [sds((2, ROWS, 2 * HC), F32)],
            ins,
            "product",
            flops=2 * n * 4 * ROWS * 2 * ROWS * 2 * HC,
            scratch=[pltpu.VMEM((n * 2 * ROWS, 2 * HC), BF16)],
            blocks=places,
        )[0]

    v1 = first(got_mine)
    u1 = first(keep)
    v2 = second(*v1)
    acc = add(None, [chip(0, 0)], [keep], [got_mine])
    big, small = call(
        left_kernel,
        [sds((2, 2, HB, 2 * ROWS), BF16), sds((2, 2, HB, 2 * ROWS), BF16)],
        [(widths, "s"), (keep, "v"), (send, "v"), (got_mine, "v"), (got_theirs, "v")],
        "left",
        flops=2 * 2 * 2 * ROWS * HB * HB,
    )
    *u1, acc, big, small = lax.optimization_barrier((*u1, acc, big, small))
    u2 = second(*u1)
    acc = add(acc, [chip(side, 0), chip(-side, 0), chip(0, 1)], u1, v1)
    v3 = over_grid(v2[2], FROM_AHEAD)
    *u2, acc = lax.optimization_barrier((*u2, acc))
    u3 = over_grid(u2[2], FROM_AHEAD)
    acc = add(acc, [chip(2, 0), chip(-side, 1), chip(side, 1)], u2, v2)
    own, sib, q = call(
        column_kernel,
        [sds((ROWS, 2 * HC), F32)] * 2 + [sds((16, 32, BIG + HB), F32)],
        [
            (structure, "s"),
            (widths, "s"),
            (acc, "v"),
            (a_own, (0,)),
            (a_sib, (0,)),
            (u3, "v"),
            (v3, "v"),
            (big, "v"),
            (small, "v"),
        ],
        "column",
        flops=2 * 4 * ROWS * 2 * ROWS * 2 * HC + 2 * 2 * 1024 * 2 * ROWS * 768,
        scratch=[
            pltpu.VMEM((2 * ROWS, 2 * HC), BF16),
            pltpu.VMEM((2, 2 * ROWS, 2 * HC), BF16),
            pltpu.VMEM((ROWS, 2 * HC), F32),
            pltpu.VMEM((ROWS, 2 * HC), F32),
            pltpu.VMEM((16, 32, BIG + HB), F32),
            pltpu.SemaphoreType.DMA((3,)),
        ],
        blocks=[chip(2, 1)],
        limit=20,
        out_space=pltpu.HBM,
    )
    other = over_grid(sib, CORE)
    sums = lax.all_to_all(q, "grid", 0, 0, tiled=True)
    column_inverse, d_keep, d_send = call(
        spread_kernel,
        [sds((2, ROWS, 3 * BIG), BF16)] + [sds((8, 48, 384), F32)] * 2,
        [(widths, "s"), (pole_weights, "s"), (own, "v"), (other, "v")],
        "spread",
        scratch=[pltpu.VMEM((ROWS, 3 * BIG), F32)],
    )
    d_got = lax.ppermute(d_send, "pole", Z_PAIR)
    sums, d_keep = lax.optimization_barrier((sums, d_keep))
    pivot_block, pay = call(
        pivot_kernel,
        [sds((2, 3, 32, BIG), F32), sds((8, 64, 384), F32)],
        [
            (widths, "s"),
            (pole_weights, "s"),
            (pivot_inverse[0], "v"),
            (sums, "v"),
            (d_keep, "v"),
            (d_got, "v"),
        ],
        "pivot",
        scratch=[pltpu.VMEM((96, BIG), F32)],
    )
    pays = lax.all_to_all(pay, "pole", 0, 0, axis_index_groups=Z_GROUPS, tiled=True)
    density_column, p_keep, p_send = call(
        density_kernel,
        [sds((ROWS, 96), F32)] + [sds((8, 384), F32)] * 2,
        [(pays, "v")],
        "density",
    )
    p_got = lax.ppermute(p_send, "pole", Z_PAIR)
    density_pivot = call(
        last_kernel, [sds((3, 32, 32), F32)], [(p_keep, "v"), (p_got, "v")], "last"
    )[0]
    return (column_inverse[None], pivot_block[None], density_column, density_pivot)


def solution(mesh):
    in_specs = (
        P("pole", None, "grid", None),
        P("pole", None, "grid", None),
        P("pole", None, None, "grid", None),
        P(),
        P(),
        P("pole", None),
    )
    out_specs = (
        P("pole", None, "grid", None),
        P("pole", None, None, "grid", None),
        P("grid", "pole"),
        P(None, "grid", "pole"),
    )
    return jax.shard_map(local, mesh=mesh, in_specs=in_specs, out_specs=out_specs, check_vma=False)
```

time: 138 us -> 120 us (0.87)
  waiting for transfers between devices: 61.5 us -> 24.6 us
  blocking collectives: 0 us -> 32.4 us
  starting transfers between devices: 48.4 us -> 29.3 us
  Pallas kernels: 17 us -> 24.8 us
  other arithmetic: 3.6 us -> 0.15 us
    ppermute x16 -> x18, waiting for transfers between devices: 43.9 us -> 8.87 us  [over_grid(): return lax.ppermute(v, 'grid', perm)]
    all_to_all x0 -> x1, blocking collectives: none -> 32.4 us  [local(): lax.all_to_all(pay, 'pole', 0, 0, axis_index_groups=Z_GROUPS, tiled=True)]
    ppermute x15 -> x2, starting transfers between devices: 33.7 us -> 4.56 us  [the longest x1 2.42 us: local(): p_got = lax.ppermute(p_send, 'pole', Z_PAIR)]
    ppermute x15 -> x2, waiting for transfers between devices: 17.6 us -> 1.67 us  [the longest x1 1.67 us: local(): p_got = lax.ppermute(p_send, 'pole', Z_PAIR)]
    all_to_all x0 -> x1, waiting for transfers between devices: none -> 14 us  [local(): sums = lax.all_to_all(q, 'grid', 0, 0, tiled=True)]
    pallas_call x10, Pallas kernels: 17 us -> 24.8 us  [the longest x4 15.5 us: call(): pl.pallas_call(body, grid_spec=grid_spec, **common)]
    all_to_all x0 -> x1, starting transfers between devices: none -> 5.71 us  [local(): sums = lax.all_to_all(q, 'grid', 0, 0, tiled=True)]
    ppermute x16 -> x18, starting transfers between devices: 14.6 us -> 19.1 us  [over_grid(): return lax.ppermute(v, 'grid', perm)]
  transfers between devices with their start and end apart: 31 -> 21, of which waited for: 18 -> 8; matrix products, arithmetic and copies ran while one was open for 3% -> 1% of each run, Pallas kernels for 8% -> 14%
where the time goes in v2:
time: 120 us; the launch traced here: 118 us
  blocking collectives  32.4 us (27%)
  starting transfers between devices  29.3 us (24%)
  Pallas kernels  24.8 us (21%)
  waiting for transfers between devices  24.6 us (20%)
  local copies, waits for them, and re-layouts  5.94 us (5%)
    all_to_all x1, blocking collectives, local(): lax.all_to_all(pay, 'pole', 0, 0, axis_index_groups=Z_GROUPS, tiled=True)  32.4 us
    ppermute x18, starting transfers between devices, over_grid(): return lax.ppermute(v, 'grid', perm)  19.1 us
    pallas_call x4, Pallas kernels, call(): pl.pallas_call(body, grid_spec=grid_spec, **common)  15.5 us
    all_to_all x1, waiting for transfers between devices, local(): sums = lax.all_to_all(q, 'grid', 0, 0, tiled=True)  14 us
    pallas_call x6, Pallas kernels, call(): pl.pallas_call(body, in_specs=specs, out_specs=out_specs, scratch_shapes=...  9.25 us
    ppermute x18, waiting for transfers between devices, over_grid(): return lax.ppermute(v, 'grid', perm)  8.87 us
    unnamed x33, local copies, waits for them, and re-layouts  5.94 us
    all_to_all x1, starting transfers between devices, local(): sums = lax.all_to_all(q, 'grid', 0, 0, tiled=True)  5.71 us
  transfers between devices with their start and end apart: 21, of which 8 were waited for; matrix products, arithmetic and copies ran while one was open for 1% of the time, Pallas kernels for 14%

profile of v2, /device:TPU:8, one launch (start us, length us, event | category | flops | bytes accessed | tf_op | source)
XLA Modules:
  0.0 118.0 jit_solution(13302963304167943000)
XLA Ops:
  0.7 0.8 copy.11.structure
  1.5 1.3 %copy-done.3 = bf16[1,2,192,1536]{3,2,1,0:T(8,128)(2,1)S(1)} copy-done((bf16[1,2,192,1536]{3,2,1,0:T(8,128)(2,1)S(1)}, bf16[1,2,192,1536]{3,2,1,0:T(8,128)(2,1)}, u32[]{:S(2)}) %copy-start.3) | copy-done | bytes 1179672
  3.5 2.3 %prep.1 = (bf16[192,768]{1,0:T(8,128)(2,1)}, bf16[192,768]{1,0:T(8,128)(2,1)S(1)}) custom-call(s32[96,3]{1,0:T(8,128)S(1)} %copy.11.structure, s32[3]{0:T(128)S(1)} %copy-done.12, bf16[2,192,1536]{2,1,0:T(8,128)(2,1)S(1)} %bitcast.22), custom_call_target="tpu_custom_call" | custom-call | flops 50331648 | bytes 1770636 | tf_op jit(solution)/shard_map/prep/pallas_call | solution.py:102
  6.3 2.8 %collective-permute-start.1 = (bf16[192,768]{1,0:T(8,128)(2,1)}, bf16[192,768]{1,0:T(8,128)(2,1)}, u32[]{:S(2)}, u32[]{:S(2)}) collective-permute-start(bf16[192,768]{1,0:T(8,128)(2,1)} %get-tuple-element.38.refs_3_.keep), channel_id=1, source_target_pairs={{2,0},{7,1},{4,2},{1,3},{6,4},{3,5},{0,6},{5,7},{10,8},{15,9},{12,... | collective-permute-start | bytes 884744 | tf_op jit(solution)/shard_map/ppermute | solution.py:357
  9.1 1.4 %collective-permute-start.3 = (bf16[192,768]{1,0:T(8,128)(2,1)}, bf16[192,768]{1,0:T(8,128)(2,1)}, u32[]{:S(2)}, u32[]{:S(2)}) collective-permute-start(bf16[192,768]{1,0:T(8,128)(2,1)} %get-tuple-element.38.refs_3_.keep), channel_id=1, source_target_pairs={{8,0},{9,1},{10,2},{11,3},{12,4},{13,5},{14,6},{15,7},{0,8},{1,9},... | collective-permute-start | bytes 884744 | tf_op jit(solution)/shard_map/ppermute | solution.py:357
  10.5 2.2 %collective-permute-start.9 = (bf16[192,768]{1,0:T(8,128)(2,1)}, bf16[192,768]{1,0:T(8,128)(2,1)}, u32[]{:S(2)}, u32[]{:S(2)}) collective-permute-start(bf16[192,768]{1,0:T(8,128)(2,1)} %collective-permute-done.4.refs_4_.got_mine), channel_id=1, source_target_pairs={{2,0},{7,1},{4,2},{1,3},{6,4},{3,5},{0,6},{5,7},{10,8},{15,9},{12,... | collective-permute-start | bytes 884744 | tf_op jit(solution)/shard_map/ppermute | solution.py:357
  12.7 1.6 %collective-permute-start.11 = (bf16[192,768]{1,0:T(8,128)(2,1)}, bf16[192,768]{1,0:T(8,128)(2,1)}, u32[]{:S(2)}, u32[]{:S(2)}) collective-permute-start(bf16[192,768]{1,0:T(8,128)(2,1)} %collective-permute-done.4.refs_4_.got_mine), channel_id=1, source_target_pairs={{8,0},{9,1},{10,2},{11,3},{12,4},{13,5},{14,6},{15,7},{0,8},{1,9},... | collective-permute-start | bytes 884744 | tf_op jit(solution)/shard_map/ppermute | solution.py:357
  14.3 1.6 %left.1 = (bf16[2,2,256,384]{3,2,1,0:T(8,128)(2,1)S(1)}, bf16[2,2,256,384]{3,2,1,0:T(8,128)(2,1)S(1)}) custom-call(s32[3]{0:T(128)S(1)} %copy-done.13, bf16[192,768]{1,0:T(8,128)(2,1)} %get-tuple-element.38.refs_3_.keep, bf16[192,768]{1,0:T(8,128)(2,1)S(1)} %get-tuple-element.40.send, bf16[192,768]{1,0:T(8,128)(2,1)} %collective-permute-done.4.refs_4_.got_mine, ...), custom_call_target="tpu_custom_call" | custom-call | flops 100663296 | bytes 2752524 | tf_op jit(solution)/shard_map/left/pallas_call | solution.py:102
  15.9 0.9 copy-done.6
  16.8 2.2 %product.3.refs_1_ = f32[2,192,768]{2,1,0:T(8,128)S(1)} custom-call(s32[1]{0:T(128)} %bitcast.6.refs_0_, bf16[384,3072]{1,0:T(8,128)(2,1)S(1)} %bitcast.14, bf16[384,3072]{1,0:T(8,128)(2,1)} %collective-permute-done.refs_2_.refs_5_.refs_6_.refs_7_.a_sib, bf16[192,768]{1,0:T(8,128)(2,1)} %get-tuple-element.38.refs_3_.keep, ...), custom_call_target="tpu_custom_call" | custom-call | flops 452984832 | bytes 1769472 | tf_op jit(solution)/shard_map/product/pallas_call | solution.py:112
  19.2 3.3 %collective-permute-start.6 = (bf16[192,768]{1,0:T(8,128)(2,1)}, bf16[192,768]{1,0:T(8,128)(2,1)}, u32[]{:S(2)}, u32[]{:S(2)}) collective-permute-start(bf16[192,768]{1,0:T(8,128)(2,1)} %collective-permute-done.1.refs_8_), channel_id=1, source_target_pairs={{2,0},{7,1},{4,2},{1,3},{6,4},{3,5},{0,6},{5,7},{10,8},{15,9},{12,... | collective-permute-start | bytes 884744 | tf_op jit(solution)/shard_map/ppermute | solution.py:357
  23.0 2.6 %collective-permute-done.11.refs_13_ = bf16[192,768]{1,0:T(8,128)(2,1)} collective-permute-done((bf16[192,768]{1,0:T(8,128)(2,1)}, bf16[192,768]{1,0:T(8,128)(2,1)}, u32[]{:S(2)}, u32[]{:S(2)}) %collective-permute-start.11) | collective-permute-done | bytes 294944 | tf_op jit(solution)/shard_map/ppermute | solution.py:357
  25.6 1.3 %collective-permute-start.14 = (bf16[192,768]{1,0:T(8,128)(2,1)}, bf16[192,768]{1,0:T(8,128)(2,1)}, u32[]{:S(2)}, u32[]{:S(2)}) collective-permute-start(bf16[192,768]{1,0:T(8,128)(2,1)} %collective-permute-done.9.refs_11_), channel_id=1, source_target_pairs={{8,0},{9,1},{10,2},{11,3},{12,4},{13,5},{14,6},{15,7},{0,8},{1,9},... | collective-permute-start | bytes 884744 | tf_op jit(solution)/shard_map/ppermute | solution.py:357
  26.9 2.7 %collective-permute-done.10.refs_12_ = bf16[192,768]{1,0:T(8,128)(2,1)} collective-permute-done((bf16[192,768]{1,0:T(8,128)(2,1)}, bf16[192,768]{1,0:T(8,128)(2,1)}, u32[]{:S(2)}, u32[]{:S(2)}) %collective-permute-start.10) | collective-permute-done | bytes 294944 | tf_op jit(solution)/shard_map/ppermute | solution.py:357
  29.6 2.0 %collective-permute-start.13 = (bf16[192,768]{1,0:T(8,128)(2,1)}, bf16[192,768]{1,0:T(8,128)(2,1)}, u32[]{:S(2)}, u32[]{:S(2)}) collective-permute-start(bf16[192,768]{1,0:T(8,128)(2,1)} %collective-permute-done.11.refs_13_), channel_id=1, source_target_pairs={{6,0},{3,1},{0,2},{5,3},{2,4},{7,5},{4,6},{1,7},{14,8},{11,9},{8,1... | collective-permute-start | bytes 884744 | tf_op jit(solution)/shard_map/ppermute | solution.py:357
  31.7 4.0 %product.4.refs_1_ = f32[2,192,768]{2,1,0:T(8,128)S(1)} custom-call(s32[3]{0:T(128)S(1)} %pad_add_fusion.1.refs_0_, f32[2,192,768]{2,1,0:T(8,128)S(1)} %product.3.refs_1_, bf16[384,3072]{1,0:T(8,128)(2,1)S(1)} %bitcast.15, bf16[384,3072]{1,0:T(8,128)(2,1)S(1)} %bitcast.16, bf16[384,3072]{1,0:T(8,128)(2,1)S(1)} %bitcast.17, ...), custom_call_target="tpu_custom_call" | custom-call | flops 1358954496 | bytes 4128768 | tf_op jit(solution)/shard_map/product/pallas_call | solution.py:112
  35.7 1.0 copy-done.1
  36.7 1.2 %collective-permute-start.15 = (bf16[192,768]{1,0:T(8,128)(2,1)}, bf16[192,768]{1,0:T(8,128)(2,1)S(1)}, u32[]{:S(2)}, u32[]{:S(2)}) collective-permute-start(bf16[192,768]{1,0:T(8,128)(2,1)} %collective-permute-done.8.refs_10_), channel_id=1, source_target_pairs={{2,0},{7,1},{4,2},{1,3},{6,4},{3,5},{0,6},{5,7},{10,8},{15,9},{12,... | collective-permute-start | bytes 884744 | tf_op jit(solution)/shard_map/ppermute | solution.py:357
  38.1 1.8 %collective-permute-start.16 = (bf16[192,768]{1,0:T(8,128)(2,1)}, bf16[192,768]{1,0:T(8,128)(2,1)S(1)}, u32[]{:S(2)}, u32[]{:S(2)}) collective-permute-start(bf16[192,768]{1,0:T(8,128)(2,1)} %collective-permute-done.14.refs_13_), channel_id=1, source_target_pairs={{2,0},{7,1},{4,2},{1,3},{6,4},{3,5},{0,6},{5,7},{10,8},{15,9},{12,... | collective-permute-start | bytes 884744 | tf_op jit(solution)/shard_map/ppermute | solution.py:357
  40.0 1.3 %copy-done.2 = f32[2,192,768]{2,1,0:T(8,128)S(1)} copy-done((f32[2,192,768]{2,1,0:T(8,128)S(1)}, f32[2,192,768]{2,1,0:T(8,128)}, u32[]{:S(2)}) %copy-start.2) | copy-done | bytes 1179672
  41.3 4.0 %product.5.old = f32[2,192,768]{2,1,0:T(8,128)S(1)} custom-call(s32[3]{0:T(128)S(1)} %pad_add_fusion.refs_0_, f32[2,192,768]{2,1,0:T(8,128)S(1)} %copy-done.2, bf16[384,3072]{1,0:T(8,128)(2,1)S(1)} %bitcast.18, bf16[384,3072]{1,0:T(8,128)(2,1)S(1)} %bitcast.19, bf16[384,3072]{1,0:T(8,128)(2,1)S(1)} %bitcast.20, ...), custom_call_target="tpu_custom_call" | custom-call | flops 1358954496 | bytes 4128768 | tf_op jit(solution)/shard_map/product/pallas_call | solution.py:112
  45.3 1.5 %collective-permute-done.16.v = bf16[192,768]{1,0:T(8,128)(2,1)S(1)} collective-permute-done((bf16[192,768]{1,0:T(8,128)(2,1)}, bf16[192,768]{1,0:T(8,128)(2,1)S(1)}, u32[]{:S(2)}, u32[]{:S(2)}) %collective-permute-start.16) | collective-permute-done | bytes 294944 | tf_op jit(solution)/shard_map/ppermute | solution.py:357
  46.8 5.3 %column.1 = (f32[192,768]{1,0:T(8,128)}, f32[192,768]{1,0:T(8,128)}, f32[16,32,768]{2,1,0:T(8,128)}) custom-call(s32[1]{0:T(128)} %bitcast._, s32[96,3]{1,0:T(8,128)S(1)} %copy-done.10, s32[3]{0:T(128)S(1)} %copy-done.13, f32[2,192,768]{2,1,0:T(8,128)S(1)} %product.5.old, bf16[384,3072]{1,0:T(8,128)(2,1)S(1)} %bitcast.21, ...), custom_call_target="tpu_custom_call" | custom-call | flops 1660944384 | bytes 6096012 | tf_op jit(solution)/shard_map/column/pallas_call | solution.py:112
  52.1 5.7 %all-to-all-start = ((f32[16,32,768]{2,1,0:T(8,128)}), f32[16,32,768]{2,1,0:T(8,128)S(1)}, u32[]{:S(2)}, u32[]{:S(2)}) async-start(f32[16,32,768]{2,1,0:T(8,128)} %get-tuple-element.58), calls=%async_computation | async-start | bytes 3145728 | tf_op jit(solution)/shard_map/all_to_all | solution.py:443
  58.1 1.9 %collective-permute-done.17.other = f32[192,768]{1,0:T(8,128)S(1)} collective-permute-done((f32[192,768]{1,0:T(8,128)S(1)}, f32[192,768]{1,0:T(8,128)S(1)}, u32[]{:S(2)}, u32[]{:S(2)}) %collective-permute-start.17) | collective-permute-done | bytes 589856 | tf_op jit(solution)/shard_map/ppermute | solution.py:357
  60.0 2.5 %spread.1 = (bf16[2,192,1536]{2,1,0:T(8,128)(2,1)}, f32[8,48,384]{2,1,0:T(8,128)S(1)}, f32[8,48,384]{2,1,0:T(8,128)}) custom-call(s32[3]{0:T(128)S(1)} %copy-done.13, f32[1,2]{1,0:T(1,128)S(1)} %copy-done.14, f32[192,768]{1,0:T(8,128)S(1)} %copy-done.8, f32[192,768]{1,0:T(8,128)S(1)} %collective-permute-done.17.other), custom_call_target="tpu_custom_call" | custom-call | bytes 3538964 | tf_op jit(solution)/shard_map/spread/pallas_call | solution.py:102
  62.4 2.1 %collective-permute-start.18 = (f32[8,48,384]{2,1,0:T(8,128)}, f32[8,48,384]{2,1,0:T(8,128)S(1)}, u32[]{:S(2)}, u32[]{:S(2)}) collective-permute-start(f32[8,48,384]{2,1,0:T(8,128)} %get-tuple-element.62), channel_id=1, source_target_pairs={{32,0},{48,16},{0,32},{16,48},{96,64},{112,80},{64,96},{80,112},{1... | collective-permute-start | bytes 1769480 | tf_op jit(solution)/shard_map/ppermute | solution.py:451
  64.6 14.0 %all-to-all-done.sums = f32[16,32,768]{2,1,0:T(8,128)S(1)} async-done(((f32[16,32,768]{2,1,0:T(8,128)}), f32[16,32,768]{2,1,0:T(8,128)S(1)}, u32[]{:S(2)}, u32[]{:S(2)}) %all-to-all-start) | async-done | bytes 1572896 | tf_op jit(solution)/shard_map/all_to_all | solution.py:443
  78.6 1.5 %pivot.1 = (f32[2,3,32,512]{3,2,1,0:T(8,128)}, f32[8,64,384]{2,1,0:T(8,128)S(1)}) custom-call(s32[3]{0:T(128)S(1)} %copy-done.13, f32[1,2]{1,0:T(1,128)S(1)} %copy-done.14, f32[2,3,32,512]{3,2,1,0:T(8,128)S(1)} %bitcast.23, f32[16,32,768]{2,1,0:T(8,128)S(1)} %all-to-all-done.sums, f32[8,48,384]{2,1,0:T(8,128)S(1)} %get-tuple-element.61.keep, ...), custom_call_target="tpu_custom_call" | custom-call | bytes 4325396 | tf_op jit(solution)/shard_map/pivot/pallas_call | solution.py:102
  80.0 32.4 %all_to_all.10.pays = f32[8,64,384]{2,1,0:T(8,128)S(1)} all-to-all(f32[8,64,384]{2,1,0:T(8,128)S(1)} %get-tuple-element.64), channel_id=1, replica_groups={{0,16,64,80,128,144,192,208},{32,48,96,112,160,176,224,240},{1,17,65,81..., dimensions={0} | all-to-all | bytes 1572864 | tf_op jit(solution)/shard_map/all_to_all | solution.py:467
  113.2 2.4 %collective-permute-start.19 = (f32[8,384]{1,0:T(8,128)S(1)}, f32[8,384]{1,0:T(8,128)S(1)}, u32[]{:S(2)}, u32[]{:S(2)}) collective-permute-start(f32[8,384]{1,0:T(8,128)S(1)} %get-tuple-element.67), channel_id=1, source_target_pairs={{32,0},{48,16},{0,32},{16,48},{96,64},{112,80},{64,96},{80,112},{1... | collective-permute-start | bytes 36872 | tf_op jit(solution)/shard_map/ppermute | solution.py:474
  115.7 1.7 %collective-permute-done.19.got = f32[8,384]{1,0:T(8,128)S(1)} collective-permute-done((f32[8,384]{1,0:T(8,128)S(1)}, f32[8,384]{1,0:T(8,128)S(1)}, u32[]{:S(2)}, u32[]{:S(2)}) %collective-permute-start.19) | collective-permute-done | bytes 12320 | tf_op jit(solution)/shard_map/ppermute | solution.py:474
  (56 shorter events, 4.0 us)
Async XLA Ops:
  0.6 13.7 %copy-start.13 = (s32[3]{0:T(128)S(1)}, s32[3]{0:T(128)}, u32[]{:S(2)}) copy-start(s32[3]{0:T(128)} %widths.9) | copy-start | bytes 40
  0.6 5.1 %collective-permute-start = (bf16[384,3072]{1,0:T(8,128)(2,1)}, bf16[384,3072]{1,0:T(8,128)(2,1)}, u32[]{:S(2)}, u32[]{:S(2)}) collective-permute-start(bf16[384,3072]{1,0:T(8,128)(2,1)} %bitcast.13), channel_id=1, source_target_pairs={{1,0},{0,1},{3,2},{2,3},{5,4},{4,5},{7,6},{6,7},{9,8},{8,9},{11,10... | collective-permute-start | bytes 7077896 | tf_op jit(solution)/shard_map/ppermute | solution.py:357
  1.5 14.4 %copy-start.9 = (s32[96,3]{1,0:T(8,128)}, s32[96,3]{1,0:T(8,128)S(1)}, u32[]{:S(2)}) copy-start(s32[96,3]{1,0:T(8,128)S(1)} %copy.11.structure) | copy-start | bytes 3460
  3.5 13.3 %copy-start = (bf16[1,2,192,3072]{3,2,1,0:T(8,128)(2,1)S(1)}, bf16[1,2,192,3072]{3,2,1,0:T(8,128)(2,1)}, u32[]{:S(2)}) copy-start(bf16[1,2,192,3072]{3,2,1,0:T(8,128)(2,1)} %param.7) | copy-start | bytes 7077892
  5.8 4.7 %collective-permute-start.5 = (bf16[192,768]{1,0:T(8,128)(2,1)}, bf16[192,768]{1,0:T(8,128)(2,1)S(1)}, u32[]{:S(2)}, u32[]{:S(2)}) collective-permute-start(bf16[192,768]{1,0:T(8,128)(2,1)} %get-tuple-element.38.refs_3_.keep), channel_id=1, source_target_pairs={{1,0},{0,1},{3,2},{2,3},{5,4},{4,5},{7,6},{6,7},{9,8},{8,9},{11,10... | collective-permute-start | bytes 884744 | tf_op jit(solution)/shard_map/ppermute | solution.py:357
  6.3 4.2 %collective-permute-start.4 = (bf16[192,768]{1,0:T(8,128)(2,1)S(1)}, bf16[192,768]{1,0:T(8,128)(2,1)}, u32[]{:S(2)}, u32[]{:S(2)}) collective-permute-start(bf16[192,768]{1,0:T(8,128)(2,1)S(1)} %get-tuple-element.40.send), channel_id=1, source_target_pairs={{1,0},{0,1},{3,2},{2,3},{5,4},{4,5},{7,6},{6,7},{9,8},{8,9},{11,10... | collective-permute-start | bytes 884744 | tf_op jit(solution)/shard_map/ppermute | solution.py:357
  6.3 12.8 %collective-permute-start.1 = (bf16[192,768]{1,0:T(8,128)(2,1)}, bf16[192,768]{1,0:T(8,128)(2,1)}, u32[]{:S(2)}, u32[]{:S(2)}) collective-permute-start(bf16[192,768]{1,0:T(8,128)(2,1)} %get-tuple-element.38.refs_3_.keep), channel_id=1, source_target_pairs={{2,0},{7,1},{4,2},{1,3},{6,4},{3,5},{0,6},{5,7},{10,8},{15,9},{12,... | collective-permute-start | bytes 884744 | tf_op jit(solution)/shard_map/ppermute | solution.py:357
  9.1 10.1 %collective-permute-start.2 = (bf16[192,768]{1,0:T(8,128)(2,1)}, bf16[192,768]{1,0:T(8,128)(2,1)}, u32[]{:S(2)}, u32[]{:S(2)}) collective-permute-start(bf16[192,768]{1,0:T(8,128)(2,1)} %get-tuple-element.38.refs_3_.keep), channel_id=1, source_target_pairs={{6,0},{3,1},{0,2},{5,3},{2,4},{7,5},{4,6},{1,7},{14,8},{11,9},{8,1... | collective-permute-start | bytes 884744 | tf_op jit(solution)/shard_map/ppermute | solution.py:357
  9.1 10.2 %collective-permute-start.3 = (bf16[192,768]{1,0:T(8,128)(2,1)}, bf16[192,768]{1,0:T(8,128)(2,1)}, u32[]{:S(2)}, u32[]{:S(2)}) collective-permute-start(bf16[192,768]{1,0:T(8,128)(2,1)} %get-tuple-element.38.refs_3_.keep), channel_id=1, source_target_pairs={{8,0},{9,1},{10,2},{11,3},{12,4},{13,5},{14,6},{15,7},{0,8},{1,9},... | collective-permute-start | bytes 884744 | tf_op jit(solution)/shard_map/ppermute | solution.py:357
  10.5 12.0 %collective-permute-start.9 = (bf16[192,768]{1,0:T(8,128)(2,1)}, bf16[192,768]{1,0:T(8,128)(2,1)}, u32[]{:S(2)}, u32[]{:S(2)}) collective-permute-start(bf16[192,768]{1,0:T(8,128)(2,1)} %collective-permute-done.4.refs_4_.got_mine), channel_id=1, source_target_pairs={{2,0},{7,1},{4,2},{1,3},{6,4},{3,5},{0,6},{5,7},{10,8},{15,9},{12,... | collective-permute-start | bytes 884744 | tf_op jit(solution)/shard_map/ppermute | solution.py:357
  12.7 12.8 %collective-permute-start.11 = (bf16[192,768]{1,0:T(8,128)(2,1)}, bf16[192,768]{1,0:T(8,128)(2,1)}, u32[]{:S(2)}, u32[]{:S(2)}) collective-permute-start(bf16[192,768]{1,0:T(8,128)(2,1)} %collective-permute-done.4.refs_4_.got_mine), channel_id=1, source_target_pairs={{8,0},{9,1},{10,2},{11,3},{12,4},{13,5},{14,6},{15,7},{0,8},{1,9},... | collective-permute-start | bytes 884744 | tf_op jit(solution)/shard_map/ppermute | solution.py:357
  16.8 2.3 %copy-start.4 = (bf16[2,2,256,384]{3,2,1,0:T(8,128)(2,1)}, bf16[2,2,256,384]{3,2,1,0:T(8,128)(2,1)S(1)}, u32[]{:S(2)}) copy-start(bf16[2,2,256,384]{3,2,1,0:T(8,128)(2,1)S(1)} %get-tuple-element.53.big) | copy-start | bytes 2359300
  19.1 10.5 %collective-permute-start.10 = (bf16[192,768]{1,0:T(8,128)(2,1)}, bf16[192,768]{1,0:T(8,128)(2,1)}, u32[]{:S(2)}, u32[]{:S(2)}) collective-permute-start(bf16[192,768]{1,0:T(8,128)(2,1)} %collective-permute-done.4.refs_4_.got_mine), channel_id=1, source_target_pairs={{6,0},{3,1},{0,2},{5,3},{2,4},{7,5},{4,6},{1,7},{14,8},{11,9},{8,1... | collective-permute-start | bytes 884744 | tf_op jit(solution)/shard_map/ppermute | solution.py:357
  19.2 10.4 %collective-permute-start.6 = (bf16[192,768]{1,0:T(8,128)(2,1)}, bf16[192,768]{1,0:T(8,128)(2,1)}, u32[]{:S(2)}, u32[]{:S(2)}) collective-permute-start(bf16[192,768]{1,0:T(8,128)(2,1)} %collective-permute-done.1.refs_8_), channel_id=1, source_target_pairs={{2,0},{7,1},{4,2},{1,3},{6,4},{3,5},{0,6},{5,7},{10,8},{15,9},{12,... | collective-permute-start | bytes 884744 | tf_op jit(solution)/shard_map/ppermute | solution.py:357
  22.6 14.1 %collective-permute-start.7 = (bf16[192,768]{1,0:T(8,128)(2,1)}, bf16[192,768]{1,0:T(8,128)(2,1)}, u32[]{:S(2)}, u32[]{:S(2)}) collective-permute-start(bf16[192,768]{1,0:T(8,128)(2,1)} %collective-permute-done.3.refs_10_), channel_id=1, source_target_pairs={{6,0},{3,1},{0,2},{5,3},{2,4},{7,5},{4,6},{1,7},{14,8},{11,9},{8,1... | collective-permute-start | bytes 884744 | tf_op jit(solution)/shard_map/ppermute | solution.py:357
  22.6 14.1 %collective-permute-start.8 = (bf16[192,768]{1,0:T(8,128)(2,1)}, bf16[192,768]{1,0:T(8,128)(2,1)}, u32[]{:S(2)}, u32[]{:S(2)}) collective-permute-start(bf16[192,768]{1,0:T(8,128)(2,1)} %collective-permute-done.1.refs_8_), channel_id=1, source_target_pairs={{8,0},{9,1},{10,2},{11,3},{12,4},{13,5},{14,6},{15,7},{0,8},{1,9},... | collective-permute-start | bytes 884744 | tf_op jit(solution)/shard_map/ppermute | solution.py:357
  25.6 12.6 %collective-permute-start.14 = (bf16[192,768]{1,0:T(8,128)(2,1)}, bf16[192,768]{1,0:T(8,128)(2,1)}, u32[]{:S(2)}, u32[]{:S(2)}) collective-permute-start(bf16[192,768]{1,0:T(8,128)(2,1)} %collective-permute-done.9.refs_11_), channel_id=1, source_target_pairs={{8,0},{9,1},{10,2},{11,3},{12,4},{13,5},{14,6},{15,7},{0,8},{1,9},... | collective-permute-start | bytes 884744 | tf_op jit(solution)/shard_map/ppermute | solution.py:357
  29.6 10.4 %collective-permute-start.12 = (bf16[192,768]{1,0:T(8,128)(2,1)}, bf16[192,768]{1,0:T(8,128)(2,1)}, u32[]{:S(2)}, u32[]{:S(2)}) collective-permute-start(bf16[192,768]{1,0:T(8,128)(2,1)} %collective-permute-done.9.refs_11_), channel_id=1, source_target_pairs={{2,0},{7,1},{4,2},{1,3},{6,4},{3,5},{0,6},{5,7},{10,8},{15,9},{12,... | collective-permute-start | bytes 884744 | tf_op jit(solution)/shard_map/ppermute | solution.py:357
  29.6 10.4 %collective-permute-start.13 = (bf16[192,768]{1,0:T(8,128)(2,1)}, bf16[192,768]{1,0:T(8,128)(2,1)}, u32[]{:S(2)}, u32[]{:S(2)}) collective-permute-start(bf16[192,768]{1,0:T(8,128)(2,1)} %collective-permute-done.11.refs_13_), channel_id=1, source_target_pairs={{6,0},{3,1},{0,2},{5,3},{2,4},{7,5},{4,6},{1,7},{14,8},{11,9},{8,1... | collective-permute-start | bytes 884744 | tf_op jit(solution)/shard_map/ppermute | solution.py:357
  36.7 8.6 %collective-permute-start.15 = (bf16[192,768]{1,0:T(8,128)(2,1)}, bf16[192,768]{1,0:T(8,128)(2,1)S(1)}, u32[]{:S(2)}, u32[]{:S(2)}) collective-permute-start(bf16[192,768]{1,0:T(8,128)(2,1)} %collective-permute-done.8.refs_10_), channel_id=1, source_target_pairs={{2,0},{7,1},{4,2},{1,3},{6,4},{3,5},{0,6},{5,7},{10,8},{15,9},{12,... | collective-permute-start | bytes 884744 | tf_op jit(solution)/shard_map/ppermute | solution.py:357
  38.1 8.7 %collective-permute-start.16 = (bf16[192,768]{1,0:T(8,128)(2,1)}, bf16[192,768]{1,0:T(8,128)(2,1)S(1)}, u32[]{:S(2)}, u32[]{:S(2)}) collective-permute-start(bf16[192,768]{1,0:T(8,128)(2,1)} %collective-permute-done.14.refs_13_), channel_id=1, source_target_pairs={{2,0},{7,1},{4,2},{1,3},{6,4},{3,5},{0,6},{5,7},{10,8},{15,9},{12,... | collective-permute-start | bytes 884744 | tf_op jit(solution)/shard_map/ppermute | solution.py:357
  41.3 5.5 %copy-start.5 = (bf16[2,2,256,384]{3,2,1,0:T(8,128)(2,1)S(1)}, bf16[2,2,256,384]{3,2,1,0:T(8,128)(2,1)}, u32[]{:S(2)}) copy-start(bf16[2,2,256,384]{3,2,1,0:T(8,128)(2,1)} %copy-done.4) | copy-start | bytes 2359300
  41.3 5.5 %copy-start.7 = (bf16[2,2,256,384]{3,2,1,0:T(8,128)(2,1)S(1)}, bf16[2,2,256,384]{3,2,1,0:T(8,128)(2,1)}, u32[]{:S(2)}) copy-start(bf16[2,2,256,384]{3,2,1,0:T(8,128)(2,1)} %copy-done.6) | copy-start | bytes 2359300
  41.3 5.5 %copy-start.10 = (s32[96,3]{1,0:T(8,128)S(1)}, s32[96,3]{1,0:T(8,128)}, u32[]{:S(2)}) copy-start(s32[96,3]{1,0:T(8,128)} %copy-done.9) | copy-start | bytes 3460
  52.1 5.8 %copy-start.15 = (f32[192,768]{1,0:T(8,128)S(1)}, f32[192,768]{1,0:T(8,128)}, u32[]{:S(2)}) copy-start(f32[192,768]{1,0:T(8,128)} %get-tuple-element.56) | copy-start | bytes 1769476
  52.1 7.8 %copy-start.8 = (f32[192,768]{1,0:T(8,128)S(1)}, f32[192,768]{1,0:T(8,128)}, u32[]{:S(2)}) copy-start(f32[192,768]{1,0:T(8,128)} %get-tuple-element.55.mine) | copy-start | bytes 1769476
  52.1 7.8 %copy-start.14 = (f32[1,2]{1,0:T(1,128)S(1)}, f32[1,2]{1,0:T(1,128)}, u32[]{:S(2)}) copy-start(f32[1,2]{1,0:T(1,128)} %weights.3) | copy-start | bytes 28
  52.1 26.4 %all-to-all-start = ((f32[16,32,768]{2,1,0:T(8,128)}), f32[16,32,768]{2,1,0:T(8,128)S(1)}, u32[]{:S(2)}, u32[]{:S(2)}) async-start(f32[16,32,768]{2,1,0:T(8,128)} %get-tuple-element.58), calls=%async_computation | async-start | bytes 3145728 | tf_op jit(solution)/shard_map/all_to_all | solution.py:443
  57.9 20.7 %copy-start.11 = (f32[1,2,3,32,512]{4,3,2,1,0:T(8,128)S(1)}, f32[1,2,3,32,512]{4,3,2,1,0:T(8,128)}, u32[]{:S(2)}) copy-start(f32[1,2,3,32,512]{4,3,2,1,0:T(8,128)} %param.8) | copy-start | bytes 1179652
  57.9 2.1 %collective-permute-start.17 = (f32[192,768]{1,0:T(8,128)S(1)}, f32[192,768]{1,0:T(8,128)S(1)}, u32[]{:S(2)}, u32[]{:S(2)}) collective-permute-start(f32[192,768]{1,0:T(8,128)S(1)} %copy-done.15), channel_id=1, source_target_pairs={{1,0},{0,1},{3,2},{2,3},{5,4},{4,5},{7,6},{6,7},{9,8},{8,9},{11,10... | collective-permute-start | bytes 1769480 | tf_op jit(solution)/shard_map/ppermute | solution.py:357
  62.4 16.1 %collective-permute-start.18 = (f32[8,48,384]{2,1,0:T(8,128)}, f32[8,48,384]{2,1,0:T(8,128)S(1)}, u32[]{:S(2)}, u32[]{:S(2)}) collective-permute-start(f32[8,48,384]{2,1,0:T(8,128)} %get-tuple-element.62), channel_id=1, source_target_pairs={{32,0},{48,16},{0,32},{16,48},{96,64},{112,80},{64,96},{80,112},{1... | collective-permute-start | bytes 1769480 | tf_op jit(solution)/shard_map/ppermute | solution.py:451
  113.2 4.1 %collective-permute-start.19 = (f32[8,384]{1,0:T(8,128)S(1)}, f32[8,384]{1,0:T(8,128)S(1)}, u32[]{:S(2)}, u32[]{:S(2)}) collective-permute-start(f32[8,384]{1,0:T(8,128)S(1)} %get-tuple-element.67), channel_id=1, source_target_pairs={{32,0},{48,16},{0,32},{16,48},{96,64},{112,80},{64,96},{80,112},{1... | collective-permute-start | bytes 36872 | tf_op jit(solution)/shard_map/ppermute | solution.py:474
  (5 other events, 5.1 us)

commit v3 on v2

v3 whole, which is shorter than its diff:
```python
import functools

import jax
import jax.numpy as jnp
from jax import lax
from jax.experimental import pallas as pl
from jax.experimental.pallas import tpu as pltpu
from jax.sharding import PartitionSpec as P

F32 = jnp.float32
BF16 = jnp.bfloat16
BIG = 512
ROWS = 192
HB = 256
HS = 128
HC = HB + HS

NX, NY, NCORE = 4, 2, 2
NZ, NH = 8, 2


def grid_perm(source):
    def at(y, x, c):
        return (y * NX + x % NX) * NCORE + c

    return [
        (at(*source(y, x, c)), at(y, x, c)) for y in range(NY) for x in range(NX) for c in range(NCORE)
    ]


CORE = grid_perm(lambda y, x, c: (y, x, 1 - c))
FROM_AHEAD = grid_perm(lambda y, x, c: (y, x + 1 - 2 * c, c))
FROM_BEHIND = grid_perm(lambda y, x, c: (y, x - 1 + 2 * c, c))
FROM_Y = grid_perm(lambda y, x, c: (1 - y, x, c))


def pole_perm(source):
    def at(z, h):
        return z * NH + h

    return [(at(*source(z, h)), at(z, h)) for z in range(NZ) for h in range(NH)]


def z_pair(bit):
    return pole_perm(lambda z, h: (z ^ bit, h))


def place():
    g = lax.axis_index("grid")
    c = lax.rem(g, 2)
    x = lax.rem(lax.div(g, 2), NX)
    y = lax.div(g, 2 * NX)
    return g, c, x, y


def z_bits():
    z = lax.div(lax.axis_index("pole"), NH)
    return lax.rem(z, 2), lax.rem(lax.div(z, 2), 2)


def supers(widths):
    kb = jnp.where(widths[0] == BIG, 0, jnp.where(widths[1] == BIG, 1, 2))
    k1 = jnp.where(kb == 0, 1, 0)
    k2 = jnp.where(kb == 2, 1, 2)
    return kb, k1, k2, widths[k1]


def iota(shape, axis):
    return lax.broadcasted_iota(jnp.int32, shape, axis)


def row_mask(structure, block, count, k, lanes):
    return jnp.concatenate(
        [jnp.full((32, lanes), structure[k, block + i].astype(F32), F32) for i in range(count)], axis=0
    )


def call(body, outs, ins, name, flops=0, scratch=(), limit=16, out_space=pltpu.VMEM):
    spaces = {"s": pltpu.SMEM, "v": pltpu.VMEM, "h": pltpu.HBM}
    size = sum(a.size * a.dtype.itemsize for a, _ in ins) + sum(
        o.size * o.dtype.itemsize for o in outs
    )
    if out_space is pltpu.HBM:
        outs = [pltpu.HBM(o.shape, o.dtype) for o in outs]
    return pl.pallas_call(
        body,
        out_shape=tuple(outs),
        in_specs=[pl.BlockSpec(memory_space=spaces[kind]) for _, kind in ins],
        out_specs=tuple(pl.BlockSpec(memory_space=out_space) for _ in outs),
        scratch_shapes=list(scratch),
        compiler_params=pltpu.CompilerParams(vmem_limit_bytes=limit * 1024 * 1024),
        cost_estimate=pl.CostEstimate(flops=flops, bytes_accessed=size, transcendentals=0),
        name=name,
    )(*[a for a, _ in ins])


def sds(shape, dtype):
    return jax.ShapeDtypeStruct(shape, dtype)


def prep_kernel(structure, widths, f, keep, send):
    g, c, _, _ = place()
    kb, k1, k2, a = supers(widths)
    base = g * 6
    mask_b = row_mask(structure, base, 6, kb, HB).astype(BF16)
    mask_1 = row_mask(structure, base, 6, k1, HB).astype(BF16)
    mask_2 = row_mask(structure, base, 6, k2, HB).astype(BF16)
    shift = (iota((HB, HB), 0) + a == iota((HB, HB), 1)).astype(BF16)
    first = iota((ROWS, HB), 1) < a

    def at(k, part):
        return pl.ds(pl.multiple_of(k * BIG + part * HB, HB), HB)

    for p in range(2):
        o = p * HC
        keep[:, o : o + HB] = f[p, :, at(kb, c)] * mask_b
        send[:, o : o + HB] = f[p, :, at(kb, 1 - c)] * mask_b
        one = (f[p, :, at(k1, 0)] * mask_1).astype(F32)
        two = jnp.dot(f[p, :, at(k2, 0)] * mask_2, shift, preferred_element_type=F32)
        small = jnp.where(first, one, two)
        low, high = small[:, :HS], small[:, HS:]
        keep[:, o + HB : o + HC] = jnp.where(c == 0, low, high).astype(BF16)
        send[:, o + HB : o + HC] = jnp.where(c == 0, high, low).astype(BF16)


def left_kernel(widths, keep, send, got_mine, got_theirs, big, small):
    _, c, _, _ = place()
    _, _, _, a = supers(widths)
    back = (iota((HB, HB), 0) == iota((HB, HB), 1) + a).astype(BF16)
    mine = jnp.concatenate([keep[...], got_mine[...]], axis=0)
    theirs = jnp.concatenate([send[...], got_theirs[...]], axis=0)
    for p in range(2):
        o = p * HC
        for part, half in ((c, mine), (1 - c, theirs)):
            at = pl.ds(pl.multiple_of((2 * part + p) * HB, HB), HB)
            big[at, :] = half[:, o : o + HB].astype(F32).T.astype(BF16)
        m, t = mine[:, o + HB : o + HC].astype(F32), theirs[:, o + HB : o + HC].astype(F32)
        low, high = jnp.where(c == 0, m, t), jnp.where(c == 0, t, m)
        both = jnp.concatenate([low, high], axis=1)
        moved = jnp.dot(both.astype(BF16), back, preferred_element_type=F32)
        small[p * HB : (p + 1) * HB] = both.T.astype(BF16)
        small[(2 + p) * HB : (3 + p) * HB] = moved.T.astype(BF16)


def rows_at(bit, count):
    return pl.ds(pl.multiple_of(bit * count, count), count)


def block_copies(offsets, a_own, a_sib, us, vs, left, rows, sems):
    _, c, x, y = place()
    side = 1 - 2 * c
    copies = []
    for i, (dx, dy) in enumerate(offsets):
        at = lax.rem(y + dy, NY) * NX + lax.rem(x + dx * side + NX, NX)
        cols = pl.ds(pl.multiple_of(at * 2 * ROWS, 2 * ROWS), 2 * ROWS)
        pairs = [
            (us[i], rows.at[i, rows_at(c, ROWS)]),
            (vs[i], rows.at[i, rows_at(1 - c, ROWS)]),
            (a_own.at[:, cols], left.at[i, : 2 * ROWS]),
            (a_sib.at[:, cols], left.at[i, 2 * ROWS :]),
        ]
        copies += [pltpu.make_async_copy(v, to, sems.at[4 * i + j]) for j, (v, to) in enumerate(pairs)]
    return copies


def add_blocks(copies, left, rows, get, put):
    z = None
    for i in range(len(copies) // 4):
        for copy in copies[4 * i : 4 * i + 4]:
            copy.wait()
        d = jnp.dot(left[i], rows[i], preferred_element_type=F32)
        z = d if z is None else z + d
    for s in range(2):
        re, im = z[2 * s * ROWS : (2 * s + 1) * ROWS], z[(2 * s + 1) * ROWS : (2 * s + 2) * ROWS]
        old_re, old_im = get(s)
        put(s, old_re + (re[:, :HC] - im[:, HC:]), old_im + (re[:, HC:] + im[:, :HC]))


def acc_kernel(offsets, has_acc, *refs):
    refs = list(refs)
    old = refs.pop(0) if has_acc else None
    n = len(offsets)
    a_own, a_sib, us, vs = refs[0], refs[1], refs[2 : 2 + n], refs[2 + n : 2 + 2 * n]
    out, left, rows, sems = refs[2 + 2 * n :]
    copies = block_copies(offsets, a_own, a_sib, us, vs, left, rows, sems)
    for copy in copies:
        copy.start()

    def get(s):
        if old is None:
            return 0.0, 0.0
        return old[s, :, :HC], old[s, :, HC:]

    def put(s, re, im):
        out[s, :, :HC] = re
        out[s, :, HC:] = im

    add_blocks(copies, left, rows, get, put)


def column_kernel(structure, widths, old, a_own, a_sib, u, v, big_in, small_in, own_out, sib_out, q_out, *scratch):
    left, rows, big, small, gs, own, sib, q, sems, in_sems = scratch
    g, c, _, _ = place()
    kb, k1, k2, a = supers(widths)

    def get(s):
        return old[s, :, :HC], old[s, :, HC:]

    def put(s, re, im):
        base = (g + s * (1 - 2 * c)) * 6
        mask_b = row_mask(structure, base, 6, kb, HB)
        mask_1 = row_mask(structure, base, 6, k1, HS)
        mask_2 = row_mask(structure, base, 6, k2, HS)
        mask_s = jnp.where(iota((ROWS, HS), 1) + c * HS < a, mask_1, mask_2)
        out = own if s == 0 else sib
        for p, w in ((0, re), (1, im)):
            vb = -(w[:, :HB] * mask_b)
            vs = -(w[:, HB:] * mask_s)
            out[:, p * HC : p * HC + HB] = vb
            out[:, p * HC + HB : (p + 1) * HC] = vs
            for part, lo, hi in ((vb, p * HB, (p + 1) * HB), (vs, 2 * HB + p * HS, 2 * HB + (p + 1) * HS)):
                top = part.astype(BF16)
                gs[s * ROWS : (s + 1) * ROWS, lo:hi] = top
                gs[(s + 2) * ROWS : (s + 3) * ROWS, lo:hi] = (part - top.astype(F32)).astype(BF16)

    blocks = block_copies([(2, 1)], a_own, a_sib, [u], [v], left, rows, in_sems)
    lefts = [
        pltpu.make_async_copy(big_in, big, in_sems.at[4]),
        pltpu.make_async_copy(small_in, small, in_sems.at[5]),
    ]
    for copy in blocks + lefts:
        copy.start()
    add_blocks(blocks, left, rows, get, put)
    copies = [pltpu.make_async_copy(sib, sib_out, sems.at[0]), pltpu.make_async_copy(own, own_out, sems.at[1])]
    for copy in copies:
        copy.start()

    def across(left, lo, hi):
        twice = jnp.concatenate([left[...], left[...]], axis=1)
        return jnp.dot(twice, gs[:, lo:hi], preferred_element_type=F32)

    lefts[0].wait()
    z = across(big, 0, BIG)
    for h in range(2):
        re, im = z[2 * h * HB : (2 * h + 1) * HB], z[(2 * h + 1) * HB : (2 * h + 2) * HB]
        for t in range(8):
            r = slice(32 * t, 32 * t + 32)
            q[8 * h + t, :, :HB] = re[r, :HB] - im[r, HB:]
            q[8 * h + t, :, HB:BIG] = re[r, HB:] + im[r, :HB]
    copies.append(pltpu.make_async_copy(q.at[:, :, :BIG], q_out.at[:, :, :BIG], sems.at[2]))
    copies[2].start()
    lefts[1].wait()
    z = across(small, BIG, BIG + HB)
    col = iota((HB, HS), 1) + c * HS
    row = iota((HB, HS), 0)
    parts = []
    for i in range(2):
        re, im = z[2 * i * HB : (2 * i + 1) * HB], z[(2 * i + 1) * HB : (2 * i + 2) * HB]
        parts.append((re[:, :HS] - im[:, HS:], re[:, HS:] + im[:, :HS]))
    for p in range(2):
        e = jnp.where(
            col < a, jnp.where(row < a, parts[0][p], 0.0), jnp.where(row < HB - a, parts[1][p], 0.0)
        )
        at = slice(BIG + p * HS, BIG + (p + 1) * HS)
        for t in range(8):
            q[t, :, at] = e[32 * t : 32 * t + 32]
            q[8 + t, :, at] = jnp.zeros((32, HS), F32)
    copies.append(pltpu.make_async_copy(q.at[:, :, BIG:], q_out.at[:, :, BIG:], sems.at[3]))
    copies[3].start()
    for copy in copies:
        copy.wait()


def spread_kernel(widths, weights, mine, other, out, keep, send, wide):
    _, c, _, _ = place()
    odd, _ = z_bits()
    kb, k1, k2, a = supers(widths)
    wr, wi = weights[0, 0], weights[0, 1]
    back = (iota((HB, HB), 0) == iota((HB, HB), 1) + a).astype(BF16)
    lane = iota((ROWS, HB), 1)
    halves = []
    for ref in (mine, other):
        halves.append([(ref[:, p * HC : p * HC + HB], ref[:, p * HC + HB : (p + 1) * HC]) for p in range(2)])

    def at(k, part):
        return pl.ds(pl.multiple_of(k * BIG + part * HB, HB), HB)

    zero = jnp.zeros((ROWS, HB), BF16)
    small = []
    for p in range(2):
        m, t = halves[0][p], halves[1][p]
        out[p, :, at(kb, c)] = m[0].astype(BF16)
        out[p, :, at(kb, 1 - c)] = t[0].astype(BF16)
        low, high = jnp.where(c == 0, m[1], t[1]), jnp.where(c == 0, t[1], m[1])
        s = jnp.concatenate([low, high], axis=1)
        sb = s.astype(BF16)
        out[p, :, at(k1, 0)] = jnp.where(lane < a, s, 0.0).astype(BF16)
        out[p, :, at(k1, 1)] = zero
        out[p, :, at(k2, 0)] = jnp.dot(sb, back, preferred_element_type=F32).astype(BF16)
        out[p, :, at(k2, 1)] = zero
        small.append(s)
    for i, part in ((0, c), (1, 1 - c)):
        wide[:, at(0, part)] = wr * halves[i][1][0] + wi * halves[i][0][0]
    wide[:, BIG:] = wr * small[1] + wi * small[0]
    keep[...] = wide[rows_at(odd, 96), :]
    send[...] = wide[rows_at(1 - odd, 96), :]


def second_kernel(old, got, keep, send, total):
    _, bit = z_bits()
    total[...] = old[...] + got[...]
    keep[...] = total[rows_at(bit, 48), :]
    send[...] = total[rows_at(1 - bit, 48), :]


def pivot_kernel(widths, weights, pivot, sums, keep, got, block, pay, wide, column):
    g = lax.axis_index("grid")
    kb, k1, k2, a = supers(widths)
    wr, wi = weights[0, 0], weights[0, 1]
    m, t = sums[0], sums[1]
    for i in range(1, 8):
        m, t = m + sums[2 * i], t + sums[2 * i + 1]
    row = iota((32, BIG), 0) + g * 32
    line = iota((32, BIG), 1)
    blank = jnp.zeros((32, HB), F32)
    q = []
    for p in range(2):
        full = jnp.concatenate([u[:, p * HB : (p + 1) * HB] for u in (m, t)], axis=1)
        e = jnp.concatenate([u[:, BIG + p * HS : BIG + (p + 1) * HS] for u in (m, t)], axis=1)
        moved = pltpu.roll(e, HB - a, 1)
        q.append((full, jnp.concatenate([e, blank], axis=1), jnp.concatenate([moved, blank], axis=1)))
    for i, (k, w) in enumerate(((kb, BIG), (k1, a), (k2, HB - a))):
        live = (row < w) & (line < w)
        blocks = []
        for p in range(2):
            b = jnp.where(live, pivot[p, k] - q[p][i], 0.0)
            block[p, k] = b
            blocks.append(b)
        wide[pl.ds(pl.multiple_of(k * 32, 32), 32), :] = wr * blocks[1] + wi * blocks[0]
    d = keep[...] + got[...]
    lane = iota((48, HB), 1)
    small = d[:, BIG:]
    none = jnp.zeros((48, HB), F32)

    def at(k, part):
        return pl.ds(pl.multiple_of(k * BIG + part * HB, HB), HB)

    for part in range(2):
        column[:, at(kb, part)] = d[:, part * HB : (part + 1) * HB]
    column[:, at(k1, 0)] = jnp.where(lane < a, small, 0.0)
    column[:, at(k1, 1)] = none
    column[:, at(k2, 0)] = jnp.where(lane < HB - a, pltpu.roll(small, HB - a, 1), 0.0)
    column[:, at(k2, 1)] = none
    v, w = column[...], wide[...]
    pad = jnp.zeros((16, 32), F32)
    for p in range(16):
        parts = [v[16 * i : 16 * i + 16, 96 * p : 96 * p + 96] for i in range(3)]
        parts += [w[16 * i : 16 * i + 16, 32 * p : 32 * p + 32] for i in range(6)]
        pay[p] = jnp.concatenate(parts + [pad], axis=1)


def density_kernel(pays, column, pivot):
    total = pays[0]
    for p in range(1, 16):
        total = total + pays[p]
    for b0 in range(2):
        for b1 in range(2):
            part = [pays[(b0 + 2 * b1 + 4 * b2) * NH + h] for b2 in range(2) for h in range(NH)]
            v = (part[0] + part[1]) + (part[2] + part[3])
            for i in range(3):
                row = 96 * b0 + 48 * b1 + 16 * i
                column[row : row + 16] = v[:, 96 * i : 96 * i + 96]
    for i in range(6):
        pivot[i // 2, 16 * (i % 2) : 16 * (i % 2) + 16] = total[:, 288 + 32 * i : 320 + 32 * i]


def local(factor_cols, ancestor_inverse, pivot_inverse, structure, widths, pole_weights):
    structure = structure.T

    def over_grid(v, perm):
        return lax.ppermute(v, "grid", perm)

    block = sds((ROWS, 2 * HC), BF16)
    keep, send = call(
        prep_kernel,
        [block, block],
        [(structure, "s"), (widths, "s"), (factor_cols[0], "v")],
        "prep",
        flops=2 * 2 * ROWS * HB * HB,
    )
    a_own = ancestor_inverse[0].reshape(2 * ROWS, -1)
    a_sib = over_grid(a_own, CORE)
    keep, send, a_sib = lax.optimization_barrier((keep, send, a_sib))
    got_mine, got_theirs = over_grid(send, CORE), over_grid(keep, CORE)
    got_mine, got_theirs = lax.optimization_barrier((got_mine, got_theirs))

    def first(v):
        return [over_grid(v, perm) for perm in (FROM_AHEAD, FROM_BEHIND, FROM_Y)]

    def second(ahead, behind, beside):
        return [over_grid(ahead, FROM_AHEAD), over_grid(beside, FROM_BEHIND), over_grid(ahead, FROM_Y)]

    def add(old, offsets, us, vs):
        n = len(offsets)
        ins = ([] if old is None else [(old, "v")]) + [(a, "h") for a in (a_own, a_sib)]
        ins += [(b, "h") for b in (*us, *vs)]
        return call(
            functools.partial(acc_kernel, offsets, old is not None),
            [sds((2, ROWS, 2 * HC), F32)],
            ins,
            "product",
            flops=2 * n * 4 * ROWS * 2 * ROWS * 2 * HC,
            scratch=[
                pltpu.VMEM((n, 4 * ROWS, 2 * ROWS), BF16),
                pltpu.VMEM((n, 2 * ROWS, 2 * HC), BF16),
                pltpu.SemaphoreType.DMA((4 * n,)),
            ],
        )[0]

    v1 = first(got_mine)
    u1 = first(keep)
    v2 = second(*v1)
    acc = add(None, [(0, 0)], [keep], [got_mine])
    big, small = call(
        left_kernel,
        [sds((4 * HB, 2 * ROWS), BF16)] * 2,
        [(widths, "s"), (keep, "v"), (send, "v"), (got_mine, "v"), (got_theirs, "v")],
        "left",
        flops=2 * 2 * 2 * ROWS * HB * HB,
    )
    *u1, acc, big, small = lax.optimization_barrier((*u1, acc, big, small))
    u2 = second(*u1)
    acc = add(acc, [(1, 0), (-1, 0), (0, 1)], u1, v1)
    v3 = over_grid(v2[2], FROM_AHEAD)
    *u2, acc = lax.optimization_barrier((*u2, acc))
    u3 = over_grid(u2[2], FROM_AHEAD)
    acc = add(acc, [(2, 0), (-1, 1), (1, 1)], u2, v2)
    own, sib, q = call(
        column_kernel,
        [sds((ROWS, 2 * HC), F32)] * 2 + [sds((16, 32, BIG + HB), F32)],
        [
            (structure, "s"),
            (widths, "s"),
            (acc, "v"),
            (a_own, "h"),
            (a_sib, "h"),
            (u3, "h"),
            (v3, "h"),
            (big, "h"),
            (small, "h"),
        ],
        "column",
        flops=2 * 4 * ROWS * 2 * ROWS * 2 * HC + 2 * 2 * 1024 * 2 * ROWS * 768,
        scratch=[
            pltpu.VMEM((1, 4 * ROWS, 2 * ROWS), BF16),
            pltpu.VMEM((1, 2 * ROWS, 2 * HC), BF16),
            pltpu.VMEM((4 * HB, 2 * ROWS), BF16),
            pltpu.VMEM((4 * HB, 2 * ROWS), BF16),
            pltpu.VMEM((4 * ROWS, 2 * HC), BF16),
            pltpu.VMEM((ROWS, 2 * HC), F32),
            pltpu.VMEM((ROWS, 2 * HC), F32),
            pltpu.VMEM((16, 32, BIG + HB), F32),
            pltpu.SemaphoreType.DMA((4,)),
            pltpu.SemaphoreType.DMA((6,)),
        ],
        limit=20,
        out_space=pltpu.HBM,
    )
    other = over_grid(sib, CORE)
    sums = lax.all_to_all(q, "grid", 0, 0, tiled=True)
    column_inverse, d_keep, d_send = call(
        spread_kernel,
        [sds((2, ROWS, 3 * BIG), BF16)] + [sds((96, 768), F32)] * 2,
        [(widths, "s"), (pole_weights, "s"), (own, "v"), (other, "v")],
        "spread",
        scratch=[pltpu.VMEM((ROWS, 768), F32)],
    )
    d_got = lax.ppermute(d_send, "pole", z_pair(1))
    d_keep, d_send = call(
        second_kernel,
        [sds((48, 768), F32)] * 2,
        [(d_keep, "v"), (d_got, "v")],
        "second",
        scratch=[pltpu.VMEM((96, 768), F32)],
    )
    d_got = lax.ppermute(d_send, "pole", z_pair(2))
    sums, d_keep = lax.optimization_barrier((sums, d_keep))
    pivot_block, pay = call(
        pivot_kernel,
        [sds((2, 3, 32, BIG), F32), sds((16, 16, 512), F32)],
        [
            (widths, "s"),
            (pole_weights, "s"),
            (pivot_inverse[0], "v"),
            (sums, "v"),
            (d_keep, "v"),
            (d_got, "v"),
        ],
        "pivot",
        scratch=[pltpu.VMEM((96, BIG), F32), pltpu.VMEM((48, 3 * BIG), F32)],
    )
    pays = lax.all_to_all(pay, "pole", 0, 0, tiled=True)
    density_column, density_pivot = call(
        density_kernel, [sds((ROWS, 96), F32), sds((3, 32, 32), F32)], [(pays, "v")], "density"
    )
    return (column_inverse[None], pivot_block[None], density_column, density_pivot)


def solution(mesh):
    in_specs = (
        P("pole", None, "grid", None),
        P("pole", None, "grid", None),
        P("pole", None, None, "grid", None),
        P(),
        P(),
        P("pole", None),
    )
    out_specs = (
        P("pole", None, "grid", None),
        P("pole", None, None, "grid", None),
        P("grid", "pole"),
        P(None, "grid", "pole"),
    )
    return jax.shard_map(local, mesh=mesh, in_specs=in_specs, out_specs=out_specs, check_vma=False)
```

time: 120 us -> 110 us (0.917)
  Pallas kernels: 24.8 us -> 18.8 us
  blocking collectives: 32.4 us -> 27.5 us
  local copies, waits for them, and re-layouts: 5.94 us -> 2.63 us
  waiting for transfers between devices: 24.6 us -> 27.3 us
  starting transfers between devices: 29.3 us -> 31.9 us
    all_to_all x1, waiting for transfers between devices: 14 us -> 3.32 us  [local(): sums = lax.all_to_all(q, 'grid', 0, 0, tiled=True)]
    ppermute x2, waiting for transfers between devices: 1.67 us -> 10.7 us  [the longest x1 7.32 us: local(): d_got = lax.ppermute(d_send, 'pole', z_pair(1))]
    pallas_call x10, Pallas kernels: 24.8 us -> 18.8 us  [call(): pl.pallas_call(body, out_shape=tuple(outs), in_specs=[pl.BlockSpec(memory...]
    all_to_all x1, blocking collectives: 32.4 us -> 27.5 us  [local(): pays = lax.all_to_all(pay, 'pole', 0, 0, tiled=True)]
    ppermute x18, waiting for transfers between devices: 8.87 us -> 13.3 us  [over_grid(): return lax.ppermute(v, 'grid', perm)]
    unnamed x33 -> x20, local copies, waits for them, and re-layouts: 5.94 us -> 2.63 us
    ppermute x18, starting transfers between devices: 19.1 us -> 20.5 us  [over_grid(): return lax.ppermute(v, 'grid', perm)]
    ppermute x2, starting transfers between devices: 4.56 us -> 5.98 us  [the longest x1 3.36 us: local(): d_got = lax.ppermute(d_send, 'pole', z_pair(2))]
  transfers between devices with their start and end apart: 21 -> 21, of which waited for: 8 -> 11; matrix products, arithmetic and copies ran while one was open for 1% -> 0% of each run, Pallas kernels for 14% -> 10%
where the time goes in v3:
time: 110 us; the launch traced here: 109 us
  starting transfers between devices  31.9 us (29%)
  blocking collectives  27.5 us (25%)
  waiting for transfers between devices  27.3 us (25%)
  Pallas kernels  18.8 us (17%)
  local copies, waits for them, and re-layouts  2.63 us (2%)
    all_to_all x1, blocking collectives, local(): pays = lax.all_to_all(pay, 'pole', 0, 0, tiled=True)  27.5 us
    ppermute x18, starting transfers between devices, over_grid(): return lax.ppermute(v, 'grid', perm)  20.5 us
    pallas_call x10, Pallas kernels, call(): pl.pallas_call(body, out_shape=tuple(outs), in_specs=[pl.BlockSpec(memory...  18.8 us
    ppermute x18, waiting for transfers between devices, over_grid(): return lax.ppermute(v, 'grid', perm)  13.3 us
    ppermute x1, waiting for transfers between devices, local(): d_got = lax.ppermute(d_send, 'pole', z_pair(1))  7.32 us
    all_to_all x1, starting transfers between devices, local(): sums = lax.all_to_all(q, 'grid', 0, 0, tiled=True)  5.42 us
    ppermute x1, waiting for transfers between devices, local(): d_got = lax.ppermute(d_send, 'pole', z_pair(2))  3.37 us
    ppermute x1, starting transfers between devices, local(): d_got = lax.ppermute(d_send, 'pole', z_pair(2))  3.36 us
  transfers between devices with their start and end apart: 21, of which 11 were waited for; matrix products, arithmetic and copies ran while one was open for 0% of the time, Pallas kernels for 10%

profile of v3, /device:TPU:8, one launch (start us, length us, event | category | flops | bytes accessed | tf_op | source)
XLA Modules:
  0.0 108.9 jit_solution(11533788827368396804)
XLA Ops:
  0.8 1.3 %copy-done.1 = bf16[1,2,192,1536]{3,2,1,0:T(8,128)(2,1)S(1)} copy-done((bf16[1,2,192,1536]{3,2,1,0:T(8,128)(2,1)S(1)}, bf16[1,2,192,1536]{3,2,1,0:T(8,128)(2,1)}, u32[]{:S(2)}) %copy-start.1) | copy-done | bytes 1179672
  4.2 1.3 %collective-permute-done.refs_1_.refs_2_.a_sib = bf16[384,3072]{1,0:T(8,128)(2,1)S(1)} collective-permute-done((bf16[384,3072]{1,0:T(8,128)(2,1)}, bf16[384,3072]{1,0:T(8,128)(2,1)S(1)}, u32[]{:S(2)}, u32[]{:S(2)}) %collective-permute-start) | collective-permute-done | bytes 2359328 | tf_op jit(solution)/shard_map/ppermute | solution.py:381
  6.0 2.8 %collective-permute-start.1 = (bf16[192,768]{1,0:T(8,128)(2,1)S(1)}, bf16[192,768]{1,0:T(8,128)(2,1)S(1)}, u32[]{:S(2)}, u32[]{:S(2)}) collective-permute-start(bf16[192,768]{1,0:T(8,128)(2,1)S(1)} %get-tuple-element.39.refs_2_.keep), channel_id=1, source_target_pairs={{2,0},{7,1},{4,2},{1,3},{6,4},{3,5},{0,6},{5,7},{10,8},{15,9},{12,... | collective-permute-start | bytes 884744 | tf_op jit(solution)/shard_map/ppermute | solution.py:381
  8.7 1.4 %collective-permute-start.3 = (bf16[192,768]{1,0:T(8,128)(2,1)S(1)}, bf16[192,768]{1,0:T(8,128)(2,1)S(1)}, u32[]{:S(2)}, u32[]{:S(2)}) collective-permute-start(bf16[192,768]{1,0:T(8,128)(2,1)S(1)} %get-tuple-element.39.refs_2_.keep), channel_id=1, source_target_pairs={{8,0},{9,1},{10,2},{11,3},{12,4},{13,5},{14,6},{15,7},{0,8},{1,9},... | collective-permute-start | bytes 884744 | tf_op jit(solution)/shard_map/ppermute | solution.py:381
  10.2 2.2 %collective-permute-start.9 = (bf16[192,768]{1,0:T(8,128)(2,1)S(1)}, bf16[192,768]{1,0:T(8,128)(2,1)S(1)}, u32[]{:S(2)}, u32[]{:S(2)}) collective-permute-start(bf16[192,768]{1,0:T(8,128)(2,1)S(1)} %collective-permute-done.4.refs_3_.got_mine), channel_id=1, source_target_pairs={{2,0},{7,1},{4,2},{1,3},{6,4},{3,5},{0,6},{5,7},{10,8},{15,9},{12,... | collective-permute-start | bytes 884744 | tf_op jit(solution)/shard_map/ppermute | solution.py:381
  12.4 1.6 %collective-permute-start.11 = (bf16[192,768]{1,0:T(8,128)(2,1)S(1)}, bf16[192,768]{1,0:T(8,128)(2,1)S(1)}, u32[]{:S(2)}, u32[]{:S(2)}) collective-permute-start(bf16[192,768]{1,0:T(8,128)(2,1)S(1)} %collective-permute-done.4.refs_3_.got_mine), channel_id=1, source_target_pairs={{8,0},{9,1},{10,2},{11,3},{12,4},{13,5},{14,6},{15,7},{0,8},{1,9},... | collective-permute-start | bytes 884744 | tf_op jit(solution)/shard_map/ppermute | solution.py:381
  14.0 1.1 left.1
  15.1 1.0 product.3.refs_0_
  16.1 0.9 collective-permute-start.10
  17.1 1.8 %collective-permute-done.2.refs_4_ = bf16[192,768]{1,0:T(8,128)(2,1)S(1)} collective-permute-done((bf16[192,768]{1,0:T(8,128)(2,1)S(1)}, bf16[192,768]{1,0:T(8,128)(2,1)S(1)}, u32[]{:S(2)}, u32[]{:S(2)}) %collective-permute-start.2) | collective-permute-done | bytes 294944 | tf_op jit(solution)/shard_map/ppermute | solution.py:381
  18.8 3.1 %collective-permute-start.6 = (bf16[192,768]{1,0:T(8,128)(2,1)S(1)}, bf16[192,768]{1,0:T(8,128)(2,1)S(1)}, u32[]{:S(2)}, u32[]{:S(2)}) collective-permute-start(bf16[192,768]{1,0:T(8,128)(2,1)S(1)} %collective-permute-done.1.refs_3_), channel_id=1, source_target_pairs={{2,0},{7,1},{4,2},{1,3},{6,4},{3,5},{0,6},{5,7},{10,8},{15,9},{12,... | collective-permute-start | bytes 884744 | tf_op jit(solution)/shard_map/ppermute | solution.py:381
  22.4 2.5 %collective-permute-done.11.refs_8_ = bf16[192,768]{1,0:T(8,128)(2,1)S(1)} collective-permute-done((bf16[192,768]{1,0:T(8,128)(2,1)S(1)}, bf16[192,768]{1,0:T(8,128)(2,1)S(1)}, u32[]{:S(2)}, u32[]{:S(2)}) %collective-permute-start.11) | collective-permute-done | bytes 294944 | tf_op jit(solution)/shard_map/ppermute | solution.py:381
  24.9 1.5 %collective-permute-start.14 = (bf16[192,768]{1,0:T(8,128)(2,1)S(1)}, bf16[192,768]{1,0:T(8,128)(2,1)S(1)}, u32[]{:S(2)}, u32[]{:S(2)}) collective-permute-start(bf16[192,768]{1,0:T(8,128)(2,1)S(1)} %collective-permute-done.9.refs_6_), channel_id=1, source_target_pairs={{8,0},{9,1},{10,2},{11,3},{12,4},{13,5},{14,6},{15,7},{0,8},{1,9},... | collective-permute-start | bytes 884744 | tf_op jit(solution)/shard_map/ppermute | solution.py:381
  26.7 1.0 collective-permute-start.12
  28.5 1.2 %collective-permute-start.13 = (bf16[192,768]{1,0:T(8,128)(2,1)S(1)}, bf16[192,768]{1,0:T(8,128)(2,1)S(1)}, u32[]{:S(2)}, u32[]{:S(2)}) collective-permute-start(bf16[192,768]{1,0:T(8,128)(2,1)S(1)} %collective-permute-done.11.refs_8_), channel_id=1, source_target_pairs={{6,0},{3,1},{0,2},{5,3},{2,4},{7,5},{4,6},{1,7},{14,8},{11,9},{8,1... | collective-permute-start | bytes 884744 | tf_op jit(solution)/shard_map/ppermute | solution.py:381
  29.7 3.0 %product.4.refs_0_ = f32[2,192,768]{2,1,0:T(8,128)S(1)} custom-call(f32[2,192,768]{2,1,0:T(8,128)S(1)} %product.3.refs_0_, bf16[384,3072]{1,0:T(8,128)(2,1)S(1)} %bitcast.8, bf16[384,3072]{1,0:T(8,128)(2,1)S(1)} %collective-permute-done.refs_1_.refs_2_.a_sib, bf16[192,768]{1,0:T(8,128)(2,1)S(1)} %collective-permute-done.1.refs_3_, ...), custom_call_target="tpu_custom_call" | custom-call | flops 1358954496 | bytes 8847360 | tf_op jit(solution)/shard_map/product/pallas_call | solution.py:85
  32.7 2.3 %collective-permute-start.15 = (bf16[192,768]{1,0:T(8,128)(2,1)S(1)}, bf16[192,768]{1,0:T(8,128)(2,1)S(1)}, u32[]{:S(2)}, u32[]{:S(2)}) collective-permute-start(bf16[192,768]{1,0:T(8,128)(2,1)S(1)} %collective-permute-done.8.refs_5_), channel_id=1, source_target_pairs={{2,0},{7,1},{4,2},{1,3},{6,4},{3,5},{0,6},{5,7},{10,8},{15,9},{12,... | collective-permute-start | bytes 884744 | tf_op jit(solution)/shard_map/ppermute | solution.py:381
  35.1 2.1 %collective-permute-done.14.refs_8_ = bf16[192,768]{1,0:T(8,128)(2,1)S(1)} collective-permute-done((bf16[192,768]{1,0:T(8,128)(2,1)S(1)}, bf16[192,768]{1,0:T(8,128)(2,1)S(1)}, u32[]{:S(2)}, u32[]{:S(2)}) %collective-permute-start.14) | collective-permute-done | bytes 294944 | tf_op jit(solution)/shard_map/ppermute | solution.py:381
  37.1 1.1 %collective-permute-start.16 = (bf16[192,768]{1,0:T(8,128)(2,1)S(1)}, bf16[192,768]{1,0:T(8,128)(2,1)S(1)}, u32[]{:S(2)}, u32[]{:S(2)}) collective-permute-start(bf16[192,768]{1,0:T(8,128)(2,1)S(1)} %collective-permute-done.14.refs_8_), channel_id=1, source_target_pairs={{2,0},{7,1},{4,2},{1,3},{6,4},{3,5},{0,6},{5,7},{10,8},{15,9},{12,... | collective-permute-start | bytes 884744 | tf_op jit(solution)/shard_map/ppermute | solution.py:381
  38.2 3.0 %product.5.old = f32[2,192,768]{2,1,0:T(8,128)S(1)} custom-call(f32[2,192,768]{2,1,0:T(8,128)S(1)} %product.4.refs_0_, bf16[384,3072]{1,0:T(8,128)(2,1)S(1)} %bitcast.9, bf16[384,3072]{1,0:T(8,128)(2,1)S(1)} %collective-permute-done.refs_1_.refs_2_.a_sib, bf16[192,768]{1,0:T(8,128)(2,1)S(1)} %collective-permute-done.6.refs_3_, ...), custom_call_target="tpu_custom_call" | custom-call | flops 1358954496 | bytes 8847360 | tf_op jit(solution)/shard_map/product/pallas_call | solution.py:85
  41.2 2.6 %collective-permute-done.16.v = bf16[192,768]{1,0:T(8,128)(2,1)S(1)} collective-permute-done((bf16[192,768]{1,0:T(8,128)(2,1)S(1)}, bf16[192,768]{1,0:T(8,128)(2,1)S(1)}, u32[]{:S(2)}, u32[]{:S(2)}) %collective-permute-start.16) | collective-permute-done | bytes 294944 | tf_op jit(solution)/shard_map/ppermute | solution.py:381
  43.8 5.8 %column.1 = (f32[192,768]{1,0:T(8,128)}, f32[192,768]{1,0:T(8,128)}, f32[16,32,768]{2,1,0:T(8,128)}) custom-call(s32[3,96]{1,0:T(4,128)S(1)} %bitcast.14, s32[3]{0:T(128)S(1)} %copy-done.5, f32[2,192,768]{2,1,0:T(8,128)S(1)} %product.5.old, bf16[384,3072]{1,0:T(8,128)(2,1)S(1)} %bitcast.10, bf16[384,3072]{1,0:T(8,128)(2,1)S(1)} %collective-permute-done.refs_1_.refs_2_.a_sib, ...), custom_call_target="tpu_custom_call" | custom-call | flops 1660944384 | bytes 10814604 | tf_op jit(solution)/shard_map/column/pallas_call | solution.py:85
  49.7 5.4 %all-to-all-start = ((f32[16,32,768]{2,1,0:T(8,128)}), f32[16,32,768]{2,1,0:T(8,128)S(1)}, u32[]{:S(2)}, u32[]{:S(2)}) async-start(f32[16,32,768]{2,1,0:T(8,128)} %get-tuple-element.59), calls=%async_computation | async-start | bytes 3145728 | tf_op jit(solution)/shard_map/all_to_all | solution.py:470
  55.3 1.9 %collective-permute-done.17.other = f32[192,768]{1,0:T(8,128)S(1)} collective-permute-done((f32[192,768]{1,0:T(8,128)S(1)}, f32[192,768]{1,0:T(8,128)S(1)}, u32[]{:S(2)}, u32[]{:S(2)}) %collective-permute-start.17) | collective-permute-done | bytes 589856 | tf_op jit(solution)/shard_map/ppermute | solution.py:381
  57.2 1.9 %spread.1 = (bf16[2,192,1536]{2,1,0:T(8,128)(2,1)}, f32[96,768]{1,0:T(8,128)S(1)}, f32[96,768]{1,0:T(8,128)S(1)}) custom-call(s32[3]{0:T(128)S(1)} %copy-done.5, f32[1,2]{1,0:T(1,128)S(1)} %copy-done.8, f32[192,768]{1,0:T(8,128)S(1)} %copy-done.2, f32[192,768]{1,0:T(8,128)S(1)} %collective-permute-done.17.other), custom_call_target="tpu_custom_call" | custom-call | bytes 2949140 | tf_op jit(solution)/shard_map/spread/pallas_call | solution.py:85
  59.1 2.6 %collective-permute-start.18 = (f32[96,768]{1,0:T(8,128)S(1)}, f32[96,768]{1,0:T(8,128)S(1)}, u32[]{:S(2)}, u32[]{:S(2)}) collective-permute-start(f32[96,768]{1,0:T(8,128)S(1)} %get-tuple-element.61), channel_id=1, source_target_pairs={{32,0},{48,16},{0,32},{16,48},{96,64},{112,80},{64,96},{80,112},{1... | collective-permute-start | bytes 884744 | tf_op jit(solution)/shard_map/ppermute | solution.py:478
  61.7 7.3 %collective-permute-done.18.got = f32[96,768]{1,0:T(8,128)S(1)} collective-permute-done((f32[96,768]{1,0:T(8,128)S(1)}, f32[96,768]{1,0:T(8,128)S(1)}, u32[]{:S(2)}, u32[]{:S(2)}) %collective-permute-start.18) | collective-permute-done | bytes 294944 | tf_op jit(solution)/shard_map/ppermute | solution.py:478
  69.1 3.4 %collective-permute-start.19 = (f32[48,768]{1,0:T(8,128)S(1)}, f32[48,768]{1,0:T(8,128)S(1)}, u32[]{:S(2)}, u32[]{:S(2)}) collective-permute-start(f32[48,768]{1,0:T(8,128)S(1)} %get-tuple-element.65), channel_id=1, source_target_pairs={{64,0},{80,16},{96,32},{112,48},{0,64},{16,80},{32,96},{48,112},{1... | collective-permute-start | bytes 442376 | tf_op jit(solution)/shard_map/ppermute | solution.py:486
  72.5 3.3 %all-to-all-done.sums = f32[16,32,768]{2,1,0:T(8,128)S(1)} async-done(((f32[16,32,768]{2,1,0:T(8,128)}), f32[16,32,768]{2,1,0:T(8,128)S(1)}, u32[]{:S(2)}, u32[]{:S(2)}) %all-to-all-start) | async-done | bytes 1572896 | tf_op jit(solution)/shard_map/all_to_all | solution.py:470
  75.8 3.4 %collective-permute-done.19.got = f32[48,768]{1,0:T(8,128)S(1)} collective-permute-done((f32[48,768]{1,0:T(8,128)S(1)}, f32[48,768]{1,0:T(8,128)S(1)}, u32[]{:S(2)}, u32[]{:S(2)}) %collective-permute-start.19) | collective-permute-done | bytes 147488 | tf_op jit(solution)/shard_map/ppermute | solution.py:486
  79.2 1.5 %pivot.1 = (f32[2,3,32,512]{3,2,1,0:T(8,128)}, f32[16,16,512]{2,1,0:T(8,128)S(1)}) custom-call(s32[3]{0:T(128)S(1)} %copy-done.5, f32[1,2]{1,0:T(1,128)S(1)} %copy-done.8, f32[2,3,32,512]{3,2,1,0:T(8,128)S(1)} %bitcast.12, f32[16,32,768]{2,1,0:T(8,128)S(1)} %all-to-all-done.sums, f32[48,768]{1,0:T(8,128)S(1)} %get-tuple-element.64.keep, ...), custom_call_target="tpu_custom_call" | custom-call | bytes 3178516 | tf_op jit(solution)/shard_map/pivot/pallas_call | solution.py:85
  80.6 27.5 %all_to_all.10.pays = f32[16,16,512]{2,1,0:T(8,128)S(1)} all-to-all(f32[16,16,512]{2,1,0:T(8,128)S(1)} %get-tuple-element.67), channel_id=1, replica_groups=mesh['pole'=16,'grid'=16] {'pole'}, dimensions={0} | all-to-all | bytes 1048576 | tf_op jit(solution)/shard_map/all_to_all | solution.py:502
  (41 shorter events, 5.4 us)
Async XLA Ops:
  0.6 13.4 %copy-start.5 = (s32[3]{0:T(128)S(1)}, s32[3]{0:T(128)}, u32[]{:S(2)}) copy-start(s32[3]{0:T(128)} %widths.9) | copy-start | bytes 40
  0.6 4.8 %collective-permute-start = (bf16[384,3072]{1,0:T(8,128)(2,1)}, bf16[384,3072]{1,0:T(8,128)(2,1)S(1)}, u32[]{:S(2)}, u32[]{:S(2)}) collective-permute-start(bf16[384,3072]{1,0:T(8,128)(2,1)} %bitcast.6), channel_id=1, source_target_pairs={{1,0},{0,1},{3,2},{2,3},{5,4},{4,5},{7,6},{6,7},{9,8},{8,9},{11,10... | collective-permute-start | bytes 7077896 | tf_op jit(solution)/shard_map/ppermute | solution.py:381
  0.7 1.3 %copy-start.1 = (bf16[1,2,192,1536]{3,2,1,0:T(8,128)(2,1)S(1)}, bf16[1,2,192,1536]{3,2,1,0:T(8,128)(2,1)}, u32[]{:S(2)}) copy-start(bf16[1,2,192,1536]{3,2,1,0:T(8,128)(2,1)} %param.6) | copy-start | bytes 3538948
  2.0 0.7 copy-start.4
  2.7 0.7 copy-start.6
  3.4 11.7 %copy-start = (bf16[1,2,192,3072]{3,2,1,0:T(8,128)(2,1)S(1)}, bf16[1,2,192,3072]{3,2,1,0:T(8,128)(2,1)}, u32[]{:S(2)}) copy-start(bf16[1,2,192,3072]{3,2,1,0:T(8,128)(2,1)} %param.7) | copy-start | bytes 7077892
  5.5 4.7 %collective-permute-start.5 = (bf16[192,768]{1,0:T(8,128)(2,1)S(1)}, bf16[192,768]{1,0:T(8,128)(2,1)S(1)}, u32[]{:S(2)}, u32[]{:S(2)}) collective-permute-start(bf16[192,768]{1,0:T(8,128)(2,1)S(1)} %get-tuple-element.39.refs_2_.keep), channel_id=1, source_target_pairs={{1,0},{0,1},{3,2},{2,3},{5,4},{4,5},{7,6},{6,7},{9,8},{8,9},{11,10... | collective-permute-start | bytes 884744 | tf_op jit(solution)/shard_map/ppermute | solution.py:381
  5.6 4.6 %collective-permute-start.4 = (bf16[192,768]{1,0:T(8,128)(2,1)S(1)}, bf16[192,768]{1,0:T(8,128)(2,1)S(1)}, u32[]{:S(2)}, u32[]{:S(2)}) collective-permute-start(bf16[192,768]{1,0:T(8,128)(2,1)S(1)} %get-tuple-element.41.send), channel_id=1, source_target_pairs={{1,0},{0,1},{3,2},{2,3},{5,4},{4,5},{7,6},{6,7},{9,8},{8,9},{11,10... | collective-permute-start | bytes 884744 | tf_op jit(solution)/shard_map/ppermute | solution.py:381
  6.0 10.2 %collective-permute-start.1 = (bf16[192,768]{1,0:T(8,128)(2,1)S(1)}, bf16[192,768]{1,0:T(8,128)(2,1)S(1)}, u32[]{:S(2)}, u32[]{:S(2)}) collective-permute-start(bf16[192,768]{1,0:T(8,128)(2,1)S(1)} %get-tuple-element.39.refs_2_.keep), channel_id=1, source_target_pairs={{2,0},{7,1},{4,2},{1,3},{6,4},{3,5},{0,6},{5,7},{10,8},{15,9},{12,... | collective-permute-start | bytes 884744 | tf_op jit(solution)/shard_map/ppermute | solution.py:381
  8.7 10.1 %collective-permute-start.2 = (bf16[192,768]{1,0:T(8,128)(2,1)S(1)}, bf16[192,768]{1,0:T(8,128)(2,1)S(1)}, u32[]{:S(2)}, u32[]{:S(2)}) collective-permute-start(bf16[192,768]{1,0:T(8,128)(2,1)S(1)} %get-tuple-element.39.refs_2_.keep), channel_id=1, source_target_pairs={{6,0},{3,1},{0,2},{5,3},{2,4},{7,5},{4,6},{1,7},{14,8},{11,9},{8,1... | collective-permute-start | bytes 884744 | tf_op jit(solution)/shard_map/ppermute | solution.py:381
  8.7 10.1 %collective-permute-start.3 = (bf16[192,768]{1,0:T(8,128)(2,1)S(1)}, bf16[192,768]{1,0:T(8,128)(2,1)S(1)}, u32[]{:S(2)}, u32[]{:S(2)}) collective-permute-start(bf16[192,768]{1,0:T(8,128)(2,1)S(1)} %get-tuple-element.39.refs_2_.keep), channel_id=1, source_target_pairs={{8,0},{9,1},{10,2},{11,3},{12,4},{13,5},{14,6},{15,7},{0,8},{1,9},... | collective-permute-start | bytes 884744 | tf_op jit(solution)/shard_map/ppermute | solution.py:381
  10.2 11.7 %collective-permute-start.9 = (bf16[192,768]{1,0:T(8,128)(2,1)S(1)}, bf16[192,768]{1,0:T(8,128)(2,1)S(1)}, u32[]{:S(2)}, u32[]{:S(2)}) collective-permute-start(bf16[192,768]{1,0:T(8,128)(2,1)S(1)} %collective-permute-done.4.refs_3_.got_mine), channel_id=1, source_target_pairs={{2,0},{7,1},{4,2},{1,3},{6,4},{3,5},{0,6},{5,7},{10,8},{15,9},{12,... | collective-permute-start | bytes 884744 | tf_op jit(solution)/shard_map/ppermute | solution.py:381
  12.4 12.4 %collective-permute-start.11 = (bf16[192,768]{1,0:T(8,128)(2,1)S(1)}, bf16[192,768]{1,0:T(8,128)(2,1)S(1)}, u32[]{:S(2)}, u32[]{:S(2)}) collective-permute-start(bf16[192,768]{1,0:T(8,128)(2,1)S(1)} %collective-permute-done.4.refs_3_.got_mine), channel_id=1, source_target_pairs={{8,0},{9,1},{10,2},{11,3},{12,4},{13,5},{14,6},{15,7},{0,8},{1,9},... | collective-permute-start | bytes 884744 | tf_op jit(solution)/shard_map/ppermute | solution.py:381
  16.1 10.5 %collective-permute-start.10 = (bf16[192,768]{1,0:T(8,128)(2,1)S(1)}, bf16[192,768]{1,0:T(8,128)(2,1)S(1)}, u32[]{:S(2)}, u32[]{:S(2)}) collective-permute-start(bf16[192,768]{1,0:T(8,128)(2,1)S(1)} %collective-permute-done.4.refs_3_.got_mine), channel_id=1, source_target_pairs={{6,0},{3,1},{0,2},{5,3},{2,4},{7,5},{4,6},{1,7},{14,8},{11,9},{8,1... | collective-permute-start | bytes 884744 | tf_op jit(solution)/shard_map/ppermute | solution.py:381
  18.8 9.7 %collective-permute-start.6 = (bf16[192,768]{1,0:T(8,128)(2,1)S(1)}, bf16[192,768]{1,0:T(8,128)(2,1)S(1)}, u32[]{:S(2)}, u32[]{:S(2)}) collective-permute-start(bf16[192,768]{1,0:T(8,128)(2,1)S(1)} %collective-permute-done.1.refs_3_), channel_id=1, source_target_pairs={{2,0},{7,1},{4,2},{1,3},{6,4},{3,5},{0,6},{5,7},{10,8},{15,9},{12,... | collective-permute-start | bytes 884744 | tf_op jit(solution)/shard_map/ppermute | solution.py:381
  21.9 10.8 %collective-permute-start.7 = (bf16[192,768]{1,0:T(8,128)(2,1)S(1)}, bf16[192,768]{1,0:T(8,128)(2,1)S(1)}, u32[]{:S(2)}, u32[]{:S(2)}) collective-permute-start(bf16[192,768]{1,0:T(8,128)(2,1)S(1)} %collective-permute-done.3.refs_5_), channel_id=1, source_target_pairs={{6,0},{3,1},{0,2},{5,3},{2,4},{7,5},{4,6},{1,7},{14,8},{11,9},{8,1... | collective-permute-start | bytes 884744 | tf_op jit(solution)/shard_map/ppermute | solution.py:381
  21.9 10.8 %collective-permute-start.8 = (bf16[192,768]{1,0:T(8,128)(2,1)S(1)}, bf16[192,768]{1,0:T(8,128)(2,1)S(1)}, u32[]{:S(2)}, u32[]{:S(2)}) collective-permute-start(bf16[192,768]{1,0:T(8,128)(2,1)S(1)} %collective-permute-done.1.refs_3_), channel_id=1, source_target_pairs={{8,0},{9,1},{10,2},{11,3},{12,4},{13,5},{14,6},{15,7},{0,8},{1,9},... | collective-permute-start | bytes 884744 | tf_op jit(solution)/shard_map/ppermute | solution.py:381
  24.9 12.2 %collective-permute-start.14 = (bf16[192,768]{1,0:T(8,128)(2,1)S(1)}, bf16[192,768]{1,0:T(8,128)(2,1)S(1)}, u32[]{:S(2)}, u32[]{:S(2)}) collective-permute-start(bf16[192,768]{1,0:T(8,128)(2,1)S(1)} %collective-permute-done.9.refs_6_), channel_id=1, source_target_pairs={{8,0},{9,1},{10,2},{11,3},{12,4},{13,5},{14,6},{15,7},{0,8},{1,9},... | collective-permute-start | bytes 884744 | tf_op jit(solution)/shard_map/ppermute | solution.py:381
  26.7 11.5 %collective-permute-start.12 = (bf16[192,768]{1,0:T(8,128)(2,1)S(1)}, bf16[192,768]{1,0:T(8,128)(2,1)S(1)}, u32[]{:S(2)}, u32[]{:S(2)}) collective-permute-start(bf16[192,768]{1,0:T(8,128)(2,1)S(1)} %collective-permute-done.9.refs_6_), channel_id=1, source_target_pairs={{2,0},{7,1},{4,2},{1,3},{6,4},{3,5},{0,6},{5,7},{10,8},{15,9},{12,... | collective-permute-start | bytes 884744 | tf_op jit(solution)/shard_map/ppermute | solution.py:381
  28.5 9.7 %collective-permute-start.13 = (bf16[192,768]{1,0:T(8,128)(2,1)S(1)}, bf16[192,768]{1,0:T(8,128)(2,1)S(1)}, u32[]{:S(2)}, u32[]{:S(2)}) collective-permute-start(bf16[192,768]{1,0:T(8,128)(2,1)S(1)} %collective-permute-done.11.refs_8_), channel_id=1, source_target_pairs={{6,0},{3,1},{0,2},{5,3},{2,4},{7,5},{4,6},{1,7},{14,8},{11,9},{8,1... | collective-permute-start | bytes 884744 | tf_op jit(solution)/shard_map/ppermute | solution.py:381
  32.7 11.2 %copy-start.7 = (s32[96,3]{0,1:T(4,128)S(1)}, s32[96,3]{0,1:T(4,128)}, u32[]{:S(2)}) copy-start(s32[96,3]{0,1:T(4,128)} %param.9) | copy-start | bytes 3460
  32.7 8.5 %collective-permute-start.15 = (bf16[192,768]{1,0:T(8,128)(2,1)S(1)}, bf16[192,768]{1,0:T(8,128)(2,1)S(1)}, u32[]{:S(2)}, u32[]{:S(2)}) collective-permute-start(bf16[192,768]{1,0:T(8,128)(2,1)S(1)} %collective-permute-done.8.refs_5_), channel_id=1, source_target_pairs={{2,0},{7,1},{4,2},{1,3},{6,4},{3,5},{0,6},{5,7},{10,8},{15,9},{12,... | collective-permute-start | bytes 884744 | tf_op jit(solution)/shard_map/ppermute | solution.py:381
  37.1 6.7 %collective-permute-start.16 = (bf16[192,768]{1,0:T(8,128)(2,1)S(1)}, bf16[192,768]{1,0:T(8,128)(2,1)S(1)}, u32[]{:S(2)}, u32[]{:S(2)}) collective-permute-start(bf16[192,768]{1,0:T(8,128)(2,1)S(1)} %collective-permute-done.14.refs_8_), channel_id=1, source_target_pairs={{2,0},{7,1},{4,2},{1,3},{6,4},{3,5},{0,6},{5,7},{10,8},{15,9},{12,... | collective-permute-start | bytes 884744 | tf_op jit(solution)/shard_map/ppermute | solution.py:381
  49.6 5.5 %copy-start.9 = (f32[192,768]{1,0:T(8,128)S(1)}, f32[192,768]{1,0:T(8,128)}, u32[]{:S(2)}) copy-start(f32[192,768]{1,0:T(8,128)} %get-tuple-element.57) | copy-start | bytes 1769476
  49.6 7.6 %copy-start.2 = (f32[192,768]{1,0:T(8,128)S(1)}, f32[192,768]{1,0:T(8,128)}, u32[]{:S(2)}) copy-start(f32[192,768]{1,0:T(8,128)} %get-tuple-element.56.mine) | copy-start | bytes 1769476
  49.6 7.6 %copy-start.8 = (f32[1,2]{1,0:T(1,128)S(1)}, f32[1,2]{1,0:T(1,128)}, u32[]{:S(2)}) copy-start(f32[1,2]{1,0:T(1,128)} %weights.3) | copy-start | bytes 28
  49.7 26.1 %all-to-all-start = ((f32[16,32,768]{2,1,0:T(8,128)}), f32[16,32,768]{2,1,0:T(8,128)S(1)}, u32[]{:S(2)}, u32[]{:S(2)}) async-start(f32[16,32,768]{2,1,0:T(8,128)} %get-tuple-element.59), calls=%async_computation | async-start | bytes 3145728 | tf_op jit(solution)/shard_map/all_to_all | solution.py:470
  55.1 24.1 %copy-start.3 = (f32[1,2,3,32,512]{4,3,2,1,0:T(8,128)S(1)}, f32[1,2,3,32,512]{4,3,2,1,0:T(8,128)}, u32[]{:S(2)}) copy-start(f32[1,2,3,32,512]{4,3,2,1,0:T(8,128)} %param.8) | copy-start | bytes 1179652
  55.1 2.1 %collective-permute-start.17 = (f32[192,768]{1,0:T(8,128)S(1)}, f32[192,768]{1,0:T(8,128)S(1)}, u32[]{:S(2)}, u32[]{:S(2)}) collective-permute-start(f32[192,768]{1,0:T(8,128)S(1)} %copy-done.9), channel_id=1, source_target_pairs={{1,0},{0,1},{3,2},{2,3},{5,4},{4,5},{7,6},{6,7},{9,8},{8,9},{11,10... | collective-permute-start | bytes 1769480 | tf_op jit(solution)/shard_map/ppermute | solution.py:381
  59.1 9.9 %collective-permute-start.18 = (f32[96,768]{1,0:T(8,128)S(1)}, f32[96,768]{1,0:T(8,128)S(1)}, u32[]{:S(2)}, u32[]{:S(2)}) collective-permute-start(f32[96,768]{1,0:T(8,128)S(1)} %get-tuple-element.61), channel_id=1, source_target_pairs={{32,0},{48,16},{0,32},{16,48},{96,64},{112,80},{64,96},{80,112},{1... | collective-permute-start | bytes 884744 | tf_op jit(solution)/shard_map/ppermute | solution.py:478
  69.1 10.0 %collective-permute-start.19 = (f32[48,768]{1,0:T(8,128)S(1)}, f32[48,768]{1,0:T(8,128)S(1)}, u32[]{:S(2)}, u32[]{:S(2)}) collective-permute-start(f32[48,768]{1,0:T(8,128)S(1)} %get-tuple-element.65), channel_id=1, source_target_pairs={{64,0},{80,16},{96,32},{112,48},{0,64},{16,80},{32,96},{48,112},{1... | collective-permute-start | bytes 442376 | tf_op jit(solution)/shard_map/ppermute | solution.py:486

commit v4 on v3

--- a/solution.py
+++ b/solution.py
@@ -31,6 +31,7 @@
 CORE = grid_perm(lambda y, x, c: (y, x, 1 - c))
 FROM_AHEAD = grid_perm(lambda y, x, c: (y, x + 1 - 2 * c, c))
 FROM_BEHIND = grid_perm(lambda y, x, c: (y, x - 1 + 2 * c, c))
+FROM_FAR = grid_perm(lambda y, x, c: (y, x + 2, c))
 FROM_Y = grid_perm(lambda y, x, c: (1 - y, x, c))
 
 
@@ -76,7 +77,7 @@
 
 
 def call(body, outs, ins, name, flops=0, scratch=(), limit=16, out_space=pltpu.VMEM):
-    spaces = {"s": pltpu.SMEM, "v": pltpu.VMEM, "h": pltpu.HBM}
+    spaces = {"s": pltpu.SMEM, "v": pltpu.VMEM, "h": pltpu.HBM, "p": pltpu.HBM}
     size = sum(a.size * a.dtype.itemsize for a, _ in ins) + sum(
         o.size * o.dtype.itemsize for o in outs
     )
@@ -91,14 +92,20 @@
         compiler_params=pltpu.CompilerParams(vmem_limit_bytes=limit * 1024 * 1024),
         cost_estimate=pl.CostEstimate(flops=flops, bytes_accessed=size, transcendentals=0),
         name=name,
-    )(*[a for a, _ in ins])
+    )(*[pltpu.with_memory_space_constraint(a, pltpu.HBM) if kind == "p" else a for a, kind in ins])
 
 
 def sds(shape, dtype):
     return jax.ShapeDtypeStruct(shape, dtype)
 
 
-def prep_kernel(structure, widths, f, keep, send):
+def prep_kernel(structure_in, widths_in, f_in, keep, send, structure, widths, f, sems):
+    pairs = ((widths_in, widths), (structure_in, structure), (f_in, f))
+    copies = [pltpu.make_async_copy(v, to, sems.at[i]) for i, (v, to) in enumerate(pairs)]
+    for copy in copies:
+        copy.start()
+    for copy in copies:
+        copy.wait()
     g, c, _, _ = place()
     kb, k1, k2, a = supers(widths)
     base = g * 6
@@ -271,39 +278,48 @@
         copy.wait()
 
 
-def spread_kernel(widths, weights, mine, other, out, keep, send, wide):
+def halves_of(mine, other):
+    return [
+        [(ref[:, p * HC : p * HC + HB], ref[:, p * HC + HB : (p + 1) * HC]) for p in range(2)]
+        for ref in (mine, other)
+    ]
+
+
+def in_order(c, first, second):
+    return jnp.concatenate([jnp.where(c == 0, first, second), jnp.where(c == 0, second, first)], axis=1)
+
+
+def term_kernel(weights, mine, other, keep, send, wide):
     _, c, _, _ = place()
     odd, _ = z_bits()
+    wr, wi = weights[0, 0], weights[0, 1]
+    m, t = ([wr * half[1][i] + wi * half[0][i] for i in range(2)] for half in halves_of(mine, other))
+    wide[:, :BIG] = in_order(c, m[0], t[0])
+    wide[:, BIG:] = in_order(c, m[1], t[1])
+    keep[...] = wide[rows_at(odd, 96), :]
+    send[...] = wide[rows_at(1 - odd, 96), :]
+
+
+def spread_kernel(widths, mine, other, out):
+    _, c, _, _ = place()
     kb, k1, k2, a = supers(widths)
-    wr, wi = weights[0, 0], weights[0, 1]
     back = (iota((HB, HB), 0) == iota((HB, HB), 1) + a).astype(BF16)
     lane = iota((ROWS, HB), 1)
-    halves = []
-    for ref in (mine, other):
-        halves.append([(ref[:, p * HC : p * HC + HB], ref[:, p * HC + HB : (p + 1) * HC]) for p in range(2)])
 
     def at(k, part):
         return pl.ds(pl.multiple_of(k * BIG + part * HB, HB), HB)
 
     zero = jnp.zeros((ROWS, HB), BF16)
-    small = []
+    halves = halves_of(mine, other)
     for p in range(2):
         m, t = halves[0][p], halves[1][p]
         out[p, :, at(kb, c)] = m[0].astype(BF16)
         out[p, :, at(kb, 1 - c)] = t[0].astype(BF16)
-        low, high = jnp.where(c == 0, m[1], t[1]), jnp.where(c == 0, t[1], m[1])
-        s = jnp.concatenate([low, high], axis=1)
-        sb = s.astype(BF16)
+        s = in_order(c, m[1], t[1])
         out[p, :, at(k1, 0)] = jnp.where(lane < a, s, 0.0).astype(BF16)
         out[p, :, at(k1, 1)] = zero
-        out[p, :, at(k2, 0)] = jnp.dot(sb, back, preferred_element_type=F32).astype(BF16)
+        out[p, :, at(k2, 0)] = jnp.dot(s.astype(BF16), back, preferred_element_type=F32).astype(BF16)
         out[p, :, at(k2, 1)] = zero
-        small.append(s)
-    for i, part in ((0, c), (1, 1 - c)):
-        wide[:, at(0, part)] = wr * halves[i][1][0] + wi * halves[i][0][0]
-    wide[:, BIG:] = wr * small[1] + wi * small[0]
-    keep[...] = wide[rows_at(odd, 96), :]
-    send[...] = wide[rows_at(1 - odd, 96), :]
 
 
 def second_kernel(old, got, keep, send, total):
@@ -384,15 +400,21 @@
     keep, send = call(
         prep_kernel,
         [block, block],
-        [(structure, "s"), (widths, "s"), (factor_cols[0], "v")],
+        [(structure, "p"), (widths, "p"), (factor_cols[0], "p")],
         "prep",
         flops=2 * 2 * ROWS * HB * HB,
+        scratch=[
+            pltpu.SMEM(structure.shape, jnp.int32),
+            pltpu.SMEM(widths.shape, jnp.int32),
+            pltpu.VMEM(factor_cols.shape[1:], BF16),
+            pltpu.SemaphoreType.DMA((3,)),
+        ],
     )
     a_own = ancestor_inverse[0].reshape(2 * ROWS, -1)
     a_sib = over_grid(a_own, CORE)
-    keep, send, a_sib = lax.optimization_barrier((keep, send, a_sib))
-    got_mine, got_theirs = over_grid(send, CORE), over_grid(keep, CORE)
-    got_mine, got_theirs = lax.optimization_barrier((got_mine, got_theirs))
+    got_mine = over_grid(send, CORE)
+    got_mine, a_sib = lax.optimization_barrier((got_mine, a_sib))
+    got_theirs = over_grid(keep, CORE)
 
     def first(v):
         return [over_grid(v, perm) for perm in (FROM_AHEAD, FROM_BEHIND, FROM_Y)]
@@ -431,9 +453,9 @@
     *u1, acc, big, small = lax.optimization_barrier((*u1, acc, big, small))
     u2 = second(*u1)
     acc = add(acc, [(1, 0), (-1, 0), (0, 1)], u1, v1)
-    v3 = over_grid(v2[2], FROM_AHEAD)
+    v3 = over_grid(v2[0], FROM_Y)
     *u2, acc = lax.optimization_barrier((*u2, acc))
-    u3 = over_grid(u2[2], FROM_AHEAD)
+    u3 = over_grid(u2[1], FROM_BEHIND)
     acc = add(acc, [(2, 0), (-1, 1), (1, 1)], u2, v2)
     own, sib, q = call(
         column_kernel,
@@ -468,14 +490,21 @@
     )
     other = over_grid(sib, CORE)
     sums = lax.all_to_all(q, "grid", 0, 0, tiled=True)
-    column_inverse, d_keep, d_send = call(
+    d_keep, d_send = call(
+        term_kernel,
+        [sds((96, 768), F32)] * 2,
+        [(pole_weights, "s"), (own, "v"), (other, "v")],
+        "term",
+        scratch=[pltpu.VMEM((ROWS, 768), F32)],
+    )
+    d_got = lax.ppermute(d_send, "pole", z_pair(1))
+    column_inverse = call(
         spread_kernel,
-        [sds((2, ROWS, 3 * BIG), BF16)] + [sds((96, 768), F32)] * 2,
-        [(widths, "s"), (pole_weights, "s"), (own, "v"), (other, "v")],
+        [sds((2, ROWS, 3 * BIG), BF16)],
+        [(widths, "s"), (own, "v"), (other, "v")],
         "spread",
-        scratch=[pltpu.VMEM((ROWS, 768), F32)],
-    )
-    d_got = lax.ppermute(d_send, "pole", z_pair(1))
+    )[0]
+    d_got, column_inverse = lax.optimization_barrier((d_got, column_inverse))
     d_keep, d_send = call(
         second_kernel,
         [sds((48, 768), F32)] * 2,

time: 110 us -> 105 us (0.955)
  local copies, waits for them, and re-layouts: 2.63 us -> 0.04 us
  waiting for transfers between devices: 27.3 us -> 24.8 us
  Pallas kernels: 18.8 us -> 20.3 us
  starting transfers between devices: 31.9 us -> 30.5 us
    unnamed x20 -> x14, local copies, waits for them, and re-layouts: 2.63 us -> 0.04 us
    ppermute x1, waiting for transfers between devices: 3.37 us -> 1.41 us  [local(): d_got = lax.ppermute(d_send, 'pole', z_pair(2))]
    all_to_all x1, waiting for transfers between devices: 3.32 us -> 5.27 us  [local(): sums = lax.all_to_all(q, 'grid', 0, 0, tiled=True)]
    ppermute x1, waiting for transfers between devices: 7.32 us -> 5.49 us  [local(): d_got = lax.ppermute(d_send, 'pole', z_pair(1))]
    pallas_call x10 -> x11, Pallas kernels: 18.8 us -> 20.3 us  [call(): pl.pallas_call(body, out_shape=tuple(outs), in_specs=[pl.BlockSpec(memory...]
  transfers between devices with their start and end apart: 21 -> 21, of which waited for: 11 -> 11; matrix products, arithmetic and copies ran while one was open for 0% -> 0% of each run, Pallas kernels for 10% -> 12%
where the time goes in v4:
time: 105 us; the launch traced here: 104 us
  starting transfers between devices  30.5 us (29%)
  blocking collectives  27.7 us (26%)
  waiting for transfers between devices  24.8 us (24%)
  Pallas kernels  20.3 us (19%)
    all_to_all x1, blocking collectives, local(): pays = lax.all_to_all(pay, 'pole', 0, 0, tiled=True)  27.7 us
    pallas_call x11, Pallas kernels, call(): pl.pallas_call(body, out_shape=tuple(outs), in_specs=[pl.BlockSpec(memory...  20.3 us
    ppermute x18, starting transfers between devices, over_grid(): return lax.ppermute(v, 'grid', perm)  19.8 us
    ppermute x18, waiting for transfers between devices, over_grid(): return lax.ppermute(v, 'grid', perm)  12.6 us
    ppermute x1, waiting for transfers between devices, local(): d_got = lax.ppermute(d_send, 'pole', z_pair(1))  5.49 us
    all_to_all x1, starting transfers between devices, local(): sums = lax.all_to_all(q, 'grid', 0, 0, tiled=True)  5.43 us
    all_to_all x1, waiting for transfers between devices, local(): sums = lax.all_to_all(q, 'grid', 0, 0, tiled=True)  5.27 us
    ppermute x1, starting transfers between devices, local(): d_got = lax.ppermute(d_send, 'pole', z_pair(2))  3.35 us
  transfers between devices with their start and end apart: 21, of which 11 were waited for; matrix products, arithmetic and copies ran while one was open for 0% of the time, Pallas kernels for 12%

profile of v4, /device:TPU:8, one launch (start us, length us, event | category | flops | bytes accessed | tf_op | source)
XLA Modules:
  0.0 104.1 jit_solution(16795403093613890252)
XLA Ops:
  0.8 1.7 %prep.1 = (bf16[192,768]{1,0:T(8,128)(2,1)S(1)}, bf16[192,768]{1,0:T(8,128)(2,1)S(1)}) custom-call(s32[3,96]{1,0:T(4,128)} %bitcast.12, s32[3]{0:T(128)} %widths.7, bf16[2,192,1536]{2,1,0:T(8,128)(2,1)} %bitcast.15), custom_call_target="tpu_custom_call" | custom-call | flops 50331648 | bytes 1770636 | tf_op jit(solution)/shard_map/prep/pallas_call | solution.py:86
  3.1 2.8 %collective-permute-start = (bf16[192,768]{1,0:T(8,128)(2,1)S(1)}, bf16[192,768]{1,0:T(8,128)(2,1)S(1)}, u32[]{:S(2)}, u32[]{:S(2)}) collective-permute-start(bf16[192,768]{1,0:T(8,128)(2,1)S(1)} %get-tuple-element.35.refs_2_.keep), channel_id=1, source_target_pairs={{2,0},{7,1},{4,2},{1,3},{6,4},{3,5},{0,6},{5,7},{10,8},{15,9},{12,... | collective-permute-start | bytes 884744 | tf_op jit(solution)/shard_map/ppermute | solution.py:397
  5.9 2.0 %collective-permute-start.2 = (bf16[192,768]{1,0:T(8,128)(2,1)S(1)}, bf16[192,768]{1,0:T(8,128)(2,1)S(1)}, u32[]{:S(2)}, u32[]{:S(2)}) collective-permute-start(bf16[192,768]{1,0:T(8,128)(2,1)S(1)} %get-tuple-element.35.refs_2_.keep), channel_id=1, source_target_pairs={{8,0},{9,1},{10,2},{11,3},{12,4},{13,5},{14,6},{15,7},{0,8},{1,9},... | collective-permute-start | bytes 884744 | tf_op jit(solution)/shard_map/ppermute | solution.py:397
  7.9 1.7 %collective-permute-start.9 = (bf16[192,768]{1,0:T(8,128)(2,1)S(1)}, bf16[192,768]{1,0:T(8,128)(2,1)S(1)}, u32[]{:S(2)}, u32[]{:S(2)}) collective-permute-start(bf16[192,768]{1,0:T(8,128)(2,1)S(1)} %collective-permute-done.3.refs_3_.got_mine), channel_id=1, source_target_pairs={{2,0},{7,1},{4,2},{1,3},{6,4},{3,5},{0,6},{5,7},{10,8},{15,9},{12,... | collective-permute-start | bytes 884744 | tf_op jit(solution)/shard_map/ppermute | solution.py:397
  9.6 1.6 %collective-permute-start.11 = (bf16[192,768]{1,0:T(8,128)(2,1)S(1)}, bf16[192,768]{1,0:T(8,128)(2,1)S(1)}, u32[]{:S(2)}, u32[]{:S(2)}) collective-permute-start(bf16[192,768]{1,0:T(8,128)(2,1)S(1)} %collective-permute-done.3.refs_3_.got_mine), channel_id=1, source_target_pairs={{8,0},{9,1},{10,2},{11,3},{12,4},{13,5},{14,6},{15,7},{0,8},{1,9},... | collective-permute-start | bytes 884744 | tf_op jit(solution)/shard_map/ppermute | solution.py:397
  11.2 1.1 %left.1 = (bf16[1024,384]{1,0:T(8,128)(2,1)S(1)}, bf16[1024,384]{1,0:T(8,128)(2,1)S(1)}) custom-call(s32[3]{0:T(128)S(1)} %copy-done.3, bf16[192,768]{1,0:T(8,128)(2,1)S(1)} %get-tuple-element.35.refs_2_.keep, bf16[192,768]{1,0:T(8,128)(2,1)S(1)} %get-tuple-element.36.send, bf16[192,768]{1,0:T(8,128)(2,1)S(1)} %collective-permute-done.3.refs_3_.got_mine, ...), custom_call_target="tpu_custom_call" | custom-call | flops 100663296 | bytes 2752524 | tf_op jit(solution)/shard_map/left/pallas_call | solution.py:86
  12.2 1.0 product.3.refs_0_
  13.9 1.8 %collective-permute-done.1.refs_4_ = bf16[192,768]{1,0:T(8,128)(2,1)S(1)} collective-permute-done((bf16[192,768]{1,0:T(8,128)(2,1)S(1)}, bf16[192,768]{1,0:T(8,128)(2,1)S(1)}, u32[]{:S(2)}, u32[]{:S(2)}) %collective-permute-start.1) | collective-permute-done | bytes 294944 | tf_op jit(solution)/shard_map/ppermute | solution.py:397
  15.8 3.3 %collective-permute-start.6 = (bf16[192,768]{1,0:T(8,128)(2,1)S(1)}, bf16[192,768]{1,0:T(8,128)(2,1)S(1)}, u32[]{:S(2)}, u32[]{:S(2)}) collective-permute-start(bf16[192,768]{1,0:T(8,128)(2,1)S(1)} %collective-permute-done.refs_3_), channel_id=1, source_target_pairs={{2,0},{7,1},{4,2},{1,3},{6,4},{3,5},{0,6},{5,7},{10,8},{15,9},{12,... | collective-permute-start | bytes 884744 | tf_op jit(solution)/shard_map/ppermute | solution.py:397
  19.1 0.6 collective-permute-start.8
  19.7 2.4 %collective-permute-done.11.refs_8_ = bf16[192,768]{1,0:T(8,128)(2,1)S(1)} collective-permute-done((bf16[192,768]{1,0:T(8,128)(2,1)S(1)}, bf16[192,768]{1,0:T(8,128)(2,1)S(1)}, u32[]{:S(2)}, u32[]{:S(2)}) %collective-permute-start.11) | collective-permute-done | bytes 294944 | tf_op jit(solution)/shard_map/ppermute | solution.py:397
  22.1 3.3 %collective-permute-start.12 = (bf16[192,768]{1,0:T(8,128)(2,1)S(1)}, bf16[192,768]{1,0:T(8,128)(2,1)S(1)}, u32[]{:S(2)}, u32[]{:S(2)}) collective-permute-start(bf16[192,768]{1,0:T(8,128)(2,1)S(1)} %collective-permute-done.9.refs_6_), channel_id=1, source_target_pairs={{2,0},{7,1},{4,2},{1,3},{6,4},{3,5},{0,6},{5,7},{10,8},{15,9},{12,... | collective-permute-start | bytes 884744 | tf_op jit(solution)/shard_map/ppermute | solution.py:397
  25.6 1.3 %collective-permute-start.13 = (bf16[192,768]{1,0:T(8,128)(2,1)S(1)}, bf16[192,768]{1,0:T(8,128)(2,1)S(1)}, u32[]{:S(2)}, u32[]{:S(2)}) collective-permute-start(bf16[192,768]{1,0:T(8,128)(2,1)S(1)} %collective-permute-done.11.refs_8_), channel_id=1, source_target_pairs={{6,0},{3,1},{0,2},{5,3},{2,4},{7,5},{4,6},{1,7},{14,8},{11,9},{8,1... | collective-permute-start | bytes 884744 | tf_op jit(solution)/shard_map/ppermute | solution.py:397
  27.0 3.0 %product.4.refs_0_ = f32[2,192,768]{2,1,0:T(8,128)S(1)} custom-call(f32[2,192,768]{2,1,0:T(8,128)S(1)} %product.3.refs_0_, bf16[384,3072]{1,0:T(8,128)(2,1)S(1)} %bitcast.8, bf16[384,3072]{1,0:T(8,128)(2,1)S(1)} %collective-permute-done.4.refs_1_.refs_2_.a_sib, bf16[192,768]{1,0:T(8,128)(2,1)S(1)} %collective-permute-done.refs_3_, ...), custom_call_target="tpu_custom_call" | custom-call | flops 1358954496 | bytes 8847360 | tf_op jit(solution)/shard_map/product/pallas_call | solution.py:86
  30.0 1.6 %collective-permute-start.15 = (bf16[192,768]{1,0:T(8,128)(2,1)S(1)}, bf16[192,768]{1,0:T(8,128)(2,1)S(1)}, u32[]{:S(2)}, u32[]{:S(2)}) collective-permute-start(bf16[192,768]{1,0:T(8,128)(2,1)S(1)} %collective-permute-done.7.refs_4_), channel_id=1, source_target_pairs={{6,0},{3,1},{0,2},{5,3},{2,4},{7,5},{4,6},{1,7},{14,8},{11,9},{8,1... | collective-permute-start | bytes 884744 | tf_op jit(solution)/shard_map/ppermute | solution.py:397
  31.6 1.2 %collective-permute-done.12.refs_6_ = bf16[192,768]{1,0:T(8,128)(2,1)S(1)} collective-permute-done((bf16[192,768]{1,0:T(8,128)(2,1)S(1)}, bf16[192,768]{1,0:T(8,128)(2,1)S(1)}, u32[]{:S(2)}, u32[]{:S(2)}) %collective-permute-start.12) | collective-permute-done | bytes 294944 | tf_op jit(solution)/shard_map/ppermute | solution.py:397
  32.8 2.6 %collective-permute-done.14.refs_8_ = bf16[192,768]{1,0:T(8,128)(2,1)S(1)} collective-permute-done((bf16[192,768]{1,0:T(8,128)(2,1)S(1)}, bf16[192,768]{1,0:T(8,128)(2,1)S(1)}, u32[]{:S(2)}, u32[]{:S(2)}) %collective-permute-start.14) | collective-permute-done | bytes 294944 | tf_op jit(solution)/shard_map/ppermute | solution.py:397
  35.3 3.0 %product.5.old = f32[2,192,768]{2,1,0:T(8,128)S(1)} custom-call(f32[2,192,768]{2,1,0:T(8,128)S(1)} %product.4.refs_0_, bf16[384,3072]{1,0:T(8,128)(2,1)S(1)} %bitcast.9, bf16[384,3072]{1,0:T(8,128)(2,1)S(1)} %collective-permute-done.4.refs_1_.refs_2_.a_sib, bf16[192,768]{1,0:T(8,128)(2,1)S(1)} %collective-permute-done.6.refs_3_, ...), custom_call_target="tpu_custom_call" | custom-call | flops 1358954496 | bytes 8847360 | tf_op jit(solution)/shard_map/product/pallas_call | solution.py:86
  38.3 2.5 %collective-permute-done.16.v = bf16[192,768]{1,0:T(8,128)(2,1)S(1)} collective-permute-done((bf16[192,768]{1,0:T(8,128)(2,1)S(1)}, bf16[192,768]{1,0:T(8,128)(2,1)S(1)}, u32[]{:S(2)}, u32[]{:S(2)}) %collective-permute-start.16) | collective-permute-done | bytes 294944 | tf_op jit(solution)/shard_map/ppermute | solution.py:397
  40.8 5.8 %column.1 = (f32[192,768]{1,0:T(8,128)}, f32[192,768]{1,0:T(8,128)}, f32[16,32,768]{2,1,0:T(8,128)}) custom-call(s32[3,96]{1,0:T(4,128)S(1)} %bitcast.13, s32[3]{0:T(128)S(1)} %copy-done.3, f32[2,192,768]{2,1,0:T(8,128)S(1)} %product.5.old, bf16[384,3072]{1,0:T(8,128)(2,1)S(1)} %bitcast.10, ...), custom_call_target="tpu_custom_call" | custom-call | flops 1660944384 | bytes 10814604 | tf_op jit(solution)/shard_map/column/pallas_call | solution.py:86
  46.7 5.4 %all-to-all-start = ((f32[16,32,768]{2,1,0:T(8,128)}), f32[16,32,768]{2,1,0:T(8,128)S(1)}, u32[]{:S(2)}, u32[]{:S(2)}) async-start(f32[16,32,768]{2,1,0:T(8,128)} %get-tuple-element.55), calls=%async_computation | async-start | bytes 3145728 | tf_op jit(solution)/shard_map/all_to_all | solution.py:492
  52.3 1.9 %collective-permute-done.17.other = f32[192,768]{1,0:T(8,128)S(1)} collective-permute-done((f32[192,768]{1,0:T(8,128)S(1)}, f32[192,768]{1,0:T(8,128)S(1)}, u32[]{:S(2)}, u32[]{:S(2)}) %collective-permute-start.17) | collective-permute-done | bytes 589856 | tf_op jit(solution)/shard_map/ppermute | solution.py:397
  54.2 0.7 term.1
  54.9 1.9 %collective-permute-start.18 = (f32[96,768]{1,0:T(8,128)S(1)}, f32[96,768]{1,0:T(8,128)S(1)}, u32[]{:S(2)}, u32[]{:S(2)}) collective-permute-start(f32[96,768]{1,0:T(8,128)S(1)} %get-tuple-element.53), channel_id=1, source_target_pairs={{32,0},{48,16},{0,32},{16,48},{96,64},{112,80},{64,96},{80,112},{1... | collective-permute-start | bytes 884744 | tf_op jit(solution)/shard_map/ppermute | solution.py:500
  56.8 1.8 %spread.1 = bf16[2,192,1536]{2,1,0:T(8,128)(2,1)} custom-call(s32[3]{0:T(128)S(1)} %copy-done.3, f32[192,768]{1,0:T(8,128)S(1)} %copy-done.1, f32[192,768]{1,0:T(8,128)S(1)} %collective-permute-done.17.other), custom_call_target="tpu_custom_call" | custom-call | bytes 2359308 | tf_op jit(solution)/shard_map/spread/pallas_call | solution.py:86
  58.6 5.5 %collective-permute-done.18.got = f32[96,768]{1,0:T(8,128)S(1)} collective-permute-done((f32[96,768]{1,0:T(8,128)S(1)}, f32[96,768]{1,0:T(8,128)S(1)}, u32[]{:S(2)}, u32[]{:S(2)}) %collective-permute-start.18) | collective-permute-done | bytes 294944 | tf_op jit(solution)/shard_map/ppermute | solution.py:500
  64.2 3.3 %collective-permute-start.19 = (f32[48,768]{1,0:T(8,128)S(1)}, f32[48,768]{1,0:T(8,128)S(1)}, u32[]{:S(2)}, u32[]{:S(2)}) collective-permute-start(f32[48,768]{1,0:T(8,128)S(1)} %get-tuple-element.61), channel_id=1, source_target_pairs={{64,0},{80,16},{96,32},{112,48},{0,64},{16,80},{32,96},{48,112},{1... | collective-permute-start | bytes 442376 | tf_op jit(solution)/shard_map/ppermute | solution.py:515
  67.5 5.3 %all-to-all-done.sums = f32[16,32,768]{2,1,0:T(8,128)S(1)} async-done(((f32[16,32,768]{2,1,0:T(8,128)}), f32[16,32,768]{2,1,0:T(8,128)S(1)}, u32[]{:S(2)}, u32[]{:S(2)}) %all-to-all-start) | async-done | bytes 1572896 | tf_op jit(solution)/shard_map/all_to_all | solution.py:492
  72.8 1.4 %collective-permute-done.19.got = f32[48,768]{1,0:T(8,128)S(1)} collective-permute-done((f32[48,768]{1,0:T(8,128)S(1)}, f32[48,768]{1,0:T(8,128)S(1)}, u32[]{:S(2)}, u32[]{:S(2)}) %collective-permute-start.19) | collective-permute-done | bytes 147488 | tf_op jit(solution)/shard_map/ppermute | solution.py:515
  74.2 1.5 %pivot.1 = (f32[2,3,32,512]{3,2,1,0:T(8,128)}, f32[16,16,512]{2,1,0:T(8,128)S(1)}) custom-call(s32[3]{0:T(128)S(1)} %copy-done.3, f32[1,2]{1,0:T(1,128)S(1)} %copy-done.5, f32[2,3,32,512]{3,2,1,0:T(8,128)S(1)} %bitcast.11, f32[16,32,768]{2,1,0:T(8,128)S(1)} %all-to-all-done.sums, f32[48,768]{1,0:T(8,128)S(1)} %get-tuple-element.60.keep, ...), custom_call_target="tpu_custom_call" | custom-call | bytes 3178516 | tf_op jit(solution)/shard_map/pivot/pallas_call | solution.py:86
  75.7 27.7 %all_to_all.10.pays = f32[16,16,512]{2,1,0:T(8,128)S(1)} all-to-all(f32[16,16,512]{2,1,0:T(8,128)S(1)} %get-tuple-element.63), channel_id=1, replica_groups=mesh['pole'=16,'grid'=16] {'pole'}, dimensions={0} | all-to-all | bytes 1048576 | tf_op jit(solution)/shard_map/all_to_all | solution.py:531
  103.4 0.8 density.1
  (36 shorter events, 2.1 us)
Async XLA Ops:
  0.6 10.5 %copy-start.3 = (s32[3]{0:T(128)S(1)}, s32[3]{0:T(128)}, u32[]{:S(2)}) copy-start(s32[3]{0:T(128)} %widths.7) | copy-start | bytes 40
  0.6 7.2 %collective-permute-start.4 = (bf16[384,3072]{1,0:T(8,128)(2,1)}, bf16[384,3072]{1,0:T(8,128)(2,1)S(1)}, u32[]{:S(2)}, u32[]{:S(2)}) collective-permute-start(bf16[384,3072]{1,0:T(8,128)(2,1)} %bitcast.6), channel_id=1, source_target_pairs={{1,0},{0,1},{3,2},{2,3},{5,4},{4,5},{7,6},{6,7},{9,8},{8,9},{11,10... | collective-permute-start | bytes 7077896 | tf_op jit(solution)/shard_map/ppermute | solution.py:397
  0.7 11.5 %copy-start = (bf16[1,2,192,3072]{3,2,1,0:T(8,128)(2,1)S(1)}, bf16[1,2,192,3072]{3,2,1,0:T(8,128)(2,1)}, u32[]{:S(2)}) copy-start(bf16[1,2,192,3072]{3,2,1,0:T(8,128)(2,1)} %param.7) | copy-start | bytes 7077892
  2.4 3.4 %collective-permute-start.3 = (bf16[192,768]{1,0:T(8,128)(2,1)S(1)}, bf16[192,768]{1,0:T(8,128)(2,1)S(1)}, u32[]{:S(2)}, u32[]{:S(2)}) collective-permute-start(bf16[192,768]{1,0:T(8,128)(2,1)S(1)} %get-tuple-element.36.send), channel_id=1, source_target_pairs={{1,0},{0,1},{3,2},{2,3},{5,4},{4,5},{7,6},{6,7},{9,8},{8,9},{11,10... | collective-permute-start | bytes 884744 | tf_op jit(solution)/shard_map/ppermute | solution.py:397
  3.0 6.6 %collective-permute-start.5 = (bf16[192,768]{1,0:T(8,128)(2,1)S(1)}, bf16[192,768]{1,0:T(8,128)(2,1)S(1)}, u32[]{:S(2)}, u32[]{:S(2)}) collective-permute-start(bf16[192,768]{1,0:T(8,128)(2,1)S(1)} %get-tuple-element.35.refs_2_.keep), channel_id=1, source_target_pairs={{1,0},{0,1},{3,2},{2,3},{5,4},{4,5},{7,6},{6,7},{9,8},{8,9},{11,10... | collective-permute-start | bytes 884744 | tf_op jit(solution)/shard_map/ppermute | solution.py:397
  3.1 10.2 %collective-permute-start = (bf16[192,768]{1,0:T(8,128)(2,1)S(1)}, bf16[192,768]{1,0:T(8,128)(2,1)S(1)}, u32[]{:S(2)}, u32[]{:S(2)}) collective-permute-start(bf16[192,768]{1,0:T(8,128)(2,1)S(1)} %get-tuple-element.35.refs_2_.keep), channel_id=1, source_target_pairs={{2,0},{7,1},{4,2},{1,3},{6,4},{3,5},{0,6},{5,7},{10,8},{15,9},{12,... | collective-permute-start | bytes 884744 | tf_op jit(solution)/shard_map/ppermute | solution.py:397
  5.9 9.8 %collective-permute-start.1 = (bf16[192,768]{1,0:T(8,128)(2,1)S(1)}, bf16[192,768]{1,0:T(8,128)(2,1)S(1)}, u32[]{:S(2)}, u32[]{:S(2)}) collective-permute-start(bf16[192,768]{1,0:T(8,128)(2,1)S(1)} %get-tuple-element.35.refs_2_.keep), channel_id=1, source_target_pairs={{6,0},{3,1},{0,2},{5,3},{2,4},{7,5},{4,6},{1,7},{14,8},{11,9},{8,1... | collective-permute-start | bytes 884744 | tf_op jit(solution)/shard_map/ppermute | solution.py:397
  5.9 9.9 %collective-permute-start.2 = (bf16[192,768]{1,0:T(8,128)(2,1)S(1)}, bf16[192,768]{1,0:T(8,128)(2,1)S(1)}, u32[]{:S(2)}, u32[]{:S(2)}) collective-permute-start(bf16[192,768]{1,0:T(8,128)(2,1)S(1)} %get-tuple-element.35.refs_2_.keep), channel_id=1, source_target_pairs={{8,0},{9,1},{10,2},{11,3},{12,4},{13,5},{14,6},{15,7},{0,8},{1,9},... | collective-permute-start | bytes 884744 | tf_op jit(solution)/shard_map/ppermute | solution.py:397
  7.9 11.2 %collective-permute-start.9 = (bf16[192,768]{1,0:T(8,128)(2,1)S(1)}, bf16[192,768]{1,0:T(8,128)(2,1)S(1)}, u32[]{:S(2)}, u32[]{:S(2)}) collective-permute-start(bf16[192,768]{1,0:T(8,128)(2,1)S(1)} %collective-permute-done.3.refs_3_.got_mine), channel_id=1, source_target_pairs={{2,0},{7,1},{4,2},{1,3},{6,4},{3,5},{0,6},{5,7},{10,8},{15,9},{12,... | collective-permute-start | bytes 884744 | tf_op jit(solution)/shard_map/ppermute | solution.py:397
  9.6 12.5 %collective-permute-start.11 = (bf16[192,768]{1,0:T(8,128)(2,1)S(1)}, bf16[192,768]{1,0:T(8,128)(2,1)S(1)}, u32[]{:S(2)}, u32[]{:S(2)}) collective-permute-start(bf16[192,768]{1,0:T(8,128)(2,1)S(1)} %collective-permute-done.3.refs_3_.got_mine), channel_id=1, source_target_pairs={{8,0},{9,1},{10,2},{11,3},{12,4},{13,5},{14,6},{15,7},{0,8},{1,9},... | collective-permute-start | bytes 884744 | tf_op jit(solution)/shard_map/ppermute | solution.py:397
  13.3 12.1 %collective-permute-start.10 = (bf16[192,768]{1,0:T(8,128)(2,1)S(1)}, bf16[192,768]{1,0:T(8,128)(2,1)S(1)}, u32[]{:S(2)}, u32[]{:S(2)}) collective-permute-start(bf16[192,768]{1,0:T(8,128)(2,1)S(1)} %collective-permute-done.3.refs_3_.got_mine), channel_id=1, source_target_pairs={{6,0},{3,1},{0,2},{5,3},{2,4},{7,5},{4,6},{1,7},{14,8},{11,9},{8,1... | collective-permute-start | bytes 884744 | tf_op jit(solution)/shard_map/ppermute | solution.py:397
  15.8 9.9 %collective-permute-start.6 = (bf16[192,768]{1,0:T(8,128)(2,1)S(1)}, bf16[192,768]{1,0:T(8,128)(2,1)S(1)}, u32[]{:S(2)}, u32[]{:S(2)}) collective-permute-start(bf16[192,768]{1,0:T(8,128)(2,1)S(1)} %collective-permute-done.refs_3_), channel_id=1, source_target_pairs={{2,0},{7,1},{4,2},{1,3},{6,4},{3,5},{0,6},{5,7},{10,8},{15,9},{12,... | collective-permute-start | bytes 884744 | tf_op jit(solution)/shard_map/ppermute | solution.py:397
  19.1 10.9 %collective-permute-start.7 = (bf16[192,768]{1,0:T(8,128)(2,1)S(1)}, bf16[192,768]{1,0:T(8,128)(2,1)S(1)}, u32[]{:S(2)}, u32[]{:S(2)}) collective-permute-start(bf16[192,768]{1,0:T(8,128)(2,1)S(1)} %collective-permute-done.2.refs_5_), channel_id=1, source_target_pairs={{6,0},{3,1},{0,2},{5,3},{2,4},{7,5},{4,6},{1,7},{14,8},{11,9},{8,1... | collective-permute-start | bytes 884744 | tf_op jit(solution)/shard_map/ppermute | solution.py:397
  19.1 10.9 %collective-permute-start.8 = (bf16[192,768]{1,0:T(8,128)(2,1)S(1)}, bf16[192,768]{1,0:T(8,128)(2,1)S(1)}, u32[]{:S(2)}, u32[]{:S(2)}) collective-permute-start(bf16[192,768]{1,0:T(8,128)(2,1)S(1)} %collective-permute-done.refs_3_), channel_id=1, source_target_pairs={{8,0},{9,1},{10,2},{11,3},{12,4},{13,5},{14,6},{15,7},{0,8},{1,9},... | collective-permute-start | bytes 884744 | tf_op jit(solution)/shard_map/ppermute | solution.py:397
  22.1 10.7 %collective-permute-start.12 = (bf16[192,768]{1,0:T(8,128)(2,1)S(1)}, bf16[192,768]{1,0:T(8,128)(2,1)S(1)}, u32[]{:S(2)}, u32[]{:S(2)}) collective-permute-start(bf16[192,768]{1,0:T(8,128)(2,1)S(1)} %collective-permute-done.9.refs_6_), channel_id=1, source_target_pairs={{2,0},{7,1},{4,2},{1,3},{6,4},{3,5},{0,6},{5,7},{10,8},{15,9},{12,... | collective-permute-start | bytes 884744 | tf_op jit(solution)/shard_map/ppermute | solution.py:397
  25.4 10.0 %collective-permute-start.14 = (bf16[192,768]{1,0:T(8,128)(2,1)S(1)}, bf16[192,768]{1,0:T(8,128)(2,1)S(1)}, u32[]{:S(2)}, u32[]{:S(2)}) collective-permute-start(bf16[192,768]{1,0:T(8,128)(2,1)S(1)} %collective-permute-done.9.refs_6_), channel_id=1, source_target_pairs={{8,0},{9,1},{10,2},{11,3},{12,4},{13,5},{14,6},{15,7},{0,8},{1,9},... | collective-permute-start | bytes 884744 | tf_op jit(solution)/shard_map/ppermute | solution.py:397
  25.6 9.7 %collective-permute-start.13 = (bf16[192,768]{1,0:T(8,128)(2,1)S(1)}, bf16[192,768]{1,0:T(8,128)(2,1)S(1)}, u32[]{:S(2)}, u32[]{:S(2)}) collective-permute-start(bf16[192,768]{1,0:T(8,128)(2,1)S(1)} %collective-permute-done.11.refs_8_), channel_id=1, source_target_pairs={{6,0},{3,1},{0,2},{5,3},{2,4},{7,5},{4,6},{1,7},{14,8},{11,9},{8,1... | collective-permute-start | bytes 884744 | tf_op jit(solution)/shard_map/ppermute | solution.py:397
  29.9 10.9 %copy-start.4 = (s32[96,3]{0,1:T(4,128)S(1)}, s32[96,3]{0,1:T(4,128)}, u32[]{:S(2)}) copy-start(s32[96,3]{0,1:T(4,128)} %param.9) | copy-start | bytes 3460
  30.0 8.3 %collective-permute-start.15 = (bf16[192,768]{1,0:T(8,128)(2,1)S(1)}, bf16[192,768]{1,0:T(8,128)(2,1)S(1)}, u32[]{:S(2)}, u32[]{:S(2)}) collective-permute-start(bf16[192,768]{1,0:T(8,128)(2,1)S(1)} %collective-permute-done.7.refs_4_), channel_id=1, source_target_pairs={{6,0},{3,1},{0,2},{5,3},{2,4},{7,5},{4,6},{1,7},{14,8},{11,9},{8,1... | collective-permute-start | bytes 884744 | tf_op jit(solution)/shard_map/ppermute | solution.py:397
  32.8 8.1 %collective-permute-start.16 = (bf16[192,768]{1,0:T(8,128)(2,1)S(1)}, bf16[192,768]{1,0:T(8,128)(2,1)S(1)}, u32[]{:S(2)}, u32[]{:S(2)}) collective-permute-start(bf16[192,768]{1,0:T(8,128)(2,1)S(1)} %collective-permute-done.12.refs_6_), channel_id=1, source_target_pairs={{8,0},{9,1},{10,2},{11,3},{12,4},{13,5},{14,6},{15,7},{0,8},{1,9},... | collective-permute-start | bytes 884744 | tf_op jit(solution)/shard_map/ppermute | solution.py:397
  46.6 5.5 %copy-start.6 = (f32[192,768]{1,0:T(8,128)S(1)}, f32[192,768]{1,0:T(8,128)}, u32[]{:S(2)}) copy-start(f32[192,768]{1,0:T(8,128)} %get-tuple-element.52) | copy-start | bytes 1769476
  46.6 7.6 %copy-start.1 = (f32[192,768]{1,0:T(8,128)S(1)}, f32[192,768]{1,0:T(8,128)}, u32[]{:S(2)}) copy-start(f32[192,768]{1,0:T(8,128)} %get-tuple-element.51.mine) | copy-start | bytes 1769476
  46.6 7.5 %copy-start.5 = (f32[1,2]{1,0:T(1,128)S(1)}, f32[1,2]{1,0:T(1,128)}, u32[]{:S(2)}) copy-start(f32[1,2]{1,0:T(1,128)} %weights.3) | copy-start | bytes 28
  46.7 26.1 %all-to-all-start = ((f32[16,32,768]{2,1,0:T(8,128)}), f32[16,32,768]{2,1,0:T(8,128)S(1)}, u32[]{:S(2)}, u32[]{:S(2)}) async-start(f32[16,32,768]{2,1,0:T(8,128)} %get-tuple-element.55), calls=%async_computation | async-start | bytes 3145728 | tf_op jit(solution)/shard_map/all_to_all | solution.py:492
  52.1 2.1 %collective-permute-start.17 = (f32[192,768]{1,0:T(8,128)S(1)}, f32[192,768]{1,0:T(8,128)S(1)}, u32[]{:S(2)}, u32[]{:S(2)}) collective-permute-start(f32[192,768]{1,0:T(8,128)S(1)} %copy-done.6), channel_id=1, source_target_pairs={{1,0},{0,1},{3,2},{2,3},{5,4},{4,5},{7,6},{6,7},{9,8},{8,9},{11,10... | collective-permute-start | bytes 1769480 | tf_op jit(solution)/shard_map/ppermute | solution.py:397
  54.9 19.3 %copy-start.2 = (f32[1,2,3,32,512]{4,3,2,1,0:T(8,128)S(1)}, f32[1,2,3,32,512]{4,3,2,1,0:T(8,128)}, u32[]{:S(2)}) copy-start(f32[1,2,3,32,512]{4,3,2,1,0:T(8,128)} %param.8) | copy-start | bytes 1179652
  54.9 9.2 %collective-permute-start.18 = (f32[96,768]{1,0:T(8,128)S(1)}, f32[96,768]{1,0:T(8,128)S(1)}, u32[]{:S(2)}, u32[]{:S(2)}) collective-permute-start(f32[96,768]{1,0:T(8,128)S(1)} %get-tuple-element.53), channel_id=1, source_target_pairs={{32,0},{48,16},{0,32},{16,48},{96,64},{112,80},{64,96},{80,112},{1... | collective-permute-start | bytes 884744 | tf_op jit(solution)/shard_map/ppermute | solution.py:500
  64.2 10.0 %collective-permute-start.19 = (f32[48,768]{1,0:T(8,128)S(1)}, f32[48,768]{1,0:T(8,128)S(1)}, u32[]{:S(2)}, u32[]{:S(2)}) collective-permute-start(f32[48,768]{1,0:T(8,128)S(1)} %get-tuple-element.61), channel_id=1, source_target_pairs={{64,0},{80,16},{96,32},{112,48},{0,64},{16,80},{32,96},{48,112},{1... | collective-permute-start | bytes 442376 | tf_op jit(solution)/shard_map/ppermute | solution.py:515

commit v5 on v4

--- a/solution.py
+++ b/solution.py
@@ -44,6 +44,10 @@
 
 def z_pair(bit):
     return pole_perm(lambda z, h: (z ^ bit, h))
+
+
+POLE_ORDER = [z * NH + h for z in (0, 5, 2, 7, 1, 4, 3, 6) for h in range(NH)]
+GRID_ORDER = list(range(16))
 
 
 def place():
@@ -252,8 +256,9 @@
         re, im = z[2 * h * HB : (2 * h + 1) * HB], z[(2 * h + 1) * HB : (2 * h + 2) * HB]
         for t in range(8):
             r = slice(32 * t, 32 * t + 32)
-            q[8 * h + t, :, :HB] = re[r, :HB] - im[r, HB:]
-            q[8 * h + t, :, HB:BIG] = re[r, HB:] + im[r, :HB]
+            to = GRID_ORDER.index(8 * h + t)
+            q[to, :, :HB] = re[r, :HB] - im[r, HB:]
+            q[to, :, HB:BIG] = re[r, HB:] + im[r, :HB]
     copies.append(pltpu.make_async_copy(q.at[:, :, :BIG], q_out.at[:, :, :BIG], sems.at[2]))
     copies[2].start()
     lefts[1].wait()
@@ -270,8 +275,8 @@
         )
         at = slice(BIG + p * HS, BIG + (p + 1) * HS)
         for t in range(8):
-            q[t, :, at] = e[32 * t : 32 * t + 32]
-            q[8 + t, :, at] = jnp.zeros((32, HS), F32)
+            q[GRID_ORDER.index(t), :, at] = e[32 * t : 32 * t + 32]
+            q[GRID_ORDER.index(8 + t), :, at] = jnp.zeros((32, HS), F32)
     copies.append(pltpu.make_async_copy(q.at[:, :, BIG:], q_out.at[:, :, BIG:], sems.at[3]))
     copies[3].start()
     for copy in copies:
@@ -333,9 +338,8 @@
     g = lax.axis_index("grid")
     kb, k1, k2, a = supers(widths)
     wr, wi = weights[0, 0], weights[0, 1]
-    m, t = sums[0], sums[1]
-    for i in range(1, 8):
-        m, t = m + sums[2 * i], t + sums[2 * i + 1]
+    parts = [[sums[GRID_ORDER.index(2 * i + core)] for i in range(8)] for core in range(2)]
+    m, t = (functools.reduce(lambda u, v: u + v, part) for part in parts)
     row = iota((32, BIG), 0) + g * 32
     line = iota((32, BIG), 1)
     blank = jnp.zeros((32, HB), F32)
@@ -369,10 +373,10 @@
     column[:, at(k2, 1)] = none
     v, w = column[...], wide[...]
     pad = jnp.zeros((16, 32), F32)
-    for p in range(16):
+    for j, p in enumerate(POLE_ORDER):
         parts = [v[16 * i : 16 * i + 16, 96 * p : 96 * p + 96] for i in range(3)]
         parts += [w[16 * i : 16 * i + 16, 32 * p : 32 * p + 32] for i in range(6)]
-        pay[p] = jnp.concatenate(parts + [pad], axis=1)
+        pay[j] = jnp.concatenate(parts + [pad], axis=1)
 
 
 def density_kernel(pays, column, pivot):
@@ -381,7 +385,7 @@
         total = total + pays[p]
     for b0 in range(2):
         for b1 in range(2):
-            part = [pays[(b0 + 2 * b1 + 4 * b2) * NH + h] for b2 in range(2) for h in range(NH)]
+            part = [pays[POLE_ORDER.index((b0 + 2 * b1 + 4 * b2) * NH + h)] for b2 in range(2) for h in range(NH)]
             v = (part[0] + part[1]) + (part[2] + part[3])
             for i in range(3):
                 row = 96 * b0 + 48 * b1 + 16 * i
@@ -489,7 +493,7 @@
         out_space=pltpu.HBM,
     )
     other = over_grid(sib, CORE)
-    sums = lax.all_to_all(q, "grid", 0, 0, tiled=True)
+    sums = lax.all_to_all(q, "grid", 0, 0, axis_index_groups=[GRID_ORDER], tiled=True)
     d_keep, d_send = call(
         term_kernel,
         [sds((96, 768), F32)] * 2,
@@ -528,7 +532,7 @@
         "pivot",
         scratch=[pltpu.VMEM((96, BIG), F32), pltpu.VMEM((48, 3 * BIG), F32)],
     )
-    pays = lax.all_to_all(pay, "pole", 0, 0, tiled=True)
+    pays = lax.all_to_all(pay, "pole", 0, 0, axis_index_groups=[POLE_ORDER], tiled=True)
     density_column, density_pivot = call(
         density_kernel, [sds((ROWS, 96), F32), sds((3, 32, 32), F32)], [(pays, "v")], "density"
     )

time: 105 us -> 104 us (level)
  no operation moved by 1% of the time
where the time goes in v5:
time: 104 us; the launch traced here: 103 us
  starting transfers between devices  30.5 us (29%)
  blocking collectives  26.9 us (26%)
  waiting for transfers between devices  24.8 us (24%)
  Pallas kernels  20.4 us (20%)
    all_to_all x1, blocking collectives, local(): lax.all_to_all(pay, 'pole', 0, 0, axis_index_groups=[POLE_ORDER], tiled=T...  26.9 us
    pallas_call x11, Pallas kernels, call(): pl.pallas_call(body, out_shape=tuple(outs), in_specs=[pl.BlockSpec(memory...  20.4 us
    ppermute x18, starting transfers between devices, over_grid(): return lax.ppermute(v, 'grid', perm)  19.8 us
    ppermute x18, waiting for transfers between devices, over_grid(): return lax.ppermute(v, 'grid', perm)  12.6 us
    ppermute x1, waiting for transfers between devices, local(): d_got = lax.ppermute(d_send, 'pole', z_pair(1))  5.49 us
    all_to_all x1, starting transfers between devices, local(): lax.all_to_all(q, 'grid', 0, 0, axis_index_groups=[GRID_ORDER], tiled=True)  5.43 us
    all_to_all x1, waiting for transfers between devices, local(): lax.all_to_all(q, 'grid', 0, 0, axis_index_groups=[GRID_ORDER], tiled=True)  5.27 us
    ppermute x1, starting transfers between devices, local(): d_got = lax.ppermute(d_send, 'pole', z_pair(2))  3.35 us
  transfers between devices with their start and end apart: 21, of which 11 were waited for; matrix products, arithmetic and copies ran while one was open for 0% of the time, Pallas kernels for 12%

profile of v5, /device:TPU:8, one launch (start us, length us, event | category | flops | bytes accessed | tf_op | source)
XLA Modules:
  0.0 103.4 jit_solution(11213873354346325682)
XLA Ops:
  0.8 1.7 %prep.1 = (bf16[192,768]{1,0:T(8,128)(2,1)S(1)}, bf16[192,768]{1,0:T(8,128)(2,1)S(1)}) custom-call(s32[3,96]{1,0:T(4,128)} %bitcast.12, s32[3]{0:T(128)} %widths.7, bf16[2,192,1536]{2,1,0:T(8,128)(2,1)} %bitcast.15), custom_call_target="tpu_custom_call" | custom-call | flops 50331648 | bytes 1770636 | tf_op jit(solution)/shard_map/prep/pallas_call | solution.py:90
  3.1 2.8 %collective-permute-start = (bf16[192,768]{1,0:T(8,128)(2,1)S(1)}, bf16[192,768]{1,0:T(8,128)(2,1)S(1)}, u32[]{:S(2)}, u32[]{:S(2)}) collective-permute-start(bf16[192,768]{1,0:T(8,128)(2,1)S(1)} %get-tuple-element.35.refs_2_.keep), channel_id=1, source_target_pairs={{2,0},{7,1},{4,2},{1,3},{6,4},{3,5},{0,6},{5,7},{10,8},{15,9},{12,... | collective-permute-start | bytes 884744 | tf_op jit(solution)/shard_map/ppermute | solution.py:401
  5.9 2.0 %collective-permute-start.2 = (bf16[192,768]{1,0:T(8,128)(2,1)S(1)}, bf16[192,768]{1,0:T(8,128)(2,1)S(1)}, u32[]{:S(2)}, u32[]{:S(2)}) collective-permute-start(bf16[192,768]{1,0:T(8,128)(2,1)S(1)} %get-tuple-element.35.refs_2_.keep), channel_id=1, source_target_pairs={{8,0},{9,1},{10,2},{11,3},{12,4},{13,5},{14,6},{15,7},{0,8},{1,9},... | collective-permute-start | bytes 884744 | tf_op jit(solution)/shard_map/ppermute | solution.py:401
  7.9 1.7 %collective-permute-start.9 = (bf16[192,768]{1,0:T(8,128)(2,1)S(1)}, bf16[192,768]{1,0:T(8,128)(2,1)S(1)}, u32[]{:S(2)}, u32[]{:S(2)}) collective-permute-start(bf16[192,768]{1,0:T(8,128)(2,1)S(1)} %collective-permute-done.3.refs_3_.got_mine), channel_id=1, source_target_pairs={{2,0},{7,1},{4,2},{1,3},{6,4},{3,5},{0,6},{5,7},{10,8},{15,9},{12,... | collective-permute-start | bytes 884744 | tf_op jit(solution)/shard_map/ppermute | solution.py:401
  9.6 1.6 %collective-permute-start.11 = (bf16[192,768]{1,0:T(8,128)(2,1)S(1)}, bf16[192,768]{1,0:T(8,128)(2,1)S(1)}, u32[]{:S(2)}, u32[]{:S(2)}) collective-permute-start(bf16[192,768]{1,0:T(8,128)(2,1)S(1)} %collective-permute-done.3.refs_3_.got_mine), channel_id=1, source_target_pairs={{8,0},{9,1},{10,2},{11,3},{12,4},{13,5},{14,6},{15,7},{0,8},{1,9},... | collective-permute-start | bytes 884744 | tf_op jit(solution)/shard_map/ppermute | solution.py:401
  11.2 1.1 %left.1 = (bf16[1024,384]{1,0:T(8,128)(2,1)S(1)}, bf16[1024,384]{1,0:T(8,128)(2,1)S(1)}) custom-call(s32[3]{0:T(128)S(1)} %copy-done.3, bf16[192,768]{1,0:T(8,128)(2,1)S(1)} %get-tuple-element.35.refs_2_.keep, bf16[192,768]{1,0:T(8,128)(2,1)S(1)} %get-tuple-element.36.send, bf16[192,768]{1,0:T(8,128)(2,1)S(1)} %collective-permute-done.3.refs_3_.got_mine, ...), custom_call_target="tpu_custom_call" | custom-call | flops 100663296 | bytes 2752524 | tf_op jit(solution)/shard_map/left/pallas_call | solution.py:90
  12.2 1.0 %product.3.refs_0_ = f32[2,192,768]{2,1,0:T(8,128)S(1)} custom-call(bf16[384,3072]{1,0:T(8,128)(2,1)S(1)} %bitcast.7, bf16[384,3072]{1,0:T(8,128)(2,1)S(1)} %collective-permute-done.4.refs_1_.refs_2_.a_sib, bf16[192,768]{1,0:T(8,128)(2,1)S(1)} %get-tuple-element.35.refs_2_.keep, bf16[192,768]{1,0:T(8,128)(2,1)S(1)} %collective-permute-done.3.refs_3_.got_mine), custom_call_target="tpu_custom_call" | custom-call | flops 452984832 | bytes 6488064 | tf_op jit(solution)/shard_map/product/pallas_call | solution.py:90
  13.9 1.8 %collective-permute-done.1.refs_4_ = bf16[192,768]{1,0:T(8,128)(2,1)S(1)} collective-permute-done((bf16[192,768]{1,0:T(8,128)(2,1)S(1)}, bf16[192,768]{1,0:T(8,128)(2,1)S(1)}, u32[]{:S(2)}, u32[]{:S(2)}) %collective-permute-start.1) | collective-permute-done | bytes 294944 | tf_op jit(solution)/shard_map/ppermute | solution.py:401
  15.8 3.3 %collective-permute-start.6 = (bf16[192,768]{1,0:T(8,128)(2,1)S(1)}, bf16[192,768]{1,0:T(8,128)(2,1)S(1)}, u32[]{:S(2)}, u32[]{:S(2)}) collective-permute-start(bf16[192,768]{1,0:T(8,128)(2,1)S(1)} %collective-permute-done.refs_3_), channel_id=1, source_target_pairs={{2,0},{7,1},{4,2},{1,3},{6,4},{3,5},{0,6},{5,7},{10,8},{15,9},{12,... | collective-permute-start | bytes 884744 | tf_op jit(solution)/shard_map/ppermute | solution.py:401
  19.1 0.6 collective-permute-start.8
  19.7 2.4 %collective-permute-done.11.refs_8_ = bf16[192,768]{1,0:T(8,128)(2,1)S(1)} collective-permute-done((bf16[192,768]{1,0:T(8,128)(2,1)S(1)}, bf16[192,768]{1,0:T(8,128)(2,1)S(1)}, u32[]{:S(2)}, u32[]{:S(2)}) %collective-permute-start.11) | collective-permute-done | bytes 294944 | tf_op jit(solution)/shard_map/ppermute | solution.py:401
  22.1 3.3 %collective-permute-start.12 = (bf16[192,768]{1,0:T(8,128)(2,1)S(1)}, bf16[192,768]{1,0:T(8,128)(2,1)S(1)}, u32[]{:S(2)}, u32[]{:S(2)}) collective-permute-start(bf16[192,768]{1,0:T(8,128)(2,1)S(1)} %collective-permute-done.9.refs_6_), channel_id=1, source_target_pairs={{2,0},{7,1},{4,2},{1,3},{6,4},{3,5},{0,6},{5,7},{10,8},{15,9},{12,... | collective-permute-start | bytes 884744 | tf_op jit(solution)/shard_map/ppermute | solution.py:401
  25.6 1.3 %collective-permute-start.13 = (bf16[192,768]{1,0:T(8,128)(2,1)S(1)}, bf16[192,768]{1,0:T(8,128)(2,1)S(1)}, u32[]{:S(2)}, u32[]{:S(2)}) collective-permute-start(bf16[192,768]{1,0:T(8,128)(2,1)S(1)} %collective-permute-done.11.refs_8_), channel_id=1, source_target_pairs={{6,0},{3,1},{0,2},{5,3},{2,4},{7,5},{4,6},{1,7},{14,8},{11,9},{8,1... | collective-permute-start | bytes 884744 | tf_op jit(solution)/shard_map/ppermute | solution.py:401
  27.0 3.0 %product.4.refs_0_ = f32[2,192,768]{2,1,0:T(8,128)S(1)} custom-call(f32[2,192,768]{2,1,0:T(8,128)S(1)} %product.3.refs_0_, bf16[384,3072]{1,0:T(8,128)(2,1)S(1)} %bitcast.8, bf16[384,3072]{1,0:T(8,128)(2,1)S(1)} %collective-permute-done.4.refs_1_.refs_2_.a_sib, bf16[192,768]{1,0:T(8,128)(2,1)S(1)} %collective-permute-done.refs_3_, ...), custom_call_target="tpu_custom_call" | custom-call | flops 1358954496 | bytes 8847360 | tf_op jit(solution)/shard_map/product/pallas_call | solution.py:90
  30.0 1.6 %collective-permute-start.15 = (bf16[192,768]{1,0:T(8,128)(2,1)S(1)}, bf16[192,768]{1,0:T(8,128)(2,1)S(1)}, u32[]{:S(2)}, u32[]{:S(2)}) collective-permute-start(bf16[192,768]{1,0:T(8,128)(2,1)S(1)} %collective-permute-done.7.refs_4_), channel_id=1, source_target_pairs={{6,0},{3,1},{0,2},{5,3},{2,4},{7,5},{4,6},{1,7},{14,8},{11,9},{8,1... | collective-permute-start | bytes 884744 | tf_op jit(solution)/shard_map/ppermute | solution.py:401
  31.6 1.2 %collective-permute-done.12.refs_6_ = bf16[192,768]{1,0:T(8,128)(2,1)S(1)} collective-permute-done((bf16[192,768]{1,0:T(8,128)(2,1)S(1)}, bf16[192,768]{1,0:T(8,128)(2,1)S(1)}, u32[]{:S(2)}, u32[]{:S(2)}) %collective-permute-start.12) | collective-permute-done | bytes 294944 | tf_op jit(solution)/shard_map/ppermute | solution.py:401
  32.8 2.6 %collective-permute-done.14.refs_8_ = bf16[192,768]{1,0:T(8,128)(2,1)S(1)} collective-permute-done((bf16[192,768]{1,0:T(8,128)(2,1)S(1)}, bf16[192,768]{1,0:T(8,128)(2,1)S(1)}, u32[]{:S(2)}, u32[]{:S(2)}) %collective-permute-start.14) | collective-permute-done | bytes 294944 | tf_op jit(solution)/shard_map/ppermute | solution.py:401
  35.3 3.0 %product.5.old = f32[2,192,768]{2,1,0:T(8,128)S(1)} custom-call(f32[2,192,768]{2,1,0:T(8,128)S(1)} %product.4.refs_0_, bf16[384,3072]{1,0:T(8,128)(2,1)S(1)} %bitcast.9, bf16[384,3072]{1,0:T(8,128)(2,1)S(1)} %collective-permute-done.4.refs_1_.refs_2_.a_sib, bf16[192,768]{1,0:T(8,128)(2,1)S(1)} %collective-permute-done.6.refs_3_, ...), custom_call_target="tpu_custom_call" | custom-call | flops 1358954496 | bytes 8847360 | tf_op jit(solution)/shard_map/product/pallas_call | solution.py:90
  38.3 2.5 %collective-permute-done.16.v = bf16[192,768]{1,0:T(8,128)(2,1)S(1)} collective-permute-done((bf16[192,768]{1,0:T(8,128)(2,1)S(1)}, bf16[192,768]{1,0:T(8,128)(2,1)S(1)}, u32[]{:S(2)}, u32[]{:S(2)}) %collective-permute-start.16) | collective-permute-done | bytes 294944 | tf_op jit(solution)/shard_map/ppermute | solution.py:401
  40.8 5.8 %column.1 = (f32[192,768]{1,0:T(8,128)}, f32[192,768]{1,0:T(8,128)}, f32[16,32,768]{2,1,0:T(8,128)}) custom-call(s32[3,96]{1,0:T(4,128)S(1)} %bitcast.13, s32[3]{0:T(128)S(1)} %copy-done.3, f32[2,192,768]{2,1,0:T(8,128)S(1)} %product.5.old, bf16[384,3072]{1,0:T(8,128)(2,1)S(1)} %bitcast.10, ...), custom_call_target="tpu_custom_call" | custom-call | flops 1660944384 | bytes 10814604 | tf_op jit(solution)/shard_map/column/pallas_call | solution.py:90
  46.7 5.4 %all-to-all-start = ((f32[16,32,768]{2,1,0:T(8,128)}), f32[16,32,768]{2,1,0:T(8,128)S(1)}, u32[]{:S(2)}, u32[]{:S(2)}) async-start(f32[16,32,768]{2,1,0:T(8,128)} %get-tuple-element.55), calls=%async_computation | async-start | bytes 3145728 | tf_op jit(solution)/shard_map/all_to_all | solution.py:496
  52.3 1.9 %collective-permute-done.17.other = f32[192,768]{1,0:T(8,128)S(1)} collective-permute-done((f32[192,768]{1,0:T(8,128)S(1)}, f32[192,768]{1,0:T(8,128)S(1)}, u32[]{:S(2)}, u32[]{:S(2)}) %collective-permute-start.17) | collective-permute-done | bytes 589856 | tf_op jit(solution)/shard_map/ppermute | solution.py:401
  54.2 0.7 term.1
  54.9 1.9 %collective-permute-start.18 = (f32[96,768]{1,0:T(8,128)S(1)}, f32[96,768]{1,0:T(8,128)S(1)}, u32[]{:S(2)}, u32[]{:S(2)}) collective-permute-start(f32[96,768]{1,0:T(8,128)S(1)} %get-tuple-element.53), channel_id=1, source_target_pairs={{32,0},{48,16},{0,32},{16,48},{96,64},{112,80},{64,96},{80,112},{1... | collective-permute-start | bytes 884744 | tf_op jit(solution)/shard_map/ppermute | solution.py:504
  56.8 1.8 %spread.1 = bf16[2,192,1536]{2,1,0:T(8,128)(2,1)} custom-call(s32[3]{0:T(128)S(1)} %copy-done.3, f32[192,768]{1,0:T(8,128)S(1)} %copy-done.1, f32[192,768]{1,0:T(8,128)S(1)} %collective-permute-done.17.other), custom_call_target="tpu_custom_call" | custom-call | bytes 2359308 | tf_op jit(solution)/shard_map/spread/pallas_call | solution.py:90
  58.6 5.5 %collective-permute-done.18.got = f32[96,768]{1,0:T(8,128)S(1)} collective-permute-done((f32[96,768]{1,0:T(8,128)S(1)}, f32[96,768]{1,0:T(8,128)S(1)}, u32[]{:S(2)}, u32[]{:S(2)}) %collective-permute-start.18) | collective-permute-done | bytes 294944 | tf_op jit(solution)/shard_map/ppermute | solution.py:504
  64.2 3.3 %collective-permute-start.19 = (f32[48,768]{1,0:T(8,128)S(1)}, f32[48,768]{1,0:T(8,128)S(1)}, u32[]{:S(2)}, u32[]{:S(2)}) collective-permute-start(f32[48,768]{1,0:T(8,128)S(1)} %get-tuple-element.61), channel_id=1, source_target_pairs={{64,0},{80,16},{96,32},{112,48},{0,64},{16,80},{32,96},{48,112},{1... | collective-permute-start | bytes 442376 | tf_op jit(solution)/shard_map/ppermute | solution.py:519
  67.5 5.3 %all-to-all-done.sums = f32[16,32,768]{2,1,0:T(8,128)S(1)} async-done(((f32[16,32,768]{2,1,0:T(8,128)}), f32[16,32,768]{2,1,0:T(8,128)S(1)}, u32[]{:S(2)}, u32[]{:S(2)}) %all-to-all-start) | async-done | bytes 1572896 | tf_op jit(solution)/shard_map/all_to_all | solution.py:496
  72.8 1.4 %collective-permute-done.19.got = f32[48,768]{1,0:T(8,128)S(1)} collective-permute-done((f32[48,768]{1,0:T(8,128)S(1)}, f32[48,768]{1,0:T(8,128)S(1)}, u32[]{:S(2)}, u32[]{:S(2)}) %collective-permute-start.19) | collective-permute-done | bytes 147488 | tf_op jit(solution)/shard_map/ppermute | solution.py:519
  74.2 1.5 %pivot.1 = (f32[2,3,32,512]{3,2,1,0:T(8,128)}, f32[16,16,512]{2,1,0:T(8,128)S(1)}) custom-call(s32[3]{0:T(128)S(1)} %copy-done.3, f32[1,2]{1,0:T(1,128)S(1)} %copy-done.5, f32[2,3,32,512]{3,2,1,0:T(8,128)S(1)} %bitcast.11, f32[16,32,768]{2,1,0:T(8,128)S(1)} %all-to-all-done.sums, f32[48,768]{1,0:T(8,128)S(1)} %get-tuple-element.60.keep, ...), custom_call_target="tpu_custom_call" | custom-call | bytes 3178516 | tf_op jit(solution)/shard_map/pivot/pallas_call | solution.py:90
  75.7 26.9 %all_to_all.10.pays = f32[16,16,512]{2,1,0:T(8,128)S(1)} all-to-all(f32[16,16,512]{2,1,0:T(8,128)S(1)} %get-tuple-element.63), channel_id=1, replica_groups={{0,16,160,176,64,80,224,240,32,48,128,144,96,112,192,208},{1,17,161,177..., dimensions={0} | all-to-all | bytes 1048576 | tf_op jit(solution)/shard_map/all_to_all | solution.py:535
  102.6 0.8 density.1
  (36 shorter events, 2.1 us)
Async XLA Ops:
  0.6 10.5 %copy-start.3 = (s32[3]{0:T(128)S(1)}, s32[3]{0:T(128)}, u32[]{:S(2)}) copy-start(s32[3]{0:T(128)} %widths.7) | copy-start | bytes 40
  0.6 7.2 %collective-permute-start.4 = (bf16[384,3072]{1,0:T(8,128)(2,1)}, bf16[384,3072]{1,0:T(8,128)(2,1)S(1)}, u32[]{:S(2)}, u32[]{:S(2)}) collective-permute-start(bf16[384,3072]{1,0:T(8,128)(2,1)} %bitcast.6), channel_id=1, source_target_pairs={{1,0},{0,1},{3,2},{2,3},{5,4},{4,5},{7,6},{6,7},{9,8},{8,9},{11,10... | collective-permute-start | bytes 7077896 | tf_op jit(solution)/shard_map/ppermute | solution.py:401
  0.7 11.5 %copy-start = (bf16[1,2,192,3072]{3,2,1,0:T(8,128)(2,1)S(1)}, bf16[1,2,192,3072]{3,2,1,0:T(8,128)(2,1)}, u32[]{:S(2)}) copy-start(bf16[1,2,192,3072]{3,2,1,0:T(8,128)(2,1)} %param.7) | copy-start | bytes 7077892
  2.4 3.4 %collective-permute-start.3 = (bf16[192,768]{1,0:T(8,128)(2,1)S(1)}, bf16[192,768]{1,0:T(8,128)(2,1)S(1)}, u32[]{:S(2)}, u32[]{:S(2)}) collective-permute-start(bf16[192,768]{1,0:T(8,128)(2,1)S(1)} %get-tuple-element.36.send), channel_id=1, source_target_pairs={{1,0},{0,1},{3,2},{2,3},{5,4},{4,5},{7,6},{6,7},{9,8},{8,9},{11,10... | collective-permute-start | bytes 884744 | tf_op jit(solution)/shard_map/ppermute | solution.py:401
  3.0 6.6 %collective-permute-start.5 = (bf16[192,768]{1,0:T(8,128)(2,1)S(1)}, bf16[192,768]{1,0:T(8,128)(2,1)S(1)}, u32[]{:S(2)}, u32[]{:S(2)}) collective-permute-start(bf16[192,768]{1,0:T(8,128)(2,1)S(1)} %get-tuple-element.35.refs_2_.keep), channel_id=1, source_target_pairs={{1,0},{0,1},{3,2},{2,3},{5,4},{4,5},{7,6},{6,7},{9,8},{8,9},{11,10... | collective-permute-start | bytes 884744 | tf_op jit(solution)/shard_map/ppermute | solution.py:401
  3.1 10.2 %collective-permute-start = (bf16[192,768]{1,0:T(8,128)(2,1)S(1)}, bf16[192,768]{1,0:T(8,128)(2,1)S(1)}, u32[]{:S(2)}, u32[]{:S(2)}) collective-permute-start(bf16[192,768]{1,0:T(8,128)(2,1)S(1)} %get-tuple-element.35.refs_2_.keep), channel_id=1, source_target_pairs={{2,0},{7,1},{4,2},{1,3},{6,4},{3,5},{0,6},{5,7},{10,8},{15,9},{12,... | collective-permute-start | bytes 884744 | tf_op jit(solution)/shard_map/ppermute | solution.py:401
  5.9 9.8 %collective-permute-start.1 = (bf16[192,768]{1,0:T(8,128)(2,1)S(1)}, bf16[192,768]{1,0:T(8,128)(2,1)S(1)}, u32[]{:S(2)}, u32[]{:S(2)}) collective-permute-start(bf16[192,768]{1,0:T(8,128)(2,1)S(1)} %get-tuple-element.35.refs_2_.keep), channel_id=1, source_target_pairs={{6,0},{3,1},{0,2},{5,3},{2,4},{7,5},{4,6},{1,7},{14,8},{11,9},{8,1... | collective-permute-start | bytes 884744 | tf_op jit(solution)/shard_map/ppermute | solution.py:401
  5.9 9.9 %collective-permute-start.2 = (bf16[192,768]{1,0:T(8,128)(2,1)S(1)}, bf16[192,768]{1,0:T(8,128)(2,1)S(1)}, u32[]{:S(2)}, u32[]{:S(2)}) collective-permute-start(bf16[192,768]{1,0:T(8,128)(2,1)S(1)} %get-tuple-element.35.refs_2_.keep), channel_id=1, source_target_pairs={{8,0},{9,1},{10,2},{11,3},{12,4},{13,5},{14,6},{15,7},{0,8},{1,9},... | collective-permute-start | bytes 884744 | tf_op jit(solution)/shard_map/ppermute | solution.py:401
  7.9 11.2 %collective-permute-start.9 = (bf16[192,768]{1,0:T(8,128)(2,1)S(1)}, bf16[192,768]{1,0:T(8,128)(2,1)S(1)}, u32[]{:S(2)}, u32[]{:S(2)}) collective-permute-start(bf16[192,768]{1,0:T(8,128)(2,1)S(1)} %collective-permute-done.3.refs_3_.got_mine), channel_id=1, source_target_pairs={{2,0},{7,1},{4,2},{1,3},{6,4},{3,5},{0,6},{5,7},{10,8},{15,9},{12,... | collective-permute-start | bytes 884744 | tf_op jit(solution)/shard_map/ppermute | solution.py:401
  9.6 12.5 %collective-permute-start.11 = (bf16[192,768]{1,0:T(8,128)(2,1)S(1)}, bf16[192,768]{1,0:T(8,128)(2,1)S(1)}, u32[]{:S(2)}, u32[]{:S(2)}) collective-permute-start(bf16[192,768]{1,0:T(8,128)(2,1)S(1)} %collective-permute-done.3.refs_3_.got_mine), channel_id=1, source_target_pairs={{8,0},{9,1},{10,2},{11,3},{12,4},{13,5},{14,6},{15,7},{0,8},{1,9},... | collective-permute-start | bytes 884744 | tf_op jit(solution)/shard_map/ppermute | solution.py:401
  13.3 12.1 %collective-permute-start.10 = (bf16[192,768]{1,0:T(8,128)(2,1)S(1)}, bf16[192,768]{1,0:T(8,128)(2,1)S(1)}, u32[]{:S(2)}, u32[]{:S(2)}) collective-permute-start(bf16[192,768]{1,0:T(8,128)(2,1)S(1)} %collective-permute-done.3.refs_3_.got_mine), channel_id=1, source_target_pairs={{6,0},{3,1},{0,2},{5,3},{2,4},{7,5},{4,6},{1,7},{14,8},{11,9},{8,1... | collective-permute-start | bytes 884744 | tf_op jit(solution)/shard_map/ppermute | solution.py:401
  15.8 9.9 %collective-permute-start.6 = (bf16[192,768]{1,0:T(8,128)(2,1)S(1)}, bf16[192,768]{1,0:T(8,128)(2,1)S(1)}, u32[]{:S(2)}, u32[]{:S(2)}) collective-permute-start(bf16[192,768]{1,0:T(8,128)(2,1)S(1)} %collective-permute-done.refs_3_), channel_id=1, source_target_pairs={{2,0},{7,1},{4,2},{1,3},{6,4},{3,5},{0,6},{5,7},{10,8},{15,9},{12,... | collective-permute-start | bytes 884744 | tf_op jit(solution)/shard_map/ppermute | solution.py:401
  19.1 10.9 %collective-permute-start.7 = (bf16[192,768]{1,0:T(8,128)(2,1)S(1)}, bf16[192,768]{1,0:T(8,128)(2,1)S(1)}, u32[]{:S(2)}, u32[]{:S(2)}) collective-permute-start(bf16[192,768]{1,0:T(8,128)(2,1)S(1)} %collective-permute-done.2.refs_5_), channel_id=1, source_target_pairs={{6,0},{3,1},{0,2},{5,3},{2,4},{7,5},{4,6},{1,7},{14,8},{11,9},{8,1... | collective-permute-start | bytes 884744 | tf_op jit(solution)/shard_map/ppermute | solution.py:401
  19.1 10.9 %collective-permute-start.8 = (bf16[192,768]{1,0:T(8,128)(2,1)S(1)}, bf16[192,768]{1,0:T(8,128)(2,1)S(1)}, u32[]{:S(2)}, u32[]{:S(2)}) collective-permute-start(bf16[192,768]{1,0:T(8,128)(2,1)S(1)} %collective-permute-done.refs_3_), channel_id=1, source_target_pairs={{8,0},{9,1},{10,2},{11,3},{12,4},{13,5},{14,6},{15,7},{0,8},{1,9},... | collective-permute-start | bytes 884744 | tf_op jit(solution)/shard_map/ppermute | solution.py:401
  22.1 10.7 %collective-permute-start.12 = (bf16[192,768]{1,0:T(8,128)(2,1)S(1)}, bf16[192,768]{1,0:T(8,128)(2,1)S(1)}, u32[]{:S(2)}, u32[]{:S(2)}) collective-permute-start(bf16[192,768]{1,0:T(8,128)(2,1)S(1)} %collective-permute-done.9.refs_6_), channel_id=1, source_target_pairs={{2,0},{7,1},{4,2},{1,3},{6,4},{3,5},{0,6},{5,7},{10,8},{15,9},{12,... | collective-permute-start | bytes 884744 | tf_op jit(solution)/shard_map/ppermute | solution.py:401
  25.4 10.0 %collective-permute-start.14 = (bf16[192,768]{1,0:T(8,128)(2,1)S(1)}, bf16[192,768]{1,0:T(8,128)(2,1)S(1)}, u32[]{:S(2)}, u32[]{:S(2)}) collective-permute-start(bf16[192,768]{1,0:T(8,128)(2,1)S(1)} %collective-permute-done.9.refs_6_), channel_id=1, source_target_pairs={{8,0},{9,1},{10,2},{11,3},{12,4},{13,5},{14,6},{15,7},{0,8},{1,9},... | collective-permute-start | bytes 884744 | tf_op jit(solution)/shard_map/ppermute | solution.py:401
  25.6 9.7 %collective-permute-start.13 = (bf16[192,768]{1,0:T(8,128)(2,1)S(1)}, bf16[192,768]{1,0:T(8,128)(2,1)S(1)}, u32[]{:S(2)}, u32[]{:S(2)}) collective-permute-start(bf16[192,768]{1,0:T(8,128)(2,1)S(1)} %collective-permute-done.11.refs_8_), channel_id=1, source_target_pairs={{6,0},{3,1},{0,2},{5,3},{2,4},{7,5},{4,6},{1,7},{14,8},{11,9},{8,1... | collective-permute-start | bytes 884744 | tf_op jit(solution)/shard_map/ppermute | solution.py:401
  29.9 10.9 %copy-start.4 = (s32[96,3]{0,1:T(4,128)S(1)}, s32[96,3]{0,1:T(4,128)}, u32[]{:S(2)}) copy-start(s32[96,3]{0,1:T(4,128)} %param.9) | copy-start | bytes 3460
  30.0 8.3 %collective-permute-start.15 = (bf16[192,768]{1,0:T(8,128)(2,1)S(1)}, bf16[192,768]{1,0:T(8,128)(2,1)S(1)}, u32[]{:S(2)}, u32[]{:S(2)}) collective-permute-start(bf16[192,768]{1,0:T(8,128)(2,1)S(1)} %collective-permute-done.7.refs_4_), channel_id=1, source_target_pairs={{6,0},{3,1},{0,2},{5,3},{2,4},{7,5},{4,6},{1,7},{14,8},{11,9},{8,1... | collective-permute-start | bytes 884744 | tf_op jit(solution)/shard_map/ppermute | solution.py:401
  32.8 8.1 %collective-permute-start.16 = (bf16[192,768]{1,0:T(8,128)(2,1)S(1)}, bf16[192,768]{1,0:T(8,128)(2,1)S(1)}, u32[]{:S(2)}, u32[]{:S(2)}) collective-permute-start(bf16[192,768]{1,0:T(8,128)(2,1)S(1)} %collective-permute-done.12.refs_6_), channel_id=1, source_target_pairs={{8,0},{9,1},{10,2},{11,3},{12,4},{13,5},{14,6},{15,7},{0,8},{1,9},... | collective-permute-start | bytes 884744 | tf_op jit(solution)/shard_map/ppermute | solution.py:401
  46.6 5.5 %copy-start.6 = (f32[192,768]{1,0:T(8,128)S(1)}, f32[192,768]{1,0:T(8,128)}, u32[]{:S(2)}) copy-start(f32[192,768]{1,0:T(8,128)} %get-tuple-element.52) | copy-start | bytes 1769476
  46.6 7.6 %copy-start.1 = (f32[192,768]{1,0:T(8,128)S(1)}, f32[192,768]{1,0:T(8,128)}, u32[]{:S(2)}) copy-start(f32[192,768]{1,0:T(8,128)} %get-tuple-element.51.mine) | copy-start | bytes 1769476
  46.6 7.5 %copy-start.5 = (f32[1,2]{1,0:T(1,128)S(1)}, f32[1,2]{1,0:T(1,128)}, u32[]{:S(2)}) copy-start(f32[1,2]{1,0:T(1,128)} %weights.3) | copy-start | bytes 28
  46.7 26.1 %all-to-all-start = ((f32[16,32,768]{2,1,0:T(8,128)}), f32[16,32,768]{2,1,0:T(8,128)S(1)}, u32[]{:S(2)}, u32[]{:S(2)}) async-start(f32[16,32,768]{2,1,0:T(8,128)} %get-tuple-element.55), calls=%async_computation | async-start | bytes 3145728 | tf_op jit(solution)/shard_map/all_to_all | solution.py:496
  52.1 2.1 %collective-permute-start.17 = (f32[192,768]{1,0:T(8,128)S(1)}, f32[192,768]{1,0:T(8,128)S(1)}, u32[]{:S(2)}, u32[]{:S(2)}) collective-permute-start(f32[192,768]{1,0:T(8,128)S(1)} %copy-done.6), channel_id=1, source_target_pairs={{1,0},{0,1},{3,2},{2,3},{5,4},{4,5},{7,6},{6,7},{9,8},{8,9},{11,10... | collective-permute-start | bytes 1769480 | tf_op jit(solution)/shard_map/ppermute | solution.py:401
  54.9 19.3 %copy-start.2 = (f32[1,2,3,32,512]{4,3,2,1,0:T(8,128)S(1)}, f32[1,2,3,32,512]{4,3,2,1,0:T(8,128)}, u32[]{:S(2)}) copy-start(f32[1,2,3,32,512]{4,3,2,1,0:T(8,128)} %param.8) | copy-start | bytes 1179652
  54.9 9.2 %collective-permute-start.18 = (f32[96,768]{1,0:T(8,128)S(1)}, f32[96,768]{1,0:T(8,128)S(1)}, u32[]{:S(2)}, u32[]{:S(2)}) collective-permute-start(f32[96,768]{1,0:T(8,128)S(1)} %get-tuple-element.53), channel_id=1, source_target_pairs={{32,0},{48,16},{0,32},{16,48},{96,64},{112,80},{64,96},{80,112},{1... | collective-permute-start | bytes 884744 | tf_op jit(solution)/shard_map/ppermute | solution.py:504
  64.2 10.0 %collective-permute-start.19 = (f32[48,768]{1,0:T(8,128)S(1)}, f32[48,768]{1,0:T(8,128)S(1)}, u32[]{:S(2)}, u32[]{:S(2)}) collective-permute-start(f32[48,768]{1,0:T(8,128)S(1)} %get-tuple-element.61), channel_id=1, source_target_pairs={{64,0},{80,16},{96,32},{112,48},{0,64},{16,80},{32,96},{48,112},{1... | collective-permute-start | bytes 442376 | tf_op jit(solution)/shard_map/ppermute | solution.py:519

commit v6 on v5

--- a/solution.py
+++ b/solution.py
@@ -35,19 +35,20 @@
 FROM_Y = grid_perm(lambda y, x, c: (1 - y, x, c))
 
 
-def pole_perm(source):
-    def at(z, h):
-        return z * NH + h
-
-    return [(at(*source(z, h)), at(z, h)) for z in range(NZ) for h in range(NH)]
-
-
 def z_pair(bit):
-    return pole_perm(lambda z, h: (z ^ bit, h))
+    def at(z, h, g):
+        return ((z % NZ) * NH + h) * NX * NY * NCORE + g
+
+    return [
+        (at((((z - g % NCORE) % NZ) ^ bit) + g % NCORE, h, g), at(z, h, g))
+        for z in range(NZ)
+        for h in range(NH)
+        for g in range(NX * NY * NCORE)
+    ]
 
 
 POLE_ORDER = [z * NH + h for z in (0, 5, 2, 7, 1, 4, 3, 6) for h in range(NH)]
-GRID_ORDER = list(range(16))
+GRID_ORDER = [(y * NX + x) * NCORE + c for x in (0, 2, 1, 3) for y in range(NY) for c in range(NCORE)]
 
 
 def place():
@@ -60,6 +61,7 @@
 
 def z_bits():
     z = lax.div(lax.axis_index("pole"), NH)
+    z = lax.rem(z + NZ - lax.rem(lax.axis_index("grid"), NCORE), NZ)
     return lax.rem(z, 2), lax.rem(lax.div(z, 2), 2)
 
 
@@ -380,12 +382,17 @@
 
 
 def density_kernel(pays, column, pivot):
+    c = lax.rem(lax.axis_index("grid"), NCORE)
     total = pays[0]
     for p in range(1, 16):
         total = total + pays[p]
     for b0 in range(2):
         for b1 in range(2):
-            part = [pays[POLE_ORDER.index((b0 + 2 * b1 + 4 * b2) * NH + h)] for b2 in range(2) for h in range(NH)]
+            part = []
+            for z in (b0 + 2 * b1, b0 + 2 * b1 + 4):
+                for h in range(NH):
+                    at = [POLE_ORDER.index((z + core) % NZ * NH + h) for core in range(NCORE)]
+                    part.append(pays[jnp.where(c == 0, at[0], at[1])])
             v = (part[0] + part[1]) + (part[2] + part[3])
             for i in range(3):
                 row = 96 * b0 + 48 * b1 + 16 * i
@@ -501,7 +508,7 @@
         "term",
         scratch=[pltpu.VMEM((ROWS, 768), F32)],
     )
-    d_got = lax.ppermute(d_send, "pole", z_pair(1))
+    d_got = lax.ppermute(d_send, ("pole", "grid"), z_pair(1))
     column_inverse = call(
         spread_kernel,
         [sds((2, ROWS, 3 * BIG), BF16)],
@@ -516,7 +523,7 @@
         "second",
         scratch=[pltpu.VMEM((96, 768), F32)],
     )
-    d_got = lax.ppermute(d_send, "pole", z_pair(2))
+    d_got = lax.ppermute(d_send, ("pole", "grid"), z_pair(2))
     sums, d_keep = lax.optimization_barrier((sums, d_keep))
     pivot_block, pay = call(
         pivot_kernel,

time: 104 us -> 104 us (level)
  blocking collectives: 26.9 us -> 28.2 us
    ppermute x2, waiting for transfers between devices: 6.9 us -> 3.08 us  [the longest x1 3.08 us: local(): d_got = lax.ppermute(d_send, ('pole', 'grid'), z_pair(1))]
    all_to_all x1, waiting for transfers between devices: 5.27 us -> 8.47 us  [local(): lax.all_to_all(q, 'grid', 0, 0, axis_index_groups=[GRID_ORDER], tiled=True)]
    all_to_all x1, blocking collectives: 26.9 us -> 28.2 us  [local(): lax.all_to_all(pay, 'pole', 0, 0, axis_index_groups=[POLE_ORDER], tiled=T...]
  transfers between devices with their start and end apart: 21 -> 21, of which waited for: 11 -> 10; matrix products, arithmetic and copies ran while one was open for 0% -> 0% of each run, Pallas kernels for 12% -> 12%
where the time goes in v6:
time: 104 us
  starting transfers between devices  30.4 us (29%)
  blocking collectives  28.2 us (27%)
  waiting for transfers between devices  24.2 us (23%)
  Pallas kernels  20.4 us (20%)
    all_to_all x1, blocking collectives, local(): lax.all_to_all(pay, 'pole', 0, 0, axis_index_groups=[POLE_ORDER], tiled=T...  28.2 us
    pallas_call x11, Pallas kernels, call(): pl.pallas_call(body, out_shape=tuple(outs), in_specs=[pl.BlockSpec(memory...  20.4 us
    ppermute x18, starting transfers between devices, over_grid(): return lax.ppermute(v, 'grid', perm)  19.8 us
    ppermute x18, waiting for transfers between devices, over_grid(): return lax.ppermute(v, 'grid', perm)  12.6 us
    all_to_all x1, waiting for transfers between devices, local(): lax.all_to_all(q, 'grid', 0, 0, axis_index_groups=[GRID_ORDER], tiled=True)  8.47 us
    all_to_all x1, starting transfers between devices, local(): lax.all_to_all(q, 'grid', 0, 0, axis_index_groups=[GRID_ORDER], tiled=True)  5.39 us
    ppermute x1, starting transfers between devices, local(): d_got = lax.ppermute(d_send, ('pole', 'grid'), z_pair(2))  3.24 us
    ppermute x1, waiting for transfers between devices, local(): d_got = lax.ppermute(d_send, ('pole', 'grid'), z_pair(1))  3.08 us
  transfers between devices with their start and end apart: 21, of which 10 were waited for; matrix products, arithmetic and copies ran while one was open for 0% of the time, Pallas kernels for 12%

profile of v6, /device:TPU:8, one launch (start us, length us, event | category | flops | bytes accessed | tf_op | source)
XLA Modules:
  0.0 104.0 jit_solution(15250090269113604863)
XLA Ops:
  0.8 1.7 %prep.1 = (bf16[192,768]{1,0:T(8,128)(2,1)S(1)}, bf16[192,768]{1,0:T(8,128)(2,1)S(1)}) custom-call(s32[3,96]{1,0:T(4,128)} %bitcast.12, s32[3]{0:T(128)} %widths.7, bf16[2,192,1536]{2,1,0:T(8,128)(2,1)} %bitcast.15), custom_call_target="tpu_custom_call" | custom-call | flops 50331648 | bytes 1770636 | tf_op jit(solution)/shard_map/prep/pallas_call | solution.py:92
  3.1 2.8 %collective-permute-start = (bf16[192,768]{1,0:T(8,128)(2,1)S(1)}, bf16[192,768]{1,0:T(8,128)(2,1)S(1)}, u32[]{:S(2)}, u32[]{:S(2)}) collective-permute-start(bf16[192,768]{1,0:T(8,128)(2,1)S(1)} %get-tuple-element.35.refs_2_.keep), channel_id=1, source_target_pairs={{2,0},{7,1},{4,2},{1,3},{6,4},{3,5},{0,6},{5,7},{10,8},{15,9},{12,... | collective-permute-start | bytes 884744 | tf_op jit(solution)/shard_map/ppermute | solution.py:408
  5.9 2.0 %collective-permute-start.2 = (bf16[192,768]{1,0:T(8,128)(2,1)S(1)}, bf16[192,768]{1,0:T(8,128)(2,1)S(1)}, u32[]{:S(2)}, u32[]{:S(2)}) collective-permute-start(bf16[192,768]{1,0:T(8,128)(2,1)S(1)} %get-tuple-element.35.refs_2_.keep), channel_id=1, source_target_pairs={{8,0},{9,1},{10,2},{11,3},{12,4},{13,5},{14,6},{15,7},{0,8},{1,9},... | collective-permute-start | bytes 884744 | tf_op jit(solution)/shard_map/ppermute | solution.py:408
  7.9 1.7 %collective-permute-start.9 = (bf16[192,768]{1,0:T(8,128)(2,1)S(1)}, bf16[192,768]{1,0:T(8,128)(2,1)S(1)}, u32[]{:S(2)}, u32[]{:S(2)}) collective-permute-start(bf16[192,768]{1,0:T(8,128)(2,1)S(1)} %collective-permute-done.3.refs_3_.got_mine), channel_id=1, source_target_pairs={{2,0},{7,1},{4,2},{1,3},{6,4},{3,5},{0,6},{5,7},{10,8},{15,9},{12,... | collective-permute-start | bytes 884744 | tf_op jit(solution)/shard_map/ppermute | solution.py:408
  9.6 1.6 %collective-permute-start.11 = (bf16[192,768]{1,0:T(8,128)(2,1)S(1)}, bf16[192,768]{1,0:T(8,128)(2,1)S(1)}, u32[]{:S(2)}, u32[]{:S(2)}) collective-permute-start(bf16[192,768]{1,0:T(8,128)(2,1)S(1)} %collective-permute-done.3.refs_3_.got_mine), channel_id=1, source_target_pairs={{8,0},{9,1},{10,2},{11,3},{12,4},{13,5},{14,6},{15,7},{0,8},{1,9},... | collective-permute-start | bytes 884744 | tf_op jit(solution)/shard_map/ppermute | solution.py:408
  11.2 1.1 %left.1 = (bf16[1024,384]{1,0:T(8,128)(2,1)S(1)}, bf16[1024,384]{1,0:T(8,128)(2,1)S(1)}) custom-call(s32[3]{0:T(128)S(1)} %copy-done.3, bf16[192,768]{1,0:T(8,128)(2,1)S(1)} %get-tuple-element.35.refs_2_.keep, bf16[192,768]{1,0:T(8,128)(2,1)S(1)} %get-tuple-element.36.send, bf16[192,768]{1,0:T(8,128)(2,1)S(1)} %collective-permute-done.3.refs_3_.got_mine, ...), custom_call_target="tpu_custom_call" | custom-call | flops 100663296 | bytes 2752524 | tf_op jit(solution)/shard_map/left/pallas_call | solution.py:92
  12.2 1.0 %product.3.refs_0_ = f32[2,192,768]{2,1,0:T(8,128)S(1)} custom-call(bf16[384,3072]{1,0:T(8,128)(2,1)S(1)} %bitcast.7, bf16[384,3072]{1,0:T(8,128)(2,1)S(1)} %collective-permute-done.4.refs_1_.refs_2_.a_sib, bf16[192,768]{1,0:T(8,128)(2,1)S(1)} %get-tuple-element.35.refs_2_.keep, bf16[192,768]{1,0:T(8,128)(2,1)S(1)} %collective-permute-done.3.refs_3_.got_mine), custom_call_target="tpu_custom_call" | custom-call | flops 452984832 | bytes 6488064 | tf_op jit(solution)/shard_map/product/pallas_call | solution.py:92
  13.3 0.6 collective-permute-start.10
  13.9 1.8 %collective-permute-done.1.refs_4_ = bf16[192,768]{1,0:T(8,128)(2,1)S(1)} collective-permute-done((bf16[192,768]{1,0:T(8,128)(2,1)S(1)}, bf16[192,768]{1,0:T(8,128)(2,1)S(1)}, u32[]{:S(2)}, u32[]{:S(2)}) %collective-permute-start.1) | collective-permute-done | bytes 294944 | tf_op jit(solution)/shard_map/ppermute | solution.py:408
  15.8 3.3 %collective-permute-start.6 = (bf16[192,768]{1,0:T(8,128)(2,1)S(1)}, bf16[192,768]{1,0:T(8,128)(2,1)S(1)}, u32[]{:S(2)}, u32[]{:S(2)}) collective-permute-start(bf16[192,768]{1,0:T(8,128)(2,1)S(1)} %collective-permute-done.refs_3_), channel_id=1, source_target_pairs={{2,0},{7,1},{4,2},{1,3},{6,4},{3,5},{0,6},{5,7},{10,8},{15,9},{12,... | collective-permute-start | bytes 884744 | tf_op jit(solution)/shard_map/ppermute | solution.py:408
  19.1 0.6 collective-permute-start.8
  19.7 2.4 %collective-permute-done.11.refs_8_ = bf16[192,768]{1,0:T(8,128)(2,1)S(1)} collective-permute-done((bf16[192,768]{1,0:T(8,128)(2,1)S(1)}, bf16[192,768]{1,0:T(8,128)(2,1)S(1)}, u32[]{:S(2)}, u32[]{:S(2)}) %collective-permute-start.11) | collective-permute-done | bytes 294944 | tf_op jit(solution)/shard_map/ppermute | solution.py:408
  22.1 3.3 %collective-permute-start.12 = (bf16[192,768]{1,0:T(8,128)(2,1)S(1)}, bf16[192,768]{1,0:T(8,128)(2,1)S(1)}, u32[]{:S(2)}, u32[]{:S(2)}) collective-permute-start(bf16[192,768]{1,0:T(8,128)(2,1)S(1)} %collective-permute-done.9.refs_6_), channel_id=1, source_target_pairs={{2,0},{7,1},{4,2},{1,3},{6,4},{3,5},{0,6},{5,7},{10,8},{15,9},{12,... | collective-permute-start | bytes 884744 | tf_op jit(solution)/shard_map/ppermute | solution.py:408
  25.6 1.3 %collective-permute-start.13 = (bf16[192,768]{1,0:T(8,128)(2,1)S(1)}, bf16[192,768]{1,0:T(8,128)(2,1)S(1)}, u32[]{:S(2)}, u32[]{:S(2)}) collective-permute-start(bf16[192,768]{1,0:T(8,128)(2,1)S(1)} %collective-permute-done.11.refs_8_), channel_id=1, source_target_pairs={{6,0},{3,1},{0,2},{5,3},{2,4},{7,5},{4,6},{1,7},{14,8},{11,9},{8,1... | collective-permute-start | bytes 884744 | tf_op jit(solution)/shard_map/ppermute | solution.py:408
  27.0 3.0 %product.4.refs_0_ = f32[2,192,768]{2,1,0:T(8,128)S(1)} custom-call(f32[2,192,768]{2,1,0:T(8,128)S(1)} %product.3.refs_0_, bf16[384,3072]{1,0:T(8,128)(2,1)S(1)} %bitcast.8, bf16[384,3072]{1,0:T(8,128)(2,1)S(1)} %collective-permute-done.4.refs_1_.refs_2_.a_sib, bf16[192,768]{1,0:T(8,128)(2,1)S(1)} %collective-permute-done.refs_3_, ...), custom_call_target="tpu_custom_call" | custom-call | flops 1358954496 | bytes 8847360 | tf_op jit(solution)/shard_map/product/pallas_call | solution.py:92
  30.0 1.6 %collective-permute-start.15 = (bf16[192,768]{1,0:T(8,128)(2,1)S(1)}, bf16[192,768]{1,0:T(8,128)(2,1)S(1)}, u32[]{:S(2)}, u32[]{:S(2)}) collective-permute-start(bf16[192,768]{1,0:T(8,128)(2,1)S(1)} %collective-permute-done.7.refs_4_), channel_id=1, source_target_pairs={{6,0},{3,1},{0,2},{5,3},{2,4},{7,5},{4,6},{1,7},{14,8},{11,9},{8,1... | collective-permute-start | bytes 884744 | tf_op jit(solution)/shard_map/ppermute | solution.py:408
  31.6 1.2 %collective-permute-done.12.refs_6_ = bf16[192,768]{1,0:T(8,128)(2,1)S(1)} collective-permute-done((bf16[192,768]{1,0:T(8,128)(2,1)S(1)}, bf16[192,768]{1,0:T(8,128)(2,1)S(1)}, u32[]{:S(2)}, u32[]{:S(2)}) %collective-permute-start.12) | collective-permute-done | bytes 294944 | tf_op jit(solution)/shard_map/ppermute | solution.py:408
  32.8 2.6 %collective-permute-done.14.refs_8_ = bf16[192,768]{1,0:T(8,128)(2,1)S(1)} collective-permute-done((bf16[192,768]{1,0:T(8,128)(2,1)S(1)}, bf16[192,768]{1,0:T(8,128)(2,1)S(1)}, u32[]{:S(2)}, u32[]{:S(2)}) %collective-permute-start.14) | collective-permute-done | bytes 294944 | tf_op jit(solution)/shard_map/ppermute | solution.py:408
  35.3 3.0 %product.5.old = f32[2,192,768]{2,1,0:T(8,128)S(1)} custom-call(f32[2,192,768]{2,1,0:T(8,128)S(1)} %product.4.refs_0_, bf16[384,3072]{1,0:T(8,128)(2,1)S(1)} %bitcast.9, bf16[384,3072]{1,0:T(8,128)(2,1)S(1)} %collective-permute-done.4.refs_1_.refs_2_.a_sib, bf16[192,768]{1,0:T(8,128)(2,1)S(1)} %collective-permute-done.6.refs_3_, ...), custom_call_target="tpu_custom_call" | custom-call | flops 1358954496 | bytes 8847360 | tf_op jit(solution)/shard_map/product/pallas_call | solution.py:92
  38.3 2.5 %collective-permute-done.16.v = bf16[192,768]{1,0:T(8,128)(2,1)S(1)} collective-permute-done((bf16[192,768]{1,0:T(8,128)(2,1)S(1)}, bf16[192,768]{1,0:T(8,128)(2,1)S(1)}, u32[]{:S(2)}, u32[]{:S(2)}) %collective-permute-start.16) | collective-permute-done | bytes 294944 | tf_op jit(solution)/shard_map/ppermute | solution.py:408
  40.8 5.8 %column.1 = (f32[192,768]{1,0:T(8,128)}, f32[192,768]{1,0:T(8,128)}, f32[16,32,768]{2,1,0:T(8,128)}) custom-call(s32[3,96]{1,0:T(4,128)S(1)} %bitcast.13, s32[3]{0:T(128)S(1)} %copy-done.3, f32[2,192,768]{2,1,0:T(8,128)S(1)} %product.5.old, bf16[384,3072]{1,0:T(8,128)(2,1)S(1)} %bitcast.10, ...), custom_call_target="tpu_custom_call" | custom-call | flops 1660944384 | bytes 10814604 | tf_op jit(solution)/shard_map/column/pallas_call | solution.py:92
  46.7 5.4 %all-to-all-start = ((f32[16,32,768]{2,1,0:T(8,128)}), f32[16,32,768]{2,1,0:T(8,128)S(1)}, u32[]{:S(2)}, u32[]{:S(2)}) async-start(f32[16,32,768]{2,1,0:T(8,128)} %get-tuple-element.55), calls=%async_computation | async-start | bytes 3145728 | tf_op jit(solution)/shard_map/all_to_all | solution.py:503
  52.3 1.9 %collective-permute-done.17.other = f32[192,768]{1,0:T(8,128)S(1)} collective-permute-done((f32[192,768]{1,0:T(8,128)S(1)}, f32[192,768]{1,0:T(8,128)S(1)}, u32[]{:S(2)}, u32[]{:S(2)}) %collective-permute-start.17) | collective-permute-done | bytes 589856 | tf_op jit(solution)/shard_map/ppermute | solution.py:408
  54.1 0.7 term.1
  54.9 1.9 %collective-permute-start.18 = (f32[96,768]{1,0:T(8,128)S(1)}, f32[96,768]{1,0:T(8,128)S(1)}, u32[]{:S(2)}, u32[]{:S(2)}) collective-permute-start(f32[96,768]{1,0:T(8,128)S(1)} %get-tuple-element.53), channel_id=1, source_target_pairs={{32,0},{225,1},{34,2},{227,3},{36,4},{229,5},{38,6},{231,7},{40,8}... | collective-permute-start | bytes 884744 | tf_op jit(solution)/shard_map/ppermute | solution.py:511
  56.8 1.8 %spread.1 = bf16[2,192,1536]{2,1,0:T(8,128)(2,1)} custom-call(s32[3]{0:T(128)S(1)} %copy-done.3, f32[192,768]{1,0:T(8,128)S(1)} %copy-done.1, f32[192,768]{1,0:T(8,128)S(1)} %collective-permute-done.17.other), custom_call_target="tpu_custom_call" | custom-call | bytes 2359308 | tf_op jit(solution)/shard_map/spread/pallas_call | solution.py:92
  58.6 3.1 %collective-permute-done.18.got = f32[96,768]{1,0:T(8,128)S(1)} collective-permute-done((f32[96,768]{1,0:T(8,128)S(1)}, f32[96,768]{1,0:T(8,128)S(1)}, u32[]{:S(2)}, u32[]{:S(2)}) %collective-permute-start.18) | collective-permute-done | bytes 294944 | tf_op jit(solution)/shard_map/ppermute | solution.py:511
  61.8 3.2 %collective-permute-start.19 = (f32[48,768]{1,0:T(8,128)S(1)}, f32[48,768]{1,0:T(8,128)S(1)}, u32[]{:S(2)}, u32[]{:S(2)}) collective-permute-start(f32[48,768]{1,0:T(8,128)S(1)} %get-tuple-element.61), channel_id=1, source_target_pairs={{64,0},{193,1},{66,2},{195,3},{68,4},{197,5},{70,6},{199,7},{72,8}... | collective-permute-start | bytes 442376 | tf_op jit(solution)/shard_map/ppermute | solution.py:526
  65.0 8.5 %all-to-all-done.sums = f32[16,32,768]{2,1,0:T(8,128)S(1)} async-done(((f32[16,32,768]{2,1,0:T(8,128)}), f32[16,32,768]{2,1,0:T(8,128)S(1)}, u32[]{:S(2)}, u32[]{:S(2)}) %all-to-all-start) | async-done | bytes 1572896 | tf_op jit(solution)/shard_map/all_to_all | solution.py:503
  73.5 1.5 %pivot.1 = (f32[2,3,32,512]{3,2,1,0:T(8,128)}, f32[16,16,512]{2,1,0:T(8,128)S(1)}) custom-call(s32[3]{0:T(128)S(1)} %copy-done.3, f32[1,2]{1,0:T(1,128)S(1)} %copy-done.5, f32[2,3,32,512]{3,2,1,0:T(8,128)S(1)} %bitcast.11, f32[16,32,768]{2,1,0:T(8,128)S(1)} %all-to-all-done.sums, f32[48,768]{1,0:T(8,128)S(1)} %get-tuple-element.60.keep, ...), custom_call_target="tpu_custom_call" | custom-call | bytes 3178516 | tf_op jit(solution)/shard_map/pivot/pallas_call | solution.py:92
  75.0 28.2 %all_to_all.10.pays = f32[16,16,512]{2,1,0:T(8,128)S(1)} all-to-all(f32[16,16,512]{2,1,0:T(8,128)S(1)} %get-tuple-element.63), channel_id=1, replica_groups={{0,16,160,176,64,80,224,240,32,48,128,144,96,112,192,208},{1,17,161,177..., dimensions={0} | all-to-all | bytes 1048576 | tf_op jit(solution)/shard_map/all_to_all | solution.py:542
  103.2 0.8 density.1
  (36 shorter events, 1.5 us)
Async XLA Ops:
  0.6 10.5 %copy-start.3 = (s32[3]{0:T(128)S(1)}, s32[3]{0:T(128)}, u32[]{:S(2)}) copy-start(s32[3]{0:T(128)} %widths.7) | copy-start | bytes 40
  0.6 7.2 %collective-permute-start.4 = (bf16[384,3072]{1,0:T(8,128)(2,1)}, bf16[384,3072]{1,0:T(8,128)(2,1)S(1)}, u32[]{:S(2)}, u32[]{:S(2)}) collective-permute-start(bf16[384,3072]{1,0:T(8,128)(2,1)} %bitcast.6), channel_id=1, source_target_pairs={{1,0},{0,1},{3,2},{2,3},{5,4},{4,5},{7,6},{6,7},{9,8},{8,9},{11,10... | collective-permute-start | bytes 7077896 | tf_op jit(solution)/shard_map/ppermute | solution.py:408
  0.7 11.5 %copy-start = (bf16[1,2,192,3072]{3,2,1,0:T(8,128)(2,1)S(1)}, bf16[1,2,192,3072]{3,2,1,0:T(8,128)(2,1)}, u32[]{:S(2)}) copy-start(bf16[1,2,192,3072]{3,2,1,0:T(8,128)(2,1)} %param.7) | copy-start | bytes 7077892
  2.4 3.4 %collective-permute-start.3 = (bf16[192,768]{1,0:T(8,128)(2,1)S(1)}, bf16[192,768]{1,0:T(8,128)(2,1)S(1)}, u32[]{:S(2)}, u32[]{:S(2)}) collective-permute-start(bf16[192,768]{1,0:T(8,128)(2,1)S(1)} %get-tuple-element.36.send), channel_id=1, source_target_pairs={{1,0},{0,1},{3,2},{2,3},{5,4},{4,5},{7,6},{6,7},{9,8},{8,9},{11,10... | collective-permute-start | bytes 884744 | tf_op jit(solution)/shard_map/ppermute | solution.py:408
  3.0 6.6 %collective-permute-start.5 = (bf16[192,768]{1,0:T(8,128)(2,1)S(1)}, bf16[192,768]{1,0:T(8,128)(2,1)S(1)}, u32[]{:S(2)}, u32[]{:S(2)}) collective-permute-start(bf16[192,768]{1,0:T(8,128)(2,1)S(1)} %get-tuple-element.35.refs_2_.keep), channel_id=1, source_target_pairs={{1,0},{0,1},{3,2},{2,3},{5,4},{4,5},{7,6},{6,7},{9,8},{8,9},{11,10... | collective-permute-start | bytes 884744 | tf_op jit(solution)/shard_map/ppermute | solution.py:408
  3.1 10.2 %collective-permute-start = (bf16[192,768]{1,0:T(8,128)(2,1)S(1)}, bf16[192,768]{1,0:T(8,128)(2,1)S(1)}, u32[]{:S(2)}, u32[]{:S(2)}) collective-permute-start(bf16[192,768]{1,0:T(8,128)(2,1)S(1)} %get-tuple-element.35.refs_2_.keep), channel_id=1, source_target_pairs={{2,0},{7,1},{4,2},{1,3},{6,4},{3,5},{0,6},{5,7},{10,8},{15,9},{12,... | collective-permute-start | bytes 884744 | tf_op jit(solution)/shard_map/ppermute | solution.py:408
  5.9 9.8 %collective-permute-start.1 = (bf16[192,768]{1,0:T(8,128)(2,1)S(1)}, bf16[192,768]{1,0:T(8,128)(2,1)S(1)}, u32[]{:S(2)}, u32[]{:S(2)}) collective-permute-start(bf16[192,768]{1,0:T(8,128)(2,1)S(1)} %get-tuple-element.35.refs_2_.keep), channel_id=1, source_target_pairs={{6,0},{3,1},{0,2},{5,3},{2,4},{7,5},{4,6},{1,7},{14,8},{11,9},{8,1... | collective-permute-start | bytes 884744 | tf_op jit(solution)/shard_map/ppermute | solution.py:408
  5.9 9.9 %collective-permute-start.2 = (bf16[192,768]{1,0:T(8,128)(2,1)S(1)}, bf16[192,768]{1,0:T(8,128)(2,1)S(1)}, u32[]{:S(2)}, u32[]{:S(2)}) collective-permute-start(bf16[192,768]{1,0:T(8,128)(2,1)S(1)} %get-tuple-element.35.refs_2_.keep), channel_id=1, source_target_pairs={{8,0},{9,1},{10,2},{11,3},{12,4},{13,5},{14,6},{15,7},{0,8},{1,9},... | collective-permute-start | bytes 884744 | tf_op jit(solution)/shard_map/ppermute | solution.py:408
  7.9 11.2 %collective-permute-start.9 = (bf16[192,768]{1,0:T(8,128)(2,1)S(1)}, bf16[192,768]{1,0:T(8,128)(2,1)S(1)}, u32[]{:S(2)}, u32[]{:S(2)}) collective-permute-start(bf16[192,768]{1,0:T(8,128)(2,1)S(1)} %collective-permute-done.3.refs_3_.got_mine), channel_id=1, source_target_pairs={{2,0},{7,1},{4,2},{1,3},{6,4},{3,5},{0,6},{5,7},{10,8},{15,9},{12,... | collective-permute-start | bytes 884744 | tf_op jit(solution)/shard_map/ppermute | solution.py:408
  9.6 12.5 %collective-permute-start.11 = (bf16[192,768]{1,0:T(8,128)(2,1)S(1)}, bf16[192,768]{1,0:T(8,128)(2,1)S(1)}, u32[]{:S(2)}, u32[]{:S(2)}) collective-permute-start(bf16[192,768]{1,0:T(8,128)(2,1)S(1)} %collective-permute-done.3.refs_3_.got_mine), channel_id=1, source_target_pairs={{8,0},{9,1},{10,2},{11,3},{12,4},{13,5},{14,6},{15,7},{0,8},{1,9},... | collective-permute-start | bytes 884744 | tf_op jit(solution)/shard_map/ppermute | solution.py:408
  13.3 12.1 %collective-permute-start.10 = (bf16[192,768]{1,0:T(8,128)(2,1)S(1)}, bf16[192,768]{1,0:T(8,128)(2,1)S(1)}, u32[]{:S(2)}, u32[]{:S(2)}) collective-permute-start(bf16[192,768]{1,0:T(8,128)(2,1)S(1)} %collective-permute-done.3.refs_3_.got_mine), channel_id=1, source_target_pairs={{6,0},{3,1},{0,2},{5,3},{2,4},{7,5},{4,6},{1,7},{14,8},{11,9},{8,1... | collective-permute-start | bytes 884744 | tf_op jit(solution)/shard_map/ppermute | solution.py:408
  15.8 9.9 %collective-permute-start.6 = (bf16[192,768]{1,0:T(8,128)(2,1)S(1)}, bf16[192,768]{1,0:T(8,128)(2,1)S(1)}, u32[]{:S(2)}, u32[]{:S(2)}) collective-permute-start(bf16[192,768]{1,0:T(8,128)(2,1)S(1)} %collective-permute-done.refs_3_), channel_id=1, source_target_pairs={{2,0},{7,1},{4,2},{1,3},{6,4},{3,5},{0,6},{5,7},{10,8},{15,9},{12,... | collective-permute-start | bytes 884744 | tf_op jit(solution)/shard_map/ppermute | solution.py:408
  19.1 10.9 %collective-permute-start.7 = (bf16[192,768]{1,0:T(8,128)(2,1)S(1)}, bf16[192,768]{1,0:T(8,128)(2,1)S(1)}, u32[]{:S(2)}, u32[]{:S(2)}) collective-permute-start(bf16[192,768]{1,0:T(8,128)(2,1)S(1)} %collective-permute-done.2.refs_5_), channel_id=1, source_target_pairs={{6,0},{3,1},{0,2},{5,3},{2,4},{7,5},{4,6},{1,7},{14,8},{11,9},{8,1... | collective-permute-start | bytes 884744 | tf_op jit(solution)/shard_map/ppermute | solution.py:408
  19.1 10.9 %collective-permute-start.8 = (bf16[192,768]{1,0:T(8,128)(2,1)S(1)}, bf16[192,768]{1,0:T(8,128)(2,1)S(1)}, u32[]{:S(2)}, u32[]{:S(2)}) collective-permute-start(bf16[192,768]{1,0:T(8,128)(2,1)S(1)} %collective-permute-done.refs_3_), channel_id=1, source_target_pairs={{8,0},{9,1},{10,2},{11,3},{12,4},{13,5},{14,6},{15,7},{0,8},{1,9},... | collective-permute-start | bytes 884744 | tf_op jit(solution)/shard_map/ppermute | solution.py:408
  22.1 10.7 %collective-permute-start.12 = (bf16[192,768]{1,0:T(8,128)(2,1)S(1)}, bf16[192,768]{1,0:T(8,128)(2,1)S(1)}, u32[]{:S(2)}, u32[]{:S(2)}) collective-permute-start(bf16[192,768]{1,0:T(8,128)(2,1)S(1)} %collective-permute-done.9.refs_6_), channel_id=1, source_target_pairs={{2,0},{7,1},{4,2},{1,3},{6,4},{3,5},{0,6},{5,7},{10,8},{15,9},{12,... | collective-permute-start | bytes 884744 | tf_op jit(solution)/shard_map/ppermute | solution.py:408
  25.4 10.0 %collective-permute-start.14 = (bf16[192,768]{1,0:T(8,128)(2,1)S(1)}, bf16[192,768]{1,0:T(8,128)(2,1)S(1)}, u32[]{:S(2)}, u32[]{:S(2)}) collective-permute-start(bf16[192,768]{1,0:T(8,128)(2,1)S(1)} %collective-permute-done.9.refs_6_), channel_id=1, source_target_pairs={{8,0},{9,1},{10,2},{11,3},{12,4},{13,5},{14,6},{15,7},{0,8},{1,9},... | collective-permute-start | bytes 884744 | tf_op jit(solution)/shard_map/ppermute | solution.py:408
  25.6 9.7 %collective-permute-start.13 = (bf16[192,768]{1,0:T(8,128)(2,1)S(1)}, bf16[192,768]{1,0:T(8,128)(2,1)S(1)}, u32[]{:S(2)}, u32[]{:S(2)}) collective-permute-start(bf16[192,768]{1,0:T(8,128)(2,1)S(1)} %collective-permute-done.11.refs_8_), channel_id=1, source_target_pairs={{6,0},{3,1},{0,2},{5,3},{2,4},{7,5},{4,6},{1,7},{14,8},{11,9},{8,1... | collective-permute-start | bytes 884744 | tf_op jit(solution)/shard_map/ppermute | solution.py:408
  29.9 10.9 %copy-start.4 = (s32[96,3]{0,1:T(4,128)S(1)}, s32[96,3]{0,1:T(4,128)}, u32[]{:S(2)}) copy-start(s32[96,3]{0,1:T(4,128)} %param.9) | copy-start | bytes 3460
  30.0 8.3 %collective-permute-start.15 = (bf16[192,768]{1,0:T(8,128)(2,1)S(1)}, bf16[192,768]{1,0:T(8,128)(2,1)S(1)}, u32[]{:S(2)}, u32[]{:S(2)}) collective-permute-start(bf16[192,768]{1,0:T(8,128)(2,1)S(1)} %collective-permute-done.7.refs_4_), channel_id=1, source_target_pairs={{6,0},{3,1},{0,2},{5,3},{2,4},{7,5},{4,6},{1,7},{14,8},{11,9},{8,1... | collective-permute-start | bytes 884744 | tf_op jit(solution)/shard_map/ppermute | solution.py:408
  32.8 8.1 %collective-permute-start.16 = (bf16[192,768]{1,0:T(8,128)(2,1)S(1)}, bf16[192,768]{1,0:T(8,128)(2,1)S(1)}, u32[]{:S(2)}, u32[]{:S(2)}) collective-permute-start(bf16[192,768]{1,0:T(8,128)(2,1)S(1)} %collective-permute-done.12.refs_6_), channel_id=1, source_target_pairs={{8,0},{9,1},{10,2},{11,3},{12,4},{13,5},{14,6},{15,7},{0,8},{1,9},... | collective-permute-start | bytes 884744 | tf_op jit(solution)/shard_map/ppermute | solution.py:408
  46.6 5.4 %copy-start.6 = (f32[192,768]{1,0:T(8,128)S(1)}, f32[192,768]{1,0:T(8,128)}, u32[]{:S(2)}) copy-start(f32[192,768]{1,0:T(8,128)} %get-tuple-element.52) | copy-start | bytes 1769476
  46.6 7.5 %copy-start.1 = (f32[192,768]{1,0:T(8,128)S(1)}, f32[192,768]{1,0:T(8,128)}, u32[]{:S(2)}) copy-start(f32[192,768]{1,0:T(8,128)} %get-tuple-element.51.mine) | copy-start | bytes 1769476
  46.6 7.5 %copy-start.5 = (f32[1,2]{1,0:T(1,128)S(1)}, f32[1,2]{1,0:T(1,128)}, u32[]{:S(2)}) copy-start(f32[1,2]{1,0:T(1,128)} %weights.3) | copy-start | bytes 28
  46.7 26.8 %all-to-all-start = ((f32[16,32,768]{2,1,0:T(8,128)}), f32[16,32,768]{2,1,0:T(8,128)S(1)}, u32[]{:S(2)}, u32[]{:S(2)}) async-start(f32[16,32,768]{2,1,0:T(8,128)} %get-tuple-element.55), calls=%async_computation | async-start | bytes 3145728 | tf_op jit(solution)/shard_map/all_to_all | solution.py:503
  52.0 2.1 %collective-permute-start.17 = (f32[192,768]{1,0:T(8,128)S(1)}, f32[192,768]{1,0:T(8,128)S(1)}, u32[]{:S(2)}, u32[]{:S(2)}) collective-permute-start(f32[192,768]{1,0:T(8,128)S(1)} %copy-done.6), channel_id=1, source_target_pairs={{1,0},{0,1},{3,2},{2,3},{5,4},{4,5},{7,6},{6,7},{9,8},{8,9},{11,10... | collective-permute-start | bytes 1769480 | tf_op jit(solution)/shard_map/ppermute | solution.py:408
  54.9 18.6 %copy-start.2 = (f32[1,2,3,32,512]{4,3,2,1,0:T(8,128)S(1)}, f32[1,2,3,32,512]{4,3,2,1,0:T(8,128)}, u32[]{:S(2)}) copy-start(f32[1,2,3,32,512]{4,3,2,1,0:T(8,128)} %param.8) | copy-start | bytes 1179652
  54.9 6.8 %collective-permute-start.18 = (f32[96,768]{1,0:T(8,128)S(1)}, f32[96,768]{1,0:T(8,128)S(1)}, u32[]{:S(2)}, u32[]{:S(2)}) collective-permute-start(f32[96,768]{1,0:T(8,128)S(1)} %get-tuple-element.53), channel_id=1, source_target_pairs={{32,0},{225,1},{34,2},{227,3},{36,4},{229,5},{38,6},{231,7},{40,8}... | collective-permute-start | bytes 884744 | tf_op jit(solution)/shard_map/ppermute | solution.py:511
  61.8 11.7 %collective-permute-start.19 = (f32[48,768]{1,0:T(8,128)S(1)}, f32[48,768]{1,0:T(8,128)S(1)}, u32[]{:S(2)}, u32[]{:S(2)}) collective-permute-start(f32[48,768]{1,0:T(8,128)S(1)} %get-tuple-element.61), channel_id=1, source_target_pairs={{64,0},{193,1},{66,2},{195,3},{68,4},{197,5},{70,6},{199,7},{72,8}... | collective-permute-start | bytes 442376 | tf_op jit(solution)/shard_map/ppermute | solution.py:526

commit v7 on v6

--- a/solution.py
+++ b/solution.py
@@ -47,7 +47,7 @@
     ]
 
 
-POLE_ORDER = [z * NH + h for z in (0, 5, 2, 7, 1, 4, 3, 6) for h in range(NH)]
+POLE_ORDER = [z * NH + h for z in (0, 7, 2, 5, 1, 6, 3, 4) for h in range(NH)]
 GRID_ORDER = [(y * NX + x) * NCORE + c for x in (0, 2, 1, 3) for y in range(NY) for c in range(NCORE)]
 
 

time: 104 us -> 104 us (level)
  no operation moved by 1% of the time
where the time goes in v7:
time: 104 us; the launch traced here: 103 us
  starting transfers between devices  30.4 us (29%)
  blocking collectives  27.4 us (26%)
  waiting for transfers between devices  24.2 us (23%)
  Pallas kernels  20.6 us (20%)
    all_to_all x1, blocking collectives, local(): lax.all_to_all(pay, 'pole', 0, 0, axis_index_groups=[POLE_ORDER], tiled=T...  27.4 us
    pallas_call x11, Pallas kernels, call(): pl.pallas_call(body, out_shape=tuple(outs), in_specs=[pl.BlockSpec(memory...  20.6 us
    ppermute x18, starting transfers between devices, over_grid(): return lax.ppermute(v, 'grid', perm)  19.8 us
    ppermute x18, waiting for transfers between devices, over_grid(): return lax.ppermute(v, 'grid', perm)  12.6 us
    all_to_all x1, waiting for transfers between devices, local(): lax.all_to_all(q, 'grid', 0, 0, axis_index_groups=[GRID_ORDER], tiled=True)  8.47 us
    all_to_all x1, starting transfers between devices, local(): lax.all_to_all(q, 'grid', 0, 0, axis_index_groups=[GRID_ORDER], tiled=True)  5.38 us
    ppermute x1, starting transfers between devices, local(): d_got = lax.ppermute(d_send, ('pole', 'grid'), z_pair(2))  3.24 us
    ppermute x1, waiting for transfers between devices, local(): d_got = lax.ppermute(d_send, ('pole', 'grid'), z_pair(1))  3.08 us
  transfers between devices with their start and end apart: 21, of which 10 were waited for; matrix products, arithmetic and copies ran while one was open for 0% of the time, Pallas kernels for 12%

profile of v7, /device:TPU:8, one launch (start us, length us, event | category | flops | bytes accessed | tf_op | source)
XLA Modules:
  0.0 103.4 jit_solution(3083313694167361040)
XLA Ops:
  0.8 1.7 %prep.1 = (bf16[192,768]{1,0:T(8,128)(2,1)S(1)}, bf16[192,768]{1,0:T(8,128)(2,1)S(1)}) custom-call(s32[3,96]{1,0:T(4,128)} %bitcast.12, s32[3]{0:T(128)} %widths.7, bf16[2,192,1536]{2,1,0:T(8,128)(2,1)} %bitcast.15), custom_call_target="tpu_custom_call" | custom-call | flops 50331648 | bytes 1770636 | tf_op jit(solution)/shard_map/prep/pallas_call | solution.py:92
  3.1 2.8 %collective-permute-start = (bf16[192,768]{1,0:T(8,128)(2,1)S(1)}, bf16[192,768]{1,0:T(8,128)(2,1)S(1)}, u32[]{:S(2)}, u32[]{:S(2)}) collective-permute-start(bf16[192,768]{1,0:T(8,128)(2,1)S(1)} %get-tuple-element.35.refs_2_.keep), channel_id=1, source_target_pairs={{2,0},{7,1},{4,2},{1,3},{6,4},{3,5},{0,6},{5,7},{10,8},{15,9},{12,... | collective-permute-start | bytes 884744 | tf_op jit(solution)/shard_map/ppermute | solution.py:408
  5.9 2.0 %collective-permute-start.2 = (bf16[192,768]{1,0:T(8,128)(2,1)S(1)}, bf16[192,768]{1,0:T(8,128)(2,1)S(1)}, u32[]{:S(2)}, u32[]{:S(2)}) collective-permute-start(bf16[192,768]{1,0:T(8,128)(2,1)S(1)} %get-tuple-element.35.refs_2_.keep), channel_id=1, source_target_pairs={{8,0},{9,1},{10,2},{11,3},{12,4},{13,5},{14,6},{15,7},{0,8},{1,9},... | collective-permute-start | bytes 884744 | tf_op jit(solution)/shard_map/ppermute | solution.py:408
  7.9 1.7 %collective-permute-start.9 = (bf16[192,768]{1,0:T(8,128)(2,1)S(1)}, bf16[192,768]{1,0:T(8,128)(2,1)S(1)}, u32[]{:S(2)}, u32[]{:S(2)}) collective-permute-start(bf16[192,768]{1,0:T(8,128)(2,1)S(1)} %collective-permute-done.3.refs_3_.got_mine), channel_id=1, source_target_pairs={{2,0},{7,1},{4,2},{1,3},{6,4},{3,5},{0,6},{5,7},{10,8},{15,9},{12,... | collective-permute-start | bytes 884744 | tf_op jit(solution)/shard_map/ppermute | solution.py:408
  9.6 1.6 %collective-permute-start.11 = (bf16[192,768]{1,0:T(8,128)(2,1)S(1)}, bf16[192,768]{1,0:T(8,128)(2,1)S(1)}, u32[]{:S(2)}, u32[]{:S(2)}) collective-permute-start(bf16[192,768]{1,0:T(8,128)(2,1)S(1)} %collective-permute-done.3.refs_3_.got_mine), channel_id=1, source_target_pairs={{8,0},{9,1},{10,2},{11,3},{12,4},{13,5},{14,6},{15,7},{0,8},{1,9},... | collective-permute-start | bytes 884744 | tf_op jit(solution)/shard_map/ppermute | solution.py:408
  11.1 1.1 %left.1 = (bf16[1024,384]{1,0:T(8,128)(2,1)S(1)}, bf16[1024,384]{1,0:T(8,128)(2,1)S(1)}) custom-call(s32[3]{0:T(128)S(1)} %copy-done.3, bf16[192,768]{1,0:T(8,128)(2,1)S(1)} %get-tuple-element.35.refs_2_.keep, bf16[192,768]{1,0:T(8,128)(2,1)S(1)} %get-tuple-element.36.send, bf16[192,768]{1,0:T(8,128)(2,1)S(1)} %collective-permute-done.3.refs_3_.got_mine, ...), custom_call_target="tpu_custom_call" | custom-call | flops 100663296 | bytes 2752524 | tf_op jit(solution)/shard_map/left/pallas_call | solution.py:92
  12.2 1.0 %product.3.refs_0_ = f32[2,192,768]{2,1,0:T(8,128)S(1)} custom-call(bf16[384,3072]{1,0:T(8,128)(2,1)S(1)} %bitcast.7, bf16[384,3072]{1,0:T(8,128)(2,1)S(1)} %collective-permute-done.4.refs_1_.refs_2_.a_sib, bf16[192,768]{1,0:T(8,128)(2,1)S(1)} %get-tuple-element.35.refs_2_.keep, bf16[192,768]{1,0:T(8,128)(2,1)S(1)} %collective-permute-done.3.refs_3_.got_mine), custom_call_target="tpu_custom_call" | custom-call | flops 452984832 | bytes 6488064 | tf_op jit(solution)/shard_map/product/pallas_call | solution.py:92
  13.3 0.6 collective-permute-start.10
  13.9 1.8 %collective-permute-done.1.refs_4_ = bf16[192,768]{1,0:T(8,128)(2,1)S(1)} collective-permute-done((bf16[192,768]{1,0:T(8,128)(2,1)S(1)}, bf16[192,768]{1,0:T(8,128)(2,1)S(1)}, u32[]{:S(2)}, u32[]{:S(2)}) %collective-permute-start.1) | collective-permute-done | bytes 294944 | tf_op jit(solution)/shard_map/ppermute | solution.py:408
  15.8 3.3 %collective-permute-start.6 = (bf16[192,768]{1,0:T(8,128)(2,1)S(1)}, bf16[192,768]{1,0:T(8,128)(2,1)S(1)}, u32[]{:S(2)}, u32[]{:S(2)}) collective-permute-start(bf16[192,768]{1,0:T(8,128)(2,1)S(1)} %collective-permute-done.refs_3_), channel_id=1, source_target_pairs={{2,0},{7,1},{4,2},{1,3},{6,4},{3,5},{0,6},{5,7},{10,8},{15,9},{12,... | collective-permute-start | bytes 884744 | tf_op jit(solution)/shard_map/ppermute | solution.py:408
  19.1 0.6 collective-permute-start.8
  19.7 2.4 %collective-permute-done.11.refs_8_ = bf16[192,768]{1,0:T(8,128)(2,1)S(1)} collective-permute-done((bf16[192,768]{1,0:T(8,128)(2,1)S(1)}, bf16[192,768]{1,0:T(8,128)(2,1)S(1)}, u32[]{:S(2)}, u32[]{:S(2)}) %collective-permute-start.11) | collective-permute-done | bytes 294944 | tf_op jit(solution)/shard_map/ppermute | solution.py:408
  22.1 3.3 %collective-permute-start.12 = (bf16[192,768]{1,0:T(8,128)(2,1)S(1)}, bf16[192,768]{1,0:T(8,128)(2,1)S(1)}, u32[]{:S(2)}, u32[]{:S(2)}) collective-permute-start(bf16[192,768]{1,0:T(8,128)(2,1)S(1)} %collective-permute-done.9.refs_6_), channel_id=1, source_target_pairs={{2,0},{7,1},{4,2},{1,3},{6,4},{3,5},{0,6},{5,7},{10,8},{15,9},{12,... | collective-permute-start | bytes 884744 | tf_op jit(solution)/shard_map/ppermute | solution.py:408
  25.6 1.3 %collective-permute-start.13 = (bf16[192,768]{1,0:T(8,128)(2,1)S(1)}, bf16[192,768]{1,0:T(8,128)(2,1)S(1)}, u32[]{:S(2)}, u32[]{:S(2)}) collective-permute-start(bf16[192,768]{1,0:T(8,128)(2,1)S(1)} %collective-permute-done.11.refs_8_), channel_id=1, source_target_pairs={{6,0},{3,1},{0,2},{5,3},{2,4},{7,5},{4,6},{1,7},{14,8},{11,9},{8,1... | collective-permute-start | bytes 884744 | tf_op jit(solution)/shard_map/ppermute | solution.py:408
  27.0 3.0 %product.4.refs_0_ = f32[2,192,768]{2,1,0:T(8,128)S(1)} custom-call(f32[2,192,768]{2,1,0:T(8,128)S(1)} %product.3.refs_0_, bf16[384,3072]{1,0:T(8,128)(2,1)S(1)} %bitcast.8, bf16[384,3072]{1,0:T(8,128)(2,1)S(1)} %collective-permute-done.4.refs_1_.refs_2_.a_sib, bf16[192,768]{1,0:T(8,128)(2,1)S(1)} %collective-permute-done.refs_3_, ...), custom_call_target="tpu_custom_call" | custom-call | flops 1358954496 | bytes 8847360 | tf_op jit(solution)/shard_map/product/pallas_call | solution.py:92
  30.0 1.6 %collective-permute-start.15 = (bf16[192,768]{1,0:T(8,128)(2,1)S(1)}, bf16[192,768]{1,0:T(8,128)(2,1)S(1)}, u32[]{:S(2)}, u32[]{:S(2)}) collective-permute-start(bf16[192,768]{1,0:T(8,128)(2,1)S(1)} %collective-permute-done.7.refs_4_), channel_id=1, source_target_pairs={{6,0},{3,1},{0,2},{5,3},{2,4},{7,5},{4,6},{1,7},{14,8},{11,9},{8,1... | collective-permute-start | bytes 884744 | tf_op jit(solution)/shard_map/ppermute | solution.py:408
  31.5 1.2 %collective-permute-done.12.refs_6_ = bf16[192,768]{1,0:T(8,128)(2,1)S(1)} collective-permute-done((bf16[192,768]{1,0:T(8,128)(2,1)S(1)}, bf16[192,768]{1,0:T(8,128)(2,1)S(1)}, u32[]{:S(2)}, u32[]{:S(2)}) %collective-permute-start.12) | collective-permute-done | bytes 294944 | tf_op jit(solution)/shard_map/ppermute | solution.py:408
  32.8 2.6 %collective-permute-done.14.refs_8_ = bf16[192,768]{1,0:T(8,128)(2,1)S(1)} collective-permute-done((bf16[192,768]{1,0:T(8,128)(2,1)S(1)}, bf16[192,768]{1,0:T(8,128)(2,1)S(1)}, u32[]{:S(2)}, u32[]{:S(2)}) %collective-permute-start.14) | collective-permute-done | bytes 294944 | tf_op jit(solution)/shard_map/ppermute | solution.py:408
  35.3 3.0 %product.5.old = f32[2,192,768]{2,1,0:T(8,128)S(1)} custom-call(f32[2,192,768]{2,1,0:T(8,128)S(1)} %product.4.refs_0_, bf16[384,3072]{1,0:T(8,128)(2,1)S(1)} %bitcast.9, bf16[384,3072]{1,0:T(8,128)(2,1)S(1)} %collective-permute-done.4.refs_1_.refs_2_.a_sib, bf16[192,768]{1,0:T(8,128)(2,1)S(1)} %collective-permute-done.6.refs_3_, ...), custom_call_target="tpu_custom_call" | custom-call | flops 1358954496 | bytes 8847360 | tf_op jit(solution)/shard_map/product/pallas_call | solution.py:92
  38.3 2.5 %collective-permute-done.16.v = bf16[192,768]{1,0:T(8,128)(2,1)S(1)} collective-permute-done((bf16[192,768]{1,0:T(8,128)(2,1)S(1)}, bf16[192,768]{1,0:T(8,128)(2,1)S(1)}, u32[]{:S(2)}, u32[]{:S(2)}) %collective-permute-start.16) | collective-permute-done | bytes 294944 | tf_op jit(solution)/shard_map/ppermute | solution.py:408
  40.8 5.8 %column.1 = (f32[192,768]{1,0:T(8,128)}, f32[192,768]{1,0:T(8,128)}, f32[16,32,768]{2,1,0:T(8,128)}) custom-call(s32[3,96]{1,0:T(4,128)S(1)} %bitcast.13, s32[3]{0:T(128)S(1)} %copy-done.3, f32[2,192,768]{2,1,0:T(8,128)S(1)} %product.5.old, bf16[384,3072]{1,0:T(8,128)(2,1)S(1)} %bitcast.10, ...), custom_call_target="tpu_custom_call" | custom-call | flops 1660944384 | bytes 10814604 | tf_op jit(solution)/shard_map/column/pallas_call | solution.py:92
  46.6 5.4 %all-to-all-start = ((f32[16,32,768]{2,1,0:T(8,128)}), f32[16,32,768]{2,1,0:T(8,128)S(1)}, u32[]{:S(2)}, u32[]{:S(2)}) async-start(f32[16,32,768]{2,1,0:T(8,128)} %get-tuple-element.55), calls=%async_computation | async-start | bytes 3145728 | tf_op jit(solution)/shard_map/all_to_all | solution.py:503
  52.3 1.9 %collective-permute-done.17.other = f32[192,768]{1,0:T(8,128)S(1)} collective-permute-done((f32[192,768]{1,0:T(8,128)S(1)}, f32[192,768]{1,0:T(8,128)S(1)}, u32[]{:S(2)}, u32[]{:S(2)}) %collective-permute-start.17) | collective-permute-done | bytes 589856 | tf_op jit(solution)/shard_map/ppermute | solution.py:408
  54.1 0.7 term.1
  54.9 1.9 %collective-permute-start.18 = (f32[96,768]{1,0:T(8,128)S(1)}, f32[96,768]{1,0:T(8,128)S(1)}, u32[]{:S(2)}, u32[]{:S(2)}) collective-permute-start(f32[96,768]{1,0:T(8,128)S(1)} %get-tuple-element.53), channel_id=1, source_target_pairs={{32,0},{225,1},{34,2},{227,3},{36,4},{229,5},{38,6},{231,7},{40,8}... | collective-permute-start | bytes 884744 | tf_op jit(solution)/shard_map/ppermute | solution.py:511
  56.8 1.8 %spread.1 = bf16[2,192,1536]{2,1,0:T(8,128)(2,1)} custom-call(s32[3]{0:T(128)S(1)} %copy-done.3, f32[192,768]{1,0:T(8,128)S(1)} %copy-done.1, f32[192,768]{1,0:T(8,128)S(1)} %collective-permute-done.17.other), custom_call_target="tpu_custom_call" | custom-call | bytes 2359308 | tf_op jit(solution)/shard_map/spread/pallas_call | solution.py:92
  58.6 3.1 %collective-permute-done.18.got = f32[96,768]{1,0:T(8,128)S(1)} collective-permute-done((f32[96,768]{1,0:T(8,128)S(1)}, f32[96,768]{1,0:T(8,128)S(1)}, u32[]{:S(2)}, u32[]{:S(2)}) %collective-permute-start.18) | collective-permute-done | bytes 294944 | tf_op jit(solution)/shard_map/ppermute | solution.py:511
  61.8 3.2 %collective-permute-start.19 = (f32[48,768]{1,0:T(8,128)S(1)}, f32[48,768]{1,0:T(8,128)S(1)}, u32[]{:S(2)}, u32[]{:S(2)}) collective-permute-start(f32[48,768]{1,0:T(8,128)S(1)} %get-tuple-element.61), channel_id=1, source_target_pairs={{64,0},{193,1},{66,2},{195,3},{68,4},{197,5},{70,6},{199,7},{72,8}... | collective-permute-start | bytes 442376 | tf_op jit(solution)/shard_map/ppermute | solution.py:526
  65.0 8.5 %all-to-all-done.sums = f32[16,32,768]{2,1,0:T(8,128)S(1)} async-done(((f32[16,32,768]{2,1,0:T(8,128)}), f32[16,32,768]{2,1,0:T(8,128)S(1)}, u32[]{:S(2)}, u32[]{:S(2)}) %all-to-all-start) | async-done | bytes 1572896 | tf_op jit(solution)/shard_map/all_to_all | solution.py:503
  73.5 1.7 %pivot.1 = (f32[2,3,32,512]{3,2,1,0:T(8,128)}, f32[16,16,512]{2,1,0:T(8,128)S(1)}) custom-call(s32[3]{0:T(128)S(1)} %copy-done.3, f32[1,2]{1,0:T(1,128)S(1)} %copy-done.5, f32[2,3,32,512]{3,2,1,0:T(8,128)S(1)} %bitcast.11, f32[16,32,768]{2,1,0:T(8,128)S(1)} %all-to-all-done.sums, f32[48,768]{1,0:T(8,128)S(1)} %get-tuple-element.60.keep, ...), custom_call_target="tpu_custom_call" | custom-call | bytes 3178516 | tf_op jit(solution)/shard_map/pivot/pallas_call | solution.py:92
  75.2 27.4 %all_to_all.10.pays = f32[16,16,512]{2,1,0:T(8,128)S(1)} all-to-all(f32[16,16,512]{2,1,0:T(8,128)S(1)} %get-tuple-element.63), channel_id=1, replica_groups={{0,16,224,240,64,80,160,176,32,48,192,208,96,112,128,144},{1,17,225,241..., dimensions={0} | all-to-all | bytes 1048576 | tf_op jit(solution)/shard_map/all_to_all | solution.py:542
  102.6 0.8 density.1
  (36 shorter events, 1.5 us)
Async XLA Ops:
  0.6 10.5 %copy-start.3 = (s32[3]{0:T(128)S(1)}, s32[3]{0:T(128)}, u32[]{:S(2)}) copy-start(s32[3]{0:T(128)} %widths.7) | copy-start | bytes 40
  0.6 7.2 %collective-permute-start.4 = (bf16[384,3072]{1,0:T(8,128)(2,1)}, bf16[384,3072]{1,0:T(8,128)(2,1)S(1)}, u32[]{:S(2)}, u32[]{:S(2)}) collective-permute-start(bf16[384,3072]{1,0:T(8,128)(2,1)} %bitcast.6), channel_id=1, source_target_pairs={{1,0},{0,1},{3,2},{2,3},{5,4},{4,5},{7,6},{6,7},{9,8},{8,9},{11,10... | collective-permute-start | bytes 7077896 | tf_op jit(solution)/shard_map/ppermute | solution.py:408
  0.7 11.5 %copy-start = (bf16[1,2,192,3072]{3,2,1,0:T(8,128)(2,1)S(1)}, bf16[1,2,192,3072]{3,2,1,0:T(8,128)(2,1)}, u32[]{:S(2)}) copy-start(bf16[1,2,192,3072]{3,2,1,0:T(8,128)(2,1)} %param.7) | copy-start | bytes 7077892
  2.4 3.4 %collective-permute-start.3 = (bf16[192,768]{1,0:T(8,128)(2,1)S(1)}, bf16[192,768]{1,0:T(8,128)(2,1)S(1)}, u32[]{:S(2)}, u32[]{:S(2)}) collective-permute-start(bf16[192,768]{1,0:T(8,128)(2,1)S(1)} %get-tuple-element.36.send), channel_id=1, source_target_pairs={{1,0},{0,1},{3,2},{2,3},{5,4},{4,5},{7,6},{6,7},{9,8},{8,9},{11,10... | collective-permute-start | bytes 884744 | tf_op jit(solution)/shard_map/ppermute | solution.py:408
  3.0 6.6 %collective-permute-start.5 = (bf16[192,768]{1,0:T(8,128)(2,1)S(1)}, bf16[192,768]{1,0:T(8,128)(2,1)S(1)}, u32[]{:S(2)}, u32[]{:S(2)}) collective-permute-start(bf16[192,768]{1,0:T(8,128)(2,1)S(1)} %get-tuple-element.35.refs_2_.keep), channel_id=1, source_target_pairs={{1,0},{0,1},{3,2},{2,3},{5,4},{4,5},{7,6},{6,7},{9,8},{8,9},{11,10... | collective-permute-start | bytes 884744 | tf_op jit(solution)/shard_map/ppermute | solution.py:408
  3.1 10.2 %collective-permute-start = (bf16[192,768]{1,0:T(8,128)(2,1)S(1)}, bf16[192,768]{1,0:T(8,128)(2,1)S(1)}, u32[]{:S(2)}, u32[]{:S(2)}) collective-permute-start(bf16[192,768]{1,0:T(8,128)(2,1)S(1)} %get-tuple-element.35.refs_2_.keep), channel_id=1, source_target_pairs={{2,0},{7,1},{4,2},{1,3},{6,4},{3,5},{0,6},{5,7},{10,8},{15,9},{12,... | collective-permute-start | bytes 884744 | tf_op jit(solution)/shard_map/ppermute | solution.py:408
  5.9 9.8 %collective-permute-start.1 = (bf16[192,768]{1,0:T(8,128)(2,1)S(1)}, bf16[192,768]{1,0:T(8,128)(2,1)S(1)}, u32[]{:S(2)}, u32[]{:S(2)}) collective-permute-start(bf16[192,768]{1,0:T(8,128)(2,1)S(1)} %get-tuple-element.35.refs_2_.keep), channel_id=1, source_target_pairs={{6,0},{3,1},{0,2},{5,3},{2,4},{7,5},{4,6},{1,7},{14,8},{11,9},{8,1... | collective-permute-start | bytes 884744 | tf_op jit(solution)/shard_map/ppermute | solution.py:408
  5.9 9.9 %collective-permute-start.2 = (bf16[192,768]{1,0:T(8,128)(2,1)S(1)}, bf16[192,768]{1,0:T(8,128)(2,1)S(1)}, u32[]{:S(2)}, u32[]{:S(2)}) collective-permute-start(bf16[192,768]{1,0:T(8,128)(2,1)S(1)} %get-tuple-element.35.refs_2_.keep), channel_id=1, source_target_pairs={{8,0},{9,1},{10,2},{11,3},{12,4},{13,5},{14,6},{15,7},{0,8},{1,9},... | collective-permute-start | bytes 884744 | tf_op jit(solution)/shard_map/ppermute | solution.py:408
  7.9 11.2 %collective-permute-start.9 = (bf16[192,768]{1,0:T(8,128)(2,1)S(1)}, bf16[192,768]{1,0:T(8,128)(2,1)S(1)}, u32[]{:S(2)}, u32[]{:S(2)}) collective-permute-start(bf16[192,768]{1,0:T(8,128)(2,1)S(1)} %collective-permute-done.3.refs_3_.got_mine), channel_id=1, source_target_pairs={{2,0},{7,1},{4,2},{1,3},{6,4},{3,5},{0,6},{5,7},{10,8},{15,9},{12,... | collective-permute-start | bytes 884744 | tf_op jit(solution)/shard_map/ppermute | solution.py:408
  9.6 12.5 %collective-permute-start.11 = (bf16[192,768]{1,0:T(8,128)(2,1)S(1)}, bf16[192,768]{1,0:T(8,128)(2,1)S(1)}, u32[]{:S(2)}, u32[]{:S(2)}) collective-permute-start(bf16[192,768]{1,0:T(8,128)(2,1)S(1)} %collective-permute-done.3.refs_3_.got_mine), channel_id=1, source_target_pairs={{8,0},{9,1},{10,2},{11,3},{12,4},{13,5},{14,6},{15,7},{0,8},{1,9},... | collective-permute-start | bytes 884744 | tf_op jit(solution)/shard_map/ppermute | solution.py:408
  13.3 12.1 %collective-permute-start.10 = (bf16[192,768]{1,0:T(8,128)(2,1)S(1)}, bf16[192,768]{1,0:T(8,128)(2,1)S(1)}, u32[]{:S(2)}, u32[]{:S(2)}) collective-permute-start(bf16[192,768]{1,0:T(8,128)(2,1)S(1)} %collective-permute-done.3.refs_3_.got_mine), channel_id=1, source_target_pairs={{6,0},{3,1},{0,2},{5,3},{2,4},{7,5},{4,6},{1,7},{14,8},{11,9},{8,1... | collective-permute-start | bytes 884744 | tf_op jit(solution)/shard_map/ppermute | solution.py:408
  15.8 9.9 %collective-permute-start.6 = (bf16[192,768]{1,0:T(8,128)(2,1)S(1)}, bf16[192,768]{1,0:T(8,128)(2,1)S(1)}, u32[]{:S(2)}, u32[]{:S(2)}) collective-permute-start(bf16[192,768]{1,0:T(8,128)(2,1)S(1)} %collective-permute-done.refs_3_), channel_id=1, source_target_pairs={{2,0},{7,1},{4,2},{1,3},{6,4},{3,5},{0,6},{5,7},{10,8},{15,9},{12,... | collective-permute-start | bytes 884744 | tf_op jit(solution)/shard_map/ppermute | solution.py:408
  19.1 10.9 %collective-permute-start.7 = (bf16[192,768]{1,0:T(8,128)(2,1)S(1)}, bf16[192,768]{1,0:T(8,128)(2,1)S(1)}, u32[]{:S(2)}, u32[]{:S(2)}) collective-permute-start(bf16[192,768]{1,0:T(8,128)(2,1)S(1)} %collective-permute-done.2.refs_5_), channel_id=1, source_target_pairs={{6,0},{3,1},{0,2},{5,3},{2,4},{7,5},{4,6},{1,7},{14,8},{11,9},{8,1... | collective-permute-start | bytes 884744 | tf_op jit(solution)/shard_map/ppermute | solution.py:408
  19.1 10.9 %collective-permute-start.8 = (bf16[192,768]{1,0:T(8,128)(2,1)S(1)}, bf16[192,768]{1,0:T(8,128)(2,1)S(1)}, u32[]{:S(2)}, u32[]{:S(2)}) collective-permute-start(bf16[192,768]{1,0:T(8,128)(2,1)S(1)} %collective-permute-done.refs_3_), channel_id=1, source_target_pairs={{8,0},{9,1},{10,2},{11,3},{12,4},{13,5},{14,6},{15,7},{0,8},{1,9},... | collective-permute-start | bytes 884744 | tf_op jit(solution)/shard_map/ppermute | solution.py:408
  22.1 10.7 %collective-permute-start.12 = (bf16[192,768]{1,0:T(8,128)(2,1)S(1)}, bf16[192,768]{1,0:T(8,128)(2,1)S(1)}, u32[]{:S(2)}, u32[]{:S(2)}) collective-permute-start(bf16[192,768]{1,0:T(8,128)(2,1)S(1)} %collective-permute-done.9.refs_6_), channel_id=1, source_target_pairs={{2,0},{7,1},{4,2},{1,3},{6,4},{3,5},{0,6},{5,7},{10,8},{15,9},{12,... | collective-permute-start | bytes 884744 | tf_op jit(solution)/shard_map/ppermute | solution.py:408
  25.4 9.9 %collective-permute-start.14 = (bf16[192,768]{1,0:T(8,128)(2,1)S(1)}, bf16[192,768]{1,0:T(8,128)(2,1)S(1)}, u32[]{:S(2)}, u32[]{:S(2)}) collective-permute-start(bf16[192,768]{1,0:T(8,128)(2,1)S(1)} %collective-permute-done.9.refs_6_), channel_id=1, source_target_pairs={{8,0},{9,1},{10,2},{11,3},{12,4},{13,5},{14,6},{15,7},{0,8},{1,9},... | collective-permute-start | bytes 884744 | tf_op jit(solution)/shard_map/ppermute | solution.py:408
  25.6 9.7 %collective-permute-start.13 = (bf16[192,768]{1,0:T(8,128)(2,1)S(1)}, bf16[192,768]{1,0:T(8,128)(2,1)S(1)}, u32[]{:S(2)}, u32[]{:S(2)}) collective-permute-start(bf16[192,768]{1,0:T(8,128)(2,1)S(1)} %collective-permute-done.11.refs_8_), channel_id=1, source_target_pairs={{6,0},{3,1},{0,2},{5,3},{2,4},{7,5},{4,6},{1,7},{14,8},{11,9},{8,1... | collective-permute-start | bytes 884744 | tf_op jit(solution)/shard_map/ppermute | solution.py:408
  29.9 10.9 %copy-start.4 = (s32[96,3]{0,1:T(4,128)S(1)}, s32[96,3]{0,1:T(4,128)}, u32[]{:S(2)}) copy-start(s32[96,3]{0,1:T(4,128)} %param.9) | copy-start | bytes 3460
  30.0 8.3 %collective-permute-start.15 = (bf16[192,768]{1,0:T(8,128)(2,1)S(1)}, bf16[192,768]{1,0:T(8,128)(2,1)S(1)}, u32[]{:S(2)}, u32[]{:S(2)}) collective-permute-start(bf16[192,768]{1,0:T(8,128)(2,1)S(1)} %collective-permute-done.7.refs_4_), channel_id=1, source_target_pairs={{6,0},{3,1},{0,2},{5,3},{2,4},{7,5},{4,6},{1,7},{14,8},{11,9},{8,1... | collective-permute-start | bytes 884744 | tf_op jit(solution)/shard_map/ppermute | solution.py:408
  32.8 8.1 %collective-permute-start.16 = (bf16[192,768]{1,0:T(8,128)(2,1)S(1)}, bf16[192,768]{1,0:T(8,128)(2,1)S(1)}, u32[]{:S(2)}, u32[]{:S(2)}) collective-permute-start(bf16[192,768]{1,0:T(8,128)(2,1)S(1)} %collective-permute-done.12.refs_6_), channel_id=1, source_target_pairs={{8,0},{9,1},{10,2},{11,3},{12,4},{13,5},{14,6},{15,7},{0,8},{1,9},... | collective-permute-start | bytes 884744 | tf_op jit(solution)/shard_map/ppermute | solution.py:408
  46.6 5.4 %copy-start.6 = (f32[192,768]{1,0:T(8,128)S(1)}, f32[192,768]{1,0:T(8,128)}, u32[]{:S(2)}) copy-start(f32[192,768]{1,0:T(8,128)} %get-tuple-element.52) | copy-start | bytes 1769476
  46.6 7.5 %copy-start.1 = (f32[192,768]{1,0:T(8,128)S(1)}, f32[192,768]{1,0:T(8,128)}, u32[]{:S(2)}) copy-start(f32[192,768]{1,0:T(8,128)} %get-tuple-element.51.mine) | copy-start | bytes 1769476
  46.6 7.5 %copy-start.5 = (f32[1,2]{1,0:T(1,128)S(1)}, f32[1,2]{1,0:T(1,128)}, u32[]{:S(2)}) copy-start(f32[1,2]{1,0:T(1,128)} %weights.3) | copy-start | bytes 28
  46.6 26.8 %all-to-all-start = ((f32[16,32,768]{2,1,0:T(8,128)}), f32[16,32,768]{2,1,0:T(8,128)S(1)}, u32[]{:S(2)}, u32[]{:S(2)}) async-start(f32[16,32,768]{2,1,0:T(8,128)} %get-tuple-element.55), calls=%async_computation | async-start | bytes 3145728 | tf_op jit(solution)/shard_map/all_to_all | solution.py:503
  52.0 2.1 %collective-permute-start.17 = (f32[192,768]{1,0:T(8,128)S(1)}, f32[192,768]{1,0:T(8,128)S(1)}, u32[]{:S(2)}, u32[]{:S(2)}) collective-permute-start(f32[192,768]{1,0:T(8,128)S(1)} %copy-done.6), channel_id=1, source_target_pairs={{1,0},{0,1},{3,2},{2,3},{5,4},{4,5},{7,6},{6,7},{9,8},{8,9},{11,10... | collective-permute-start | bytes 1769480 | tf_op jit(solution)/shard_map/ppermute | solution.py:408
  54.9 18.6 %copy-start.2 = (f32[1,2,3,32,512]{4,3,2,1,0:T(8,128)S(1)}, f32[1,2,3,32,512]{4,3,2,1,0:T(8,128)}, u32[]{:S(2)}) copy-start(f32[1,2,3,32,512]{4,3,2,1,0:T(8,128)} %param.8) | copy-start | bytes 1179652
  54.9 6.8 %collective-permute-start.18 = (f32[96,768]{1,0:T(8,128)S(1)}, f32[96,768]{1,0:T(8,128)S(1)}, u32[]{:S(2)}, u32[]{:S(2)}) collective-permute-start(f32[96,768]{1,0:T(8,128)S(1)} %get-tuple-element.53), channel_id=1, source_target_pairs={{32,0},{225,1},{34,2},{227,3},{36,4},{229,5},{38,6},{231,7},{40,8}... | collective-permute-start | bytes 884744 | tf_op jit(solution)/shard_map/ppermute | solution.py:511
  61.8 11.7 %collective-permute-start.19 = (f32[48,768]{1,0:T(8,128)S(1)}, f32[48,768]{1,0:T(8,128)S(1)}, u32[]{:S(2)}, u32[]{:S(2)}) collective-permute-start(f32[48,768]{1,0:T(8,128)S(1)} %get-tuple-element.61), channel_id=1, source_target_pairs={{64,0},{193,1},{66,2},{195,3},{68,4},{197,5},{70,6},{199,7},{72,8}... | collective-permute-start | bytes 442376 | tf_op jit(solution)/shard_map/ppermute | solution.py:526
